TPU v7x, 32 devices: a whole 2x2x4 slice. The times are simulated.
32 devices in a mesh: dp: 2 (over x), expert: 16 (over z, y, core).
Axes of the slice: x: 2, y: 2, z: 4, core: 2. Of those that a mesh axis runs over, the one named last changes fastest.
Arguments:
- tokens: bfloat16 [4096, 4096], P(('dp', 'expert')), may hold values from -6 to 6
- routes: int32 [32, 2, 4], P(('dp', 'expert')), may hold values from 0 to 127, as said below
- gate_values: float32 [32, 2, 4], P(('dp', 'expert')), may hold values from 0.1 to 1
- gate_weight: bfloat16 [16, 4096, 256], P('expert', 'dp'), may hold values from -0.09375 to 0.09375
- up_weight: bfloat16 [16, 4096, 256], P('expert', 'dp'), may hold values from -0.09375 to 0.09375
- down_weight: bfloat16 [16, 4096, 256], P('expert', 'dp'), may hold values from -0.125 to 0.125
- cotangent: bfloat16 [4096, 4096], P(('dp', 'expert')), may hold values from -6 to 6
Outputs:
- layer_out: bfloat16 [4096, 4096], P(('dp', 'expert'))
- token_grad: bfloat16 [4096, 4096], P(('dp', 'expert'))
- gate_grad: bfloat16 [16, 4096, 256], P('expert', 'dp')
- up_grad: bfloat16 [16, 4096, 256], P('expert', 'dp')
- down_grad: bfloat16 [16, 4096, 256], P('expert', 'dp')
Inputs may be any that keep to these rules, and one draw needn't show every extreme that they name: `routes`: for each home block and each expert, 4 distinct positions within that block.
All inputs are finite; a program needn't handle non-finite values.
Results may differ from a plain program's by a relative error of at most 0.025.
Values may be sent and summed in bfloat16 or wider, within the bound.
No kernel may reach another device: no remote copies, remote signals or barrier semaphores. Data moves between devices by JAX's collectives and lax.ppermute only.
A program may use at most 128 MiB of HBM per device.

v0:
```python
import jax
import jax.numpy as jnp
from jax import lax
from jax.sharding import PartitionSpec as P

SPLIT = 8


def send_out(payload):
    expert_count, slot_count, width = payload.shape
    widened = jnp.repeat(payload, SPLIT, axis=0)
    received = lax.all_to_all(widened, "expert", split_axis=0, concat_axis=0, tiled=True)
    return received.reshape(-1, width)


def bring_back(partial_value, expert_count):
    total_rows, width = partial_value.shape
    home_count = lax.axis_size("expert")
    returned = lax.all_to_all(
        partial_value.reshape(home_count, -1, width),
        "expert",
        split_axis=0,
        concat_axis=0,
        tiled=True,
    )
    slot_count = returned.shape[1]
    returned = returned.reshape(expert_count, SPLIT, slot_count, width)
    return jnp.sum(returned.astype(jnp.float32), axis=1)


def shards(tokens, routes, gate_values, gate_weight, up_weight, down_weight, cotangent):
    width = tokens.shape[1]
    expert_count = routes.shape[1]
    chosen = routes[0]
    scales = gate_values[0][:, :, None]
    contract_last = (((1,), (1,)), ((), ()))
    contract_first = (((0,), (0,)), ((), ()))
    full_gate, full_up, full_down = (
        lax.all_gather(gate_weight, "dp", axis=1, tiled=True),
        lax.all_gather(up_weight, "dp", axis=1, tiled=True),
        lax.all_gather(down_weight, "dp", axis=1, tiled=True),
    )
    full_gate = full_gate[0]
    full_up = full_up[0]
    full_down = full_down[0]
    token_rows = send_out(tokens[chosen])
    gate_pre = jnp.dot(token_rows, full_gate, preferred_element_type=jnp.float32)
    up_pre = jnp.dot(token_rows, full_up, preferred_element_type=jnp.float32)
    gate_sigma = jax.nn.sigmoid(gate_pre)
    hidden = (gate_pre * gate_sigma * up_pre).astype(jnp.bfloat16)
    partial_value = lax.dot_general(
        hidden, full_down, contract_last, preferred_element_type=jnp.float32
    ).astype(jnp.bfloat16)
    combined = bring_back(partial_value, expert_count)
    layer_out = jnp.zeros((tokens.shape[0], width), jnp.float32).at[chosen].add(scales * combined)
    scaled_cot = (scales * cotangent[chosen].astype(jnp.float32)).astype(jnp.bfloat16)
    cot_rows = send_out(scaled_cot)
    hidden_grad = jnp.dot(cot_rows, full_down, preferred_element_type=jnp.float32)
    gate_rows = (hidden_grad * up_pre * gate_sigma * (1.0 + gate_pre * (1.0 - gate_sigma))).astype(
        jnp.bfloat16
    )
    up_rows = (hidden_grad * gate_pre * gate_sigma).astype(jnp.bfloat16)
    partial_grad = (
        lax.dot_general(gate_rows, full_gate, contract_last, preferred_element_type=jnp.float32)
        + lax.dot_general(up_rows, full_up, contract_last, preferred_element_type=jnp.float32)
    ).astype(jnp.bfloat16)
    token_grad = (
        jnp.zeros((tokens.shape[0], width), jnp.float32)
        .at[chosen]
        .add(bring_back(partial_grad, expert_count))
    )
    grad_sums = lax.psum_scatter(
        jnp.concatenate(
            [
                lax.dot_general(
                    token_rows, gate_rows, contract_first, preferred_element_type=jnp.float32
                ),
                lax.dot_general(
                    token_rows, up_rows, contract_first, preferred_element_type=jnp.float32
                ),
                lax.dot_general(
                    cot_rows, hidden, contract_first, preferred_element_type=jnp.float32
                ),
            ],
            axis=1,
        ).astype(jnp.bfloat16),
        "dp",
        scatter_dimension=0,
        tiled=True,
    ).astype(jnp.float32)
    hidden_width = hidden.shape[1]
    gate_grad = grad_sums[:, :hidden_width].astype(jnp.bfloat16)[None]
    up_grad = grad_sums[:, hidden_width : 2 * hidden_width].astype(jnp.bfloat16)[None]
    down_grad = grad_sums[:, 2 * hidden_width :].astype(jnp.bfloat16)[None]
    return (
        layer_out.astype(jnp.bfloat16),
        token_grad.astype(jnp.bfloat16),
        gate_grad,
        up_grad,
        down_grad,
    )


def solution(mesh):
    placed = (
        P(("dp", "expert"), None),
        P(("dp", "expert"), None, None),
        P(("dp", "expert"), None, None),
        P("expert", "dp", None),
        P("expert", "dp", None),
        P("expert", "dp", None),
        P(("dp", "expert"), None),
    )
    return jax.shard_map(
        shards,
        mesh=mesh,
        in_specs=placed,
        out_specs=(
            P(("dp", "expert"), None),
            P(("dp", "expert"), None),
            P("expert", "dp", None),
            P("expert", "dp", None),
            P("expert", "dp", None),
        ),
        check_vma=False,
    )
```

profile of v0, /device:TPU:0, one launch (start us, length us, event | category | flops | bytes accessed | tf_op | source)
XLA Modules:
  0.0 220.3 jit_solution(5372515010636029825)
XLA Ops:
  7.2 0.7 all-gather.6.cloned.1.call-update
  8.0 0.7 all-gather.4.cloned.1.call-update
  8.7 0.1 reshape.89
  8.8 0.6 gather_fusion.1
  9.5 0.1 multiply_convert_fusion
  9.6 1.0 broadcast_in_dim.20
  10.6 7.4 %all-to-all-start.2 = ((bf16[16,4,4096]{2,1,0:T(4,128)(2,1)}), bf16[16,4,4096]{2,1,0:T(4,128)(2,1)S(1)}, u32[]{:S(2)}, u32[]{:S(2)}) async-start(bf16[16,4,4096]{2,1,0:T(4,128)(2,1)} %bitcast.7), calls=%async_computation.2 | async-start | bytes 1048576 | tf_op jit(solution)/shard_map/all_to_all | solution.py:12
  18.0 0.0 all-gather.8.cloned.1.call-start
  18.0 0.7 all-gather.8.cloned.1.call-update
  18.7 0.6 gather_fusion
  19.3 13.1 %all-to-all-done.2 = bf16[16,4,4096]{2,1,0:T(4,128)(2,1)S(1)} async-done(((bf16[16,4,4096]{2,1,0:T(4,128)(2,1)}), bf16[16,4,4096]{2,1,0:T(4,128)(2,1)S(1)}, u32[]{:S(2)}, u32[]{:S(2)}) %all-to-all-start.2) | async-done | bytes 524320 | tf_op jit(solution)/shard_map/all_to_all | solution.py:12
  32.4 1.0 broadcast_in_dim.19
  33.4 4.1 %all-to-all-start = ((bf16[16,4,4096]{2,1,0:T(4,128)(2,1)}), bf16[16,4,4096]{2,1,0:T(4,128)(2,1)S(1)}, u32[]{:S(2)}, u32[]{:S(2)}) async-start(bf16[16,4,4096]{2,1,0:T(4,128)(2,1)} %bitcast.2), calls=%async_computation | async-start | bytes 1048576 | tf_op jit(solution)/shard_map/all_to_all | solution.py:12
  37.5 0.0 reduce-scatter.2.cloned.1.call-start
  37.6 0.1 reshape.67
  37.7 14.3 %all-to-all-done = bf16[16,4,4096]{2,1,0:T(4,128)(2,1)S(1)} async-done(((bf16[16,4,4096]{2,1,0:T(4,128)(2,1)}), bf16[16,4,4096]{2,1,0:T(4,128)(2,1)S(1)}, u32[]{:S(2)}, u32[]{:S(2)}) %all-to-all-start) | async-done | bytes 524320 | tf_op jit(solution)/shard_map/all_to_all | solution.py:12
  52.0 0.1 reshape.64
  52.1 2.2 %fusion.5 = f32[64,256]{1,0:T(8,128)S(1)} fusion(bf16[64,4096]{1,0:T(8,128)(2,1)S(1)} %reshape.64, bf16[1,4096,256]{2,1,0:T(8,128)(2,1)} %all-gather.6.cloned.1.call-done), kind=kOutput, calls=%fused_computation.15 | convolution fusion | flops 134217728 | bytes 2686976 | tf_op jit(solution)/shard_map/dot_general | solution.py:48
  54.4 25.7 %all-gather.4.cloned.1.call-done = bf16[1,4096,256]{2,1,0:T(8,128)(2,1)} async-done(((bf16[1,2048,256]{2,1,0:T(8,128)(2,1)}), bf16[1,4096,256]{2,1,0:T(8,128)(2,1)}) %all-gather.4.cloned.1.call-update) | async-done | bytes 2097168 | tf_op jit(solution)/shard_map/all_gather | solution.py:39
  80.1 2.0 fusion.9
  82.2 32.6 %all-gather.8.cloned.1.call-done = bf16[1,4096,256]{2,1,0:T(8,128)(2,1)} async-done(((bf16[1,2048,256]{2,1,0:T(8,128)(2,1)}), bf16[1,4096,256]{2,1,0:T(8,128)(2,1)}) %all-gather.8.cloned.1.call-update) | async-done | bytes 2097168 | tf_op jit(solution)/shard_map/all_gather | solution.py:41
  114.8 2.1 multiply_convert_fusion.1
  116.9 0.7 convolution_convert_fusion
  117.6 0.7 convolution_convert_fusion.1
  118.4 0.7 convolution_convert_fusion.2
  119.1 9.4 %pad_maximum_fusion = bf16[4096,768]{0,1:T(8,128)(2,1)} fusion(bf16[4096,256]{0,1:T(8,128)(2,1)S(1)} %convolution_convert_fusion, bf16[4096,256]{0,1:T(8,128)(2,1)S(1)} %convolution_convert_fusion.1, bf16[4096,256]{0,1:T(8,128)(2,1)S(1)} %convolution_convert_fusion.2), kind=kLoop, calls=%fused_computation.4 | loop fusion | flops 18874368 | bytes 12582912 | tf_op jit(solution)/shard_map/concatenate | solution.py:73
  128.6 1.6 copy-done.2
  130.1 1.5 convolution_convert_fusion.3
  131.7 2.0 reshape.65
  133.7 5.9 %all-to-all-start.1 = ((bf16[16,4,4096]{2,1,0:T(4,128)(2,1)}), bf16[16,4,4096]{2,1,0:T(4,128)(2,1)}, u32[]{:S(2)}, u32[]{:S(2)}) async-start(bf16[16,4,4096]{2,1,0:T(4,128)(2,1)} %reshape.65), calls=%async_computation.1 | async-start | bytes 1048576 | tf_op jit(solution)/shard_map/all_to_all | solution.py:19
  139.6 2.3 %fusion.7 = f32[64,4096]{1,0:T(8,128)S(1)} fusion(bf16[64,256]{1,0:T(8,128)(2,1)S(1)} %get-tuple-element.19, bf16[1,4096,256]{2,1,0:T(8,128)(2,1)} %all-gather.4.cloned.1.call-done), kind=kOutput, calls=%fused_computation.17 | convolution fusion | flops 134217728 | bytes 3178496 | tf_op jit(solution)/shard_map/dot_general | solution.py:64
  142.0 1.6 fusion
  143.5 2.0 reshape.68
  145.6 8.6 %all-to-all-done.1 = bf16[16,4,4096]{2,1,0:T(4,128)(2,1)} async-done(((bf16[16,4,4096]{2,1,0:T(4,128)(2,1)}), bf16[16,4,4096]{2,1,0:T(4,128)(2,1)}, u32[]{:S(2)}, u32[]{:S(2)}) %all-to-all-start.1) | async-done | bytes 524320 | tf_op jit(solution)/shard_map/all_to_all | solution.py:19
  154.2 4.1 %all-to-all-start.3 = ((bf16[16,4,4096]{2,1,0:T(4,128)(2,1)}), bf16[16,4,4096]{2,1,0:T(4,128)(2,1)S(1)}, u32[]{:S(2)}, u32[]{:S(2)}) async-start(bf16[16,4,4096]{2,1,0:T(4,128)(2,1)} %reshape.68), calls=%async_computation.3 | async-start | bytes 1048576 | tf_op jit(solution)/shard_map/all_to_all | solution.py:19
  158.3 1.3 convert_reduce_fusion.1
  159.6 0.1 broadcast_multiply_fusion
  159.7 13.0 %all-to-all-done.3 = bf16[16,4,4096]{2,1,0:T(4,128)(2,1)S(1)} async-done(((bf16[16,4,4096]{2,1,0:T(4,128)(2,1)}), bf16[16,4,4096]{2,1,0:T(4,128)(2,1)S(1)}, u32[]{:S(2)}, u32[]{:S(2)}) %all-to-all-start.3) | async-done | bytes 524320 | tf_op jit(solution)/shard_map/all_to_all | solution.py:19
  172.7 0.2 convert_reduce_fusion
  173.0 1.3 scatter_custom_fusion.1
  174.3 1.1 convert_element_type.56
  175.4 1.3 scatter_custom_fusion
  176.7 1.1 convert_element_type.48
  177.8 28.0 %reduce-scatter.2.cloned.1.call-done = bf16[2048,768]{0,1:T(8,128)(2,1)} async-done(((bf16[4096,768]{0,1:T(8,128)(2,1)}), bf16[2048,768]{0,1:T(8,128)(2,1)}) %reduce-scatter.2.cloned.1.call-update) | async-done | bytes 3145744 | tf_op jit(solution)/shard_map/reduce_scatter | solution.py:72
  205.8 3.1 %slice_bitcast_fusion = (bf16[1,2048,256]{1,2,0:T(8,128)(2,1)}, bf16[1,2048,256]{1,2,0:T(8,128)(2,1)S(1)}, bf16[1,2048,256]{1,2,0:T(8,128)(2,1)S(1)}) fusion(bf16[2048,768]{0,1:T(8,128)(2,1)} %reduce-scatter.2.cloned.1.call-done), kind=kLoop, calls=%fused_computation.21 | loop fusion | bytes 6291456 | tf_op jit(solution)/shard_map/broadcast_in_dim | solution.py:94
  208.9 2.3 %copy.17 = bf16[1,2048,256]{2,1,0:T(8,128)(2,1)} copy(bf16[1,2048,256]{1,2,0:T(8,128)(2,1)} %get-tuple-element.15) | data formatting | bytes 2097152
  211.1 1.3 copy.16
  212.4 1.3 copy.15
  (21 shorter events, 0.3 us)
Async XLA Ops:
  7.2 1.6 copy-start
  7.2 1.5 copy-start.5
  7.2 2.3 %copy-start.4 = (f32[1,2,4]{2,1,0:T(2,128)S(1)}, f32[1,2,4]{2,1,0:T(2,128)}, u32[]{:S(2)}) copy-start(f32[1,2,4]{2,1,0:T(2,128)} %param.9) | copy-start | bytes 100
  7.2 44.9 %all-gather.6.cloned.1.call-start = ((), (), s32[]{:S(2)}) async-start(), calls=%async_computation.6 | async-start | bytes 3145728 | tf_op jit(solution)/shard_map/all_gather | solution.py:40
  7.9 72.2 %all-gather.4.cloned.1.call-start = ((), (), s32[]{:S(2)}) async-start(), calls=%async_computation.5 | async-start | bytes 3145728 | tf_op jit(solution)/shard_map/all_gather | solution.py:39
  8.7 10.0 %copy-start.3 = (bf16[128,4096]{1,0:T(8,128)(2,1)S(1)}, bf16[128,4096]{1,0:T(8,128)(2,1)}, u32[]{:S(2)}) copy-start(bf16[128,4096]{1,0:T(8,128)(2,1)} %param.7) | copy-start | bytes 3145732
  10.6 21.9 %all-to-all-start.2 = ((bf16[16,4,4096]{2,1,0:T(4,128)(2,1)}), bf16[16,4,4096]{2,1,0:T(4,128)(2,1)S(1)}, u32[]{:S(2)}, u32[]{:S(2)}) async-start(bf16[16,4,4096]{2,1,0:T(4,128)(2,1)} %bitcast.7), calls=%async_computation.2 | async-start | bytes 1048576 | tf_op jit(solution)/shard_map/all_to_all | solution.py:12
  18.0 96.9 %all-gather.8.cloned.1.call-start = ((), (), s32[]{:S(2)}) async-start(), calls=%async_computation.7 | async-start | bytes 3145728 | tf_op jit(solution)/shard_map/all_gather | solution.py:41
  33.4 18.6 %all-to-all-start = ((bf16[16,4,4096]{2,1,0:T(4,128)(2,1)}), bf16[16,4,4096]{2,1,0:T(4,128)(2,1)S(1)}, u32[]{:S(2)}, u32[]{:S(2)}) async-start(bf16[16,4,4096]{2,1,0:T(4,128)(2,1)} %bitcast.2), calls=%async_computation | async-start | bytes 1048576 | tf_op jit(solution)/shard_map/all_to_all | solution.py:12
  37.5 168.2 %reduce-scatter.2.cloned.1.call-start = ((), (), s32[]{:S(2)}) async-start(), calls=%async_computation.8 | async-start | bytes 9437184 | tf_op jit(solution)/shard_map/reduce_scatter | solution.py:72
  128.5 1.6 copy-start.2
  133.7 8.3 %copy-start.1 = (bf16[1,4096,256]{2,1,0:T(8,128)(2,1)S(1)}, bf16[1,4096,256]{2,1,0:T(8,128)(2,1)}, u32[]{:S(2)}) copy-start(bf16[1,4096,256]{2,1,0:T(8,128)(2,1)} %all-gather.6.cloned.1.call-done) | copy-start | bytes 6291460
  133.7 20.5 %all-to-all-start.1 = ((bf16[16,4,4096]{2,1,0:T(4,128)(2,1)}), bf16[16,4,4096]{2,1,0:T(4,128)(2,1)}, u32[]{:S(2)}, u32[]{:S(2)}) async-start(bf16[16,4,4096]{2,1,0:T(4,128)(2,1)} %reshape.65), calls=%async_computation.1 | async-start | bytes 1048576 | tf_op jit(solution)/shard_map/all_to_all | solution.py:19
  154.2 18.6 %all-to-all-start.3 = ((bf16[16,4,4096]{2,1,0:T(4,128)(2,1)}), bf16[16,4,4096]{2,1,0:T(4,128)(2,1)S(1)}, u32[]{:S(2)}, u32[]{:S(2)}) async-start(bf16[16,4,4096]{2,1,0:T(4,128)(2,1)} %reshape.68), calls=%async_computation.3 | async-start | bytes 1048576 | tf_op jit(solution)/shard_map/all_to_all | solution.py:19
Sparse Core Ops, SparseCore 0:
  9.6 35.7 all-gather.5
  47.0 33.1 all-gather.3
  81.7 33.1 all-gather.7
  128.7 77.0 reduce-scatter.1
where the time goes:
time: 221 us; the launch traced here: 220 us
  waiting for transfers between devices  137 us (62%)
  starting transfers between devices  21.7 us (10%)
  local copies, waits for them, and re-layouts  17.3 us (8%)
  other arithmetic  15.9 us (7%)
  matrix products  14 us (6%)
  between operations  14 us (6%)
    all_gather x1, waiting for transfers between devices, shards(): lax.all_gather(down_weight, 'dp', axis=1, tiled=True)  32.6 us
    reduce_scatter x1, waiting for transfers between devices, shards(): lax.psum_scatter(jnp.concatenate([lax.dot_general(token_rows, gate_rows,...  28 us
    all_to_all x2, waiting for transfers between devices, send_out(): lax.all_to_all(widened, 'expert', split_axis=0, concat_axis=0, tiled=True)  27.4 us
    all_gather x1, waiting for transfers between devices, shards(): lax.all_gather(gate_weight, 'dp', axis=1, tiled=True)  25.7 us
    all_to_all x2, waiting for transfers between devices, bring_back(): lax.all_to_all(partial_value.reshape(home_count, -1, width), 'expert', sp...  21.6 us
    all_to_all x2, starting transfers between devices, send_out(): lax.all_to_all(widened, 'expert', split_axis=0, concat_axis=0, tiled=True)  11.5 us
    all_to_all x2, starting transfers between devices, bring_back(): lax.all_to_all(partial_value.reshape(home_count, -1, width), 'expert', sp...  10 us
    concatenate x1, other arithmetic, shards(): jnp.concatenate([lax.dot_general(token_rows, gate_rows, contract_first, p...  9.41 us
  transfers between devices with their start and end apart: 8, of which 7 were waited for; matrix products, arithmetic and copies ran while one was open for 11% of the time, Pallas kernels for 0%

commit v1 on v0

v1 whole, which is shorter than its diff:
```python
import functools

import jax
import jax.numpy as jnp
from jax import lax
from jax.experimental import pallas as pl
from jax.experimental.pallas import tpu as pltpu
from jax.sharding import PartitionSpec as P

SPLIT = 8
BF = jnp.bfloat16
F32 = jnp.float32
AXES = ("dp", "expert")
NT = (((1,), (1,)), ((), ()))
TN = (((0,), (0,)), ((), ()))
VMEM_LIMIT = 48 * 1024 * 1024


def mm(a, b, dims=None):
    if dims is None:
        return jnp.dot(a, b, preferred_element_type=F32)
    return lax.dot_general(a, b, dims, preferred_element_type=F32)


def call(body, out_shape, n_smem, n_vmem, flops=0, moved=0, scratch=()):
    specs = [pl.BlockSpec(memory_space=pltpu.SMEM)] * n_smem
    specs += [pl.BlockSpec(memory_space=pltpu.VMEM)] * n_vmem
    return pl.pallas_call(
        body,
        out_shape=out_shape,
        in_specs=specs,
        out_specs=jax.tree.map(lambda _: pl.BlockSpec(memory_space=pltpu.VMEM), out_shape),
        scratch_shapes=list(scratch),
        compiler_params=pltpu.CompilerParams(vmem_limit_bytes=VMEM_LIMIT),
        cost_estimate=pl.CostEstimate(flops=flops, bytes_accessed=moved, transcendentals=0),
    )


def slot_values(read, count, slots, expert, experts, axis):
    shape = (count, 1) if axis == 0 else (1, count)
    place = lax.broadcasted_iota(jnp.int32, shape, axis)
    value = None
    for k in range(experts):
        e = lax.rem(expert + k, experts)
        for j in range(2 * slots):
            here = read(e, j % slots)
            if value is None:
                value = jnp.full(shape, here)
            else:
                value = jnp.where(place == k * 2 * slots + j, here, value)
    return value


def own_expert(experts):
    return lax.div(lax.axis_index("expert"), SPLIT)


def gather_body(n_dp, experts, slots, routes, gates, tokens, cot, *outs):
    batch = lax.axis_index("dp")
    expert = own_expert(experts)
    count = 2 * slots * experts
    block = tokens.shape[0]
    half = tokens.shape[1] // n_dp
    pos = slot_values(lambda e, s: routes[e, s], count, slots, expert, experts, 0)
    gate = slot_values(lambda e, s: gates[e, s], count, slots, expert, experts, 0)
    is_token = lax.rem(lax.broadcasted_iota(jnp.int32, (count, 1), 0), 2 * slots) < slots
    scale = jnp.where(is_token, 1.0, gate)
    hit = lax.broadcasted_iota(jnp.int32, (count, block), 1) == pos
    pick_token = jnp.where(hit & is_token, 1.0, 0.0).astype(BF)
    pick_cot = jnp.where(hit & ~is_token, 1.0, 0.0).astype(BF)
    for dx in range(n_dp):
        at = pl.ds(pl.multiple_of(lax.rem(batch + dx, n_dp) * half, 128), half)
        rows = mm(pick_token, tokens[:, at]) + mm(pick_cot, cot[:, at])
        rows = (rows * scale).astype(BF)
        for k in range(experts):
            outs[dx * experts + k][...] = rows[k * 2 * slots : (k + 1) * 2 * slots]


def arrange_body(n_dp, experts, slots, *refs):
    *msgs, out, wide = refs
    batch = lax.axis_index("dp")
    each = 2 * slots
    total = each * n_dp * experts
    for m, msg in enumerate(msgs):
        wide[m * each : (m + 1) * each, :] = msg[...].astype(F32)
    r = lax.broadcasted_iota(jnp.int32, (total, 1), 0)
    kind, rest = lax.div(r, total // 2), lax.rem(r, total // 2)
    b, rest = lax.div(rest, experts * slots), lax.rem(rest, experts * slots)
    k, s = lax.div(rest, slots), lax.rem(rest, slots)
    dx = lax.rem(batch - b + n_dp, n_dp)
    source = (dx * experts + k) * each + kind * slots + s
    pick = lax.broadcasted_iota(jnp.int32, (total, total), 1) == source
    out[...] = mm(jnp.where(pick, 1.0, 0.0).astype(BF), wide[...].astype(BF)).astype(BF)


def forward_body(*refs):
    *pieces, wg, wu, wd, xs, ys, part, part_sent = refs
    n = pieces[0].shape[0] // 2
    hid = wg.shape[2]
    for q, piece in enumerate(pieces):
        xs[q * n : (q + 1) * n, :] = piece[:n, :]
        ys[q * n : (q + 1) * n, :] = piece[n:, :]
    for i, (rows, w) in enumerate(((xs, wg), (xs, wu), (ys, wd))):
        got = mm(rows[...], w[0])
        part[:, i * hid : (i + 1) * hid] = got
        part_sent[:, i * hid : (i + 1) * hid] = got.astype(BF)


def backward_body(n_recv, *refs):
    part, *rest = refs
    recv, rest = rest[:n_recv], rest[n_recv:]
    wg, wu, wd, hidden, rows_a, rows_b, own, sib = rest
    hid = wg.shape[2]
    total = part[...]
    for other in recv:
        total = total + other[...].astype(F32)
    g, u, q = total[:, :hid], total[:, hid : 2 * hid], total[:, 2 * hid :]
    sig = jax.nn.sigmoid(g)
    h = (g * sig * u).astype(BF)
    a = (q * u * sig * (1.0 + g * (1.0 - sig))).astype(BF)
    b = (q * g * sig).astype(BF)
    hidden[...] = h
    rows_a[...] = a
    rows_b[...] = b
    p = mm(h, wd[0], NT).astype(BF)
    e = (mm(a, wg[0], NT) + mm(b, wu[0], NT)).astype(BF)
    n = part.shape[0] // SPLIT
    for piece in range(SPLIT):
        out = own if piece % 2 == 0 else sib
        at = (piece // 2) * 2 * n
        out[at : at + n, :] = p[piece * n : (piece + 1) * n]
        out[at + n : at + 2 * n, :] = e[piece * n : (piece + 1) * n]


def pair_sum_body(own, got, *outs):
    n = own.shape[0] // len(outs)
    for j, out in enumerate(outs):
        at = slice(j * n, (j + 1) * n)
        out[...] = (own[at, :].astype(F32) + got[at, :].astype(F32)).astype(BF)


def return_body(n_dp, experts, slots, n_in, *refs):
    ins, outs = refs[:n_in], refs[n_in:]
    batch = lax.axis_index("dp")
    each = 2 * slots
    total = each * n_dp * experts
    value = ins[0][...].astype(F32)
    for other in ins[1:]:
        value = value + other[...].astype(F32)
    r = lax.broadcasted_iota(jnp.int32, (total, 1), 0)
    m, j = lax.div(r, each), lax.rem(r, each)
    dx, k = lax.div(m, experts), lax.rem(m, experts)
    kind, s = lax.div(j, slots), lax.rem(j, slots)
    b = lax.rem(batch - dx + n_dp, n_dp)
    source = kind * (total // 2) + (b * experts + k) * slots + s
    pick = lax.broadcasted_iota(jnp.int32, (total, total), 1) == source
    rows = mm(jnp.where(pick, 1.0, 0.0).astype(BF), value.astype(BF)).astype(BF)
    for i, out in enumerate(outs):
        out[...] = rows[i * each : (i + 1) * each]


def home_body(n_dp, experts, slots, routes, gates, *refs):
    *msgs, layer_out, token_grad, wide = refs
    batch = lax.axis_index("dp")
    expert = own_expert(experts)
    each = 2 * slots
    count = each * experts
    block = layer_out.shape[0]
    half = layer_out.shape[1] // n_dp
    pos = slot_values(lambda e, s: routes[e, s], count, slots, expert, experts, 1)
    gate = slot_values(lambda e, s: gates[e, s], count, slots, expert, experts, 0)
    is_out = lax.rem(lax.broadcasted_iota(jnp.int32, (count, 1), 0), each) < slots
    is_out_lane = lax.rem(lax.broadcasted_iota(jnp.int32, (1, count), 1), each) < slots
    scale = jnp.where(is_out, gate, 1.0)
    hit = lax.broadcasted_iota(jnp.int32, (block, count), 0) == pos
    put_out = jnp.where(hit & is_out_lane, 1.0, 0.0).astype(BF)
    put_grad = jnp.where(hit & ~is_out_lane, 1.0, 0.0).astype(BF)
    for dx in range(n_dp):
        at = pl.ds(pl.multiple_of(lax.rem(batch + dx, n_dp) * half, 128), half)
        for k in range(experts):
            wide[k * each : (k + 1) * each, :] = msgs[dx * experts + k][...].astype(F32)
        value = wide[...] * scale
        high = value.astype(BF)
        low = (value - high.astype(F32)).astype(BF)
        layer_out[:, at] = (mm(put_out, high) + mm(put_out, low)).astype(BF)
        token_grad[:, at] = mm(put_grad, high).astype(BF)


def grads_body(xs, ys, rows_a, rows_b, hidden, gate_grad, up_grad, down_grad):
    gate_grad[0] = mm(xs[...], rows_a[...], TN).astype(BF)
    up_grad[0] = mm(xs[...], rows_b[...], TN).astype(BF)
    down_grad[0] = mm(ys[...], hidden[...], TN).astype(BF)


def shards(n_dp, n_exp, tokens, routes, gate_values, wg, wu, wd, cot):
    block, width = tokens.shape
    experts = routes.shape[1]
    slots = routes.shape[2]
    hid = wg.shape[2]
    half = width // n_dp
    each = 2 * slots
    block_rows = each * n_dp * experts
    n_rows = block_rows // 2 * SPLIT
    n_msg = n_dp * experts
    sds = jax.ShapeDtypeStruct

    def home_perm(dx, k, sign):
        return [
            (
                d * n_exp + i,
                (d + sign * dx) % n_dp * n_exp + (i // SPLIT + sign * k) % experts * SPLIT + i % SPLIT,
            )
            for d in range(n_dp)
            for i in range(n_exp)
        ]

    def part_perm(q):
        return [(d * n_exp + i, d * n_exp + (i ^ q)) for d in range(n_dp) for i in range(n_exp)]

    def batch_perm(dx):
        return [
            (d * n_exp + i, (d + dx) % n_dp * n_exp + i) for d in range(n_dp) for i in range(n_exp)
        ]

    def send(x, perm):
        return lax.ppermute(x, AXES, perm)

    kinds = [(dx, k) for dx in range(n_dp) for k in range(experts)]
    small = [sds((each, half), BF)] * n_msg
    msgs = call(
        functools.partial(gather_body, n_dp, experts, slots), small, 2, 2, moved=4 * block * width
    )(routes[0], gate_values[0], tokens, cot)
    got = [m if kind == (0, 0) else send(m, home_perm(*kind, 1)) for kind, m in zip(kinds, msgs)]
    piece = call(
        functools.partial(arrange_body, n_dp, experts, slots),
        sds((block_rows, half), BF),
        0,
        n_msg,
        scratch=[pltpu.VMEM((block_rows, half), F32)],
    )(*got)
    pieces = [None] * SPLIT
    for q in range(0, SPLIT, 2):
        pieces[q] = piece if q == 0 else send(piece, part_perm(q))
        pieces[q + 1] = send(pieces[q], part_perm(1))
    xs, ys, part, part_sent = call(
        forward_body,
        [
            sds((n_rows, half), BF),
            sds((n_rows, half), BF),
            sds((n_rows, 3 * hid), F32),
            sds((n_rows, 3 * hid), BF),
        ],
        0,
        SPLIT + 3,
    )(*pieces, wg, wu, wd)
    recv = [send(part_sent, batch_perm(dx)) for dx in range(1, n_dp)]
    hidden, rows_a, rows_b, own, sib = call(
        functools.partial(backward_body, n_dp - 1),
        [sds((n_rows, hid), BF)] * 3 + [sds((n_rows, half), BF)] * 2,
        0,
        n_dp + 3,
    )(part, *recv, wg, wu, wd)
    sums = call(pair_sum_body, [sds((block_rows, half), BF)] * (SPLIT // 2), 0, 2)(
        own, send(sib, part_perm(1))
    )
    back = [sums[0]] + [send(sums[j], part_perm(2 * j)) for j in range(1, SPLIT // 2)]
    gate_grad, up_grad, down_grad = call(
        grads_body,
        [sds((1, half, hid), BF)] * 3,
        0,
        5,
        flops=6 * n_rows * half * hid,
        moved=6 * half * hid,
    )(xs, ys, rows_a, rows_b, hidden)
    msgs = call(
        functools.partial(return_body, n_dp, experts, slots, len(back)), small, 0, len(back)
    )(*back)
    got = [m if kind == (0, 0) else send(m, home_perm(*kind, -1)) for kind, m in zip(kinds, msgs)]
    layer_out, token_grad = call(
        functools.partial(home_body, n_dp, experts, slots),
        [sds((block, width), BF)] * 2,
        2,
        n_msg,
        scratch=[pltpu.VMEM((each * experts, half), F32)],
    )(routes[0], gate_values[0], *got)
    return layer_out, token_grad, gate_grad, up_grad, down_grad


def solution(mesh):
    rows = P(AXES, None)
    slots = P(AXES, None, None)
    weights = P("expert", "dp", None)
    return jax.shard_map(
        functools.partial(shards, mesh.shape["dp"], mesh.shape["expert"]),
        mesh=mesh,
        in_specs=(rows, slots, slots, weights, weights, weights, rows),
        out_specs=(rows, rows, weights, weights, weights),
        check_vma=False,
    )
```

time: 221 us -> 58.7 us (0.27)
  waiting for transfers between devices: 137 us -> 26.8 us
  other arithmetic: 15.9 us -> 0 us
  matrix products: 14 us -> 0 us
  between operations: 14 us -> 0.73 us
  local copies, waits for them, and re-layouts: 17.3 us -> 4.36 us
  Pallas kernels: 0 us -> 8.26 us
  starting transfers between devices: 21.7 us -> 18.3 us
    all_gather x3 -> x0, waiting for transfers between devices: 58.4 us -> none  [the longest x1 32.6 us: shards(): lax.all_gather(down_weight, 'dp', axis=1, tiled=True)]
    all_to_all x4 -> x0, waiting for transfers between devices: 49 us -> none  [the longest x2 27.4 us: send_out(): lax.all_to_all(widened, 'expert', split_axis=0, concat_axis=0, tiled=True)]
    reduce_scatter x1 -> x0, waiting for transfers between devices: 28 us -> none  [shards(): lax.psum_scatter(jnp.concatenate([lax.dot_general(token_rows, gate_rows,...]
    ppermute x0 -> x18, waiting for transfers between devices: none -> 26.8 us  [send(): return lax.ppermute(x, AXES, perm)]
    all_to_all x4 -> x0, starting transfers between devices: 21.5 us -> none  [the longest x2 11.5 us: send_out(): lax.all_to_all(widened, 'expert', split_axis=0, concat_axis=0, tiled=True)]
    ppermute x0 -> x18, starting transfers between devices: none -> 18.3 us  [send(): return lax.ppermute(x, AXES, perm)]
    dot_general x9 -> x0, matrix products: 14 us -> none  [the longest x1 2.34 us: shards(): lax.dot_general(gate_rows, full_gate, contract_last, preferred_element_ty...]
    concatenate x1 -> x0, other arithmetic: 9.41 us -> none  [shards(): jnp.concatenate([lax.dot_general(token_rows, gate_rows, contract_first, p...]
  transfers between devices with their start and end apart: 8 -> 18, of which waited for: 7 -> 13; matrix products, arithmetic and copies ran while one was open for 11% -> 0% of each run, Pallas kernels for 0% -> 4%
where the time goes in v1:
time: 58.7 us; the launch traced here: 58.4 us
  waiting for transfers between devices  26.8 us (46%)
  starting transfers between devices  18.3 us (31%)
  Pallas kernels  8.26 us (14%)
  local copies, waits for them, and re-layouts  4.36 us (7%)
  between operations  0.73 us (1%)
    ppermute x18, waiting for transfers between devices, send(): return lax.ppermute(x, AXES, perm)  26.8 us
    ppermute x18, starting transfers between devices, send(): return lax.ppermute(x, AXES, perm)  18.3 us
    unnamed x14, local copies, waits for them, and re-layouts  4.36 us
    pallas_call x1, Pallas kernels, shards(): call(functools.partial(home_body, n_dp, experts, slots), [sds((block, wid...  2.72 us
    pallas_call x1, Pallas kernels, shards(): call(grads_body, [sds((1, half, hid), BF)] * 3, 0, 5, flops=6 * n_rows *...  2.38 us
  transfers between devices with their start and end apart: 18, of which 13 were waited for; matrix products, arithmetic and copies ran while one was open for 0% of the time, Pallas kernels for 4%

profile of v1, /device:TPU:0, one launch (start us, length us, event | category | flops | bytes accessed | tf_op | source)
XLA Modules:
  0.0 58.4 jit_solution(13254319977670290411)
XLA Ops:
  0.7 0.7 %copy-done.6 = f32[1,2,4]{2,1,0:T(2,128)S(1)} copy-done((f32[1,2,4]{2,1,0:T(2,128)S(1)}, f32[1,2,4]{2,1,0:T(2,128)}, u32[]{:S(2)}) %copy-start.6) | copy-done | bytes 56
  1.3 0.0 copy-done.5
  1.3 1.2 %copy-done.3 = bf16[128,4096]{1,0:T(8,128)(2,1)S(1)} copy-done((bf16[128,4096]{1,0:T(8,128)(2,1)S(1)}, bf16[128,4096]{1,0:T(8,128)(2,1)}, u32[]{:S(2)}) %copy-start.3) | copy-done | bytes 1048600
  2.6 1.2 %copy-done.4 = bf16[128,4096]{1,0:T(8,128)(2,1)S(1)} copy-done((bf16[128,4096]{1,0:T(8,128)(2,1)S(1)}, bf16[128,4096]{1,0:T(8,128)(2,1)}, u32[]{:S(2)}) %copy-start.4) | copy-done | bytes 1048600
  3.8 1.0 %shard_map.110 = (bf16[8,2048]{1,0:T(8,128)(2,1)S(1)}, bf16[8,2048]{1,0:T(8,128)(2,1)S(1)}, bf16[8,2048]{1,0:T(8,128)(2,1)S(1)}, bf16[8,2048]{1,0:T(8,128)(2,1)S(1)}) custom-call(s32[2,4]{1,0:T(2,128)S(1)} %bitcast.2, f32[2,4]{1,0:T(2,128)S(1)} %bitcast.4, bf16[128,4096]{1,0:T(8,128)(2,1)S(1)} %copy-done.3, bf16[128,4096]{1,0:T(8,128)(2,1)S(1)} %copy-done.4), custom_call_target="tpu_custom_call" | custom-call | bytes 2097152 | tf_op jit(solution)/shard_map/pallas_call | solution.py:230
  4.7 4.1 %collective-permute-start = (bf16[8,2048]{1,0:T(8,128)(2,1)S(1)}, bf16[8,2048]{1,0:T(8,128)(2,1)S(1)}, u32[]{:S(2)}, u32[]{:S(2)}) collective-permute-start(bf16[8,2048]{1,0:T(8,128)(2,1)S(1)} %get-tuple-element.32), channel_id=1, source_target_pairs={{0,8},{1,9},{2,10},{3,11},{4,12},{5,13},{6,14},{7,15},{8,0},{9,1},... | collective-permute-start | bytes 98312 | tf_op jit(solution)/shard_map/ppermute | solution.py:226
  8.8 1.5 %collective-permute-start.1 = (bf16[8,2048]{1,0:T(8,128)(2,1)S(1)}, bf16[8,2048]{1,0:T(8,128)(2,1)S(1)}, u32[]{:S(2)}, u32[]{:S(2)}) collective-permute-start(bf16[8,2048]{1,0:T(8,128)(2,1)S(1)} %get-tuple-element.33), channel_id=1, source_target_pairs={{0,16},{1,17},{2,18},{3,19},{4,20},{5,21},{6,22},{7,23},{8,24},{9,... | collective-permute-start | bytes 98312 | tf_op jit(solution)/shard_map/ppermute | solution.py:226
  10.3 0.0 collective-permute-start.2
  10.4 0.7 %collective-permute-done.refs_1_ = bf16[8,2048]{1,0:T(8,128)(2,1)S(1)} collective-permute-done((bf16[8,2048]{1,0:T(8,128)(2,1)S(1)}, bf16[8,2048]{1,0:T(8,128)(2,1)S(1)}, u32[]{:S(2)}, u32[]{:S(2)}) %collective-permute-start) | collective-permute-done | bytes 32800 | tf_op jit(solution)/shard_map/ppermute | solution.py:226
  11.1 1.7 %collective-permute-done.1.refs_2_ = bf16[8,2048]{1,0:T(8,128)(2,1)S(1)} collective-permute-done((bf16[8,2048]{1,0:T(8,128)(2,1)S(1)}, bf16[8,2048]{1,0:T(8,128)(2,1)S(1)}, u32[]{:S(2)}, u32[]{:S(2)}) %collective-permute-start.1) | collective-permute-done | bytes 32800 | tf_op jit(solution)/shard_map/ppermute | solution.py:226
  12.7 3.3 %collective-permute-done.2.refs_3_ = bf16[8,2048]{1,0:T(8,128)(2,1)S(1)} collective-permute-done((bf16[8,2048]{1,0:T(8,128)(2,1)S(1)}, bf16[8,2048]{1,0:T(8,128)(2,1)S(1)}, u32[]{:S(2)}, u32[]{:S(2)}) %collective-permute-start.2) | collective-permute-done | bytes 32800 | tf_op jit(solution)/shard_map/ppermute | solution.py:226
  16.0 0.2 shard_map.111.refs_0_
  16.2 1.6 %collective-permute-start.4 = (bf16[32,2048]{1,0:T(8,128)(2,1)S(1)}, bf16[32,2048]{1,0:T(8,128)(2,1)S(1)}, u32[]{:S(2)}, u32[]{:S(2)}) collective-permute-start(bf16[32,2048]{1,0:T(8,128)(2,1)S(1)} %shard_map.111.refs_0_), channel_id=1, source_target_pairs={{0,2},{1,3},{2,0},{3,1},{4,6},{5,7},{6,4},{7,5},{8,10},{9,11},{10,... | collective-permute-start | bytes 393224 | tf_op jit(solution)/shard_map/ppermute | solution.py:226
  17.8 1.6 %collective-permute-start.6 = (bf16[32,2048]{1,0:T(8,128)(2,1)S(1)}, bf16[32,2048]{1,0:T(8,128)(2,1)S(1)}, u32[]{:S(2)}, u32[]{:S(2)}) collective-permute-start(bf16[32,2048]{1,0:T(8,128)(2,1)S(1)} %shard_map.111.refs_0_), channel_id=1, source_target_pairs={{0,4},{1,5},{2,6},{3,7},{4,0},{5,1},{6,2},{7,3},{8,12},{9,13},{10,... | collective-permute-start | bytes 393224 | tf_op jit(solution)/shard_map/ppermute | solution.py:226
  19.4 0.4 collective-permute-start.8
  19.8 2.9 %collective-permute-done.4.refs_2_ = bf16[32,2048]{1,0:T(8,128)(2,1)S(1)} collective-permute-done((bf16[32,2048]{1,0:T(8,128)(2,1)S(1)}, bf16[32,2048]{1,0:T(8,128)(2,1)S(1)}, u32[]{:S(2)}, u32[]{:S(2)}) %collective-permute-start.4) | collective-permute-done | bytes 131104 | tf_op jit(solution)/shard_map/ppermute | solution.py:226
  22.6 0.0 collective-permute-start.5
  22.7 0.1 collective-permute-done.6.refs_4_
  22.8 0.4 collective-permute-start.7
  23.2 2.1 %collective-permute-done.8.refs_6_ = bf16[32,2048]{1,0:T(8,128)(2,1)S(1)} collective-permute-done((bf16[32,2048]{1,0:T(8,128)(2,1)S(1)}, bf16[32,2048]{1,0:T(8,128)(2,1)S(1)}, u32[]{:S(2)}, u32[]{:S(2)}) %collective-permute-start.8) | collective-permute-done | bytes 131104 | tf_op jit(solution)/shard_map/ppermute | solution.py:226
  25.2 0.0 collective-permute-start.9
  25.2 0.0 collective-permute-done.3.refs_1_
  25.2 0.0 collective-permute-done.5.refs_3_
  25.3 0.0 collective-permute-done.7.refs_5_
  25.3 1.3 %collective-permute-done.9.refs_7_ = bf16[32,2048]{1,0:T(8,128)(2,1)S(1)} collective-permute-done((bf16[32,2048]{1,0:T(8,128)(2,1)S(1)}, bf16[32,2048]{1,0:T(8,128)(2,1)S(1)}, u32[]{:S(2)}, u32[]{:S(2)}) %collective-permute-start.9) | collective-permute-done | bytes 131104 | tf_op jit(solution)/shard_map/ppermute | solution.py:226
  26.6 1.2 %copy-done.2 = bf16[1,2048,256]{2,1,0:T(8,128)(2,1)S(1)} copy-done((bf16[1,2048,256]{2,1,0:T(8,128)(2,1)S(1)}, bf16[1,2048,256]{2,1,0:T(8,128)(2,1)}, u32[]{:S(2)}) %copy-start.2) | copy-done | bytes 1048600
  27.8 0.6 shard_map.112
  28.4 0.6 %collective-permute-start.10 = (bf16[128,768]{1,0:T(8,128)(2,1)S(1)}, bf16[128,768]{1,0:T(8,128)(2,1)S(1)}, u32[]{:S(2)}, u32[]{:S(2)}) collective-permute-start(bf16[128,768]{1,0:T(8,128)(2,1)S(1)} %get-tuple-element.36), channel_id=1, source_target_pairs={{0,16},{1,17},{2,18},{3,19},{4,20},{5,21},{6,22},{7,23},{8,24},{9,... | collective-permute-start | bytes 589832 | tf_op jit(solution)/shard_map/ppermute | solution.py:226
  29.0 6.4 %collective-permute-done.10.refs_1_ = bf16[128,768]{1,0:T(8,128)(2,1)S(1)} collective-permute-done((bf16[128,768]{1,0:T(8,128)(2,1)S(1)}, bf16[128,768]{1,0:T(8,128)(2,1)S(1)}, u32[]{:S(2)}, u32[]{:S(2)}) %collective-permute-start.10) | collective-permute-done | bytes 196640 | tf_op jit(solution)/shard_map/ppermute | solution.py:226
  35.4 1.1 %shard_map.113 = (bf16[128,256]{1,0:T(8,128)(2,1)S(1)}, bf16[128,256]{1,0:T(8,128)(2,1)S(1)}, bf16[128,256]{1,0:T(8,128)(2,1)S(1)}, bf16[128,2048]{1,0:T(8,128)(2,1)S(1)}, bf16[128,2048]{1,0:T(8,128)(2,1)S(1)}) custom-call(f32[128,768]{1,0:T(8,128)S(1)} %get-tuple-element.35.refs_0_, bf16[128,768]{1,0:T(8,128)(2,1)S(1)} %collective-permute-done.10.refs_1_, ...), custom_call_target="tpu_custom_call" | custom-call | tf_op jit(solution)/shard_map/pallas_call | solution.py:257
  36.6 0.1 collective-permute-start.11
  36.7 1.9 %collective-permute-done.11.got = bf16[128,2048]{1,0:T(8,128)(2,1)S(1)} collective-permute-done((bf16[128,2048]{1,0:T(8,128)(2,1)S(1)}, bf16[128,2048]{1,0:T(8,128)(2,1)S(1)}, u32[]{:S(2)}, u32[]{:S(2)}) %collective-permute-start.11) | collective-permute-done | bytes 524320 | tf_op jit(solution)/shard_map/ppermute | solution.py:226
  38.6 0.1 shard_map.114
  38.7 0.6 collective-permute-start.12
  39.2 1.5 %collective-permute-start.13 = (bf16[32,2048]{1,0:T(8,128)(2,1)S(1)}, bf16[32,2048]{1,0:T(8,128)(2,1)S(1)}, u32[]{:S(2)}, u32[]{:S(2)}) collective-permute-start(bf16[32,2048]{1,0:T(8,128)(2,1)S(1)} %get-tuple-element.41), channel_id=1, source_target_pairs={{0,4},{1,5},{2,6},{3,7},{4,0},{5,1},{6,2},{7,3},{8,12},{9,13},{10,... | collective-permute-start | bytes 393224 | tf_op jit(solution)/shard_map/ppermute | solution.py:226
  40.7 1.5 %collective-permute-start.14 = (bf16[32,2048]{1,0:T(8,128)(2,1)S(1)}, bf16[32,2048]{1,0:T(8,128)(2,1)S(1)}, u32[]{:S(2)}, u32[]{:S(2)}) collective-permute-start(bf16[32,2048]{1,0:T(8,128)(2,1)S(1)} %get-tuple-element.42), channel_id=1, source_target_pairs={{0,6},{1,7},{2,4},{3,5},{4,2},{5,3},{6,0},{7,1},{8,14},{9,15},{10,... | collective-permute-start | bytes 393224 | tf_op jit(solution)/shard_map/ppermute | solution.py:226
  42.2 2.0 %collective-permute-done.12.refs_1_ = bf16[32,2048]{1,0:T(8,128)(2,1)S(1)} collective-permute-done((bf16[32,2048]{1,0:T(8,128)(2,1)S(1)}, bf16[32,2048]{1,0:T(8,128)(2,1)S(1)}, u32[]{:S(2)}, u32[]{:S(2)}) %collective-permute-start.12) | collective-permute-done | bytes 131104 | tf_op jit(solution)/shard_map/ppermute | solution.py:226
  44.3 1.4 %collective-permute-done.13.refs_2_ = bf16[32,2048]{1,0:T(8,128)(2,1)S(1)} collective-permute-done((bf16[32,2048]{1,0:T(8,128)(2,1)S(1)}, bf16[32,2048]{1,0:T(8,128)(2,1)S(1)}, u32[]{:S(2)}, u32[]{:S(2)}) %collective-permute-start.13) | collective-permute-done | bytes 131104 | tf_op jit(solution)/shard_map/ppermute | solution.py:226
  45.6 2.6 %collective-permute-done.14.refs_3_ = bf16[32,2048]{1,0:T(8,128)(2,1)S(1)} collective-permute-done((bf16[32,2048]{1,0:T(8,128)(2,1)S(1)}, bf16[32,2048]{1,0:T(8,128)(2,1)S(1)}, u32[]{:S(2)}, u32[]{:S(2)}) %collective-permute-start.14) | collective-permute-done | bytes 131104 | tf_op jit(solution)/shard_map/ppermute | solution.py:226
  48.3 0.2 shard_map.115
  48.5 0.6 %collective-permute-start.15 = (bf16[8,2048]{1,0:T(8,128)(2,1)S(1)}, bf16[8,2048]{1,0:T(8,128)(2,1)S(1)}, u32[]{:S(2)}, u32[]{:S(2)}) collective-permute-start(bf16[8,2048]{1,0:T(8,128)(2,1)S(1)} %get-tuple-element.44), channel_id=1, source_target_pairs={{0,8},{1,9},{2,10},{3,11},{4,12},{5,13},{6,14},{7,15},{8,0},{9,1},... | collective-permute-start | bytes 98312 | tf_op jit(solution)/shard_map/ppermute | solution.py:226
  49.1 0.5 collective-permute-start.16
  49.7 3.3 %collective-permute-start.17 = (bf16[8,2048]{1,0:T(8,128)(2,1)S(1)}, bf16[8,2048]{1,0:T(8,128)(2,1)S(1)}, u32[]{:S(2)}, u32[]{:S(2)}) collective-permute-start(bf16[8,2048]{1,0:T(8,128)(2,1)S(1)} %get-tuple-element.46), channel_id=1, source_target_pairs={{0,24},{1,25},{2,26},{3,27},{4,28},{5,29},{6,30},{7,31},{8,16},{9,... | collective-permute-start | bytes 98312 | tf_op jit(solution)/shard_map/ppermute | solution.py:226
  52.9 2.4 %shard_map.117 = (bf16[1,2048,256]{2,1,0:T(8,128)(2,1)}, bf16[1,2048,256]{2,1,0:T(8,128)(2,1)}, bf16[1,2048,256]{2,1,0:T(8,128)(2,1)}) custom-call(bf16[128,2048]{1,0:T(8,128)(2,1)S(1)} %get-tuple-element.49.xs, bf16[128,2048]{1,0:T(8,128)(2,1)S(1)} %get-tuple-element.50.ys, bf16[128,256]{1,0:T(8,128)(2,1)S(1)} %get-tuple-element.51.rows_a, ...), custom_call_target="tpu_custom_call" | custom-call | flops 402653184 | bytes 3145728 | tf_op jit(solution)/shard_map/pallas_call | solution.py:267
  55.3 0.0 collective-permute-done.15.refs_1_
  55.3 0.0 collective-permute-done.16.refs_2_
  55.3 0.4 collective-permute-done.17.refs_3_
  55.7 2.7 %shard_map.116 = (bf16[128,4096]{1,0:T(8,128)(2,1)}, bf16[128,4096]{1,0:T(8,128)(2,1)}) custom-call(s32[2,4]{1,0:T(2,128)S(1)} %bitcast.3, f32[2,4]{1,0:T(2,128)S(1)} %bitcast.5, bf16[8,2048]{1,0:T(8,128)(2,1)S(1)} %get-tuple-element.43.refs_0_, bf16[8,2048]{1,0:T(8,128)(2,1)S(1)} %collective-permute-done.15.refs_1_, ...), custom_call_target="tpu_custom_call" | custom-call | tf_op jit(solution)/shard_map/pallas_call | solution.py:279
  (10 shorter events, 0.0 us)
Async XLA Ops:
  0.6 0.7 %copy-start.6 = (f32[1,2,4]{2,1,0:T(2,128)S(1)}, f32[1,2,4]{2,1,0:T(2,128)}, u32[]{:S(2)}) copy-start(f32[1,2,4]{2,1,0:T(2,128)} %param.9) | copy-start | bytes 100
  0.6 0.7 %copy-start.5 = (s32[1,2,4]{2,1,0:T(2,128)S(1)}, s32[1,2,4]{2,1,0:T(2,128)}, u32[]{:S(2)}) copy-start(s32[1,2,4]{2,1,0:T(2,128)} %param.8) | copy-start | bytes 100
  1.3 1.2 %copy-start.3 = (bf16[128,4096]{1,0:T(8,128)(2,1)S(1)}, bf16[128,4096]{1,0:T(8,128)(2,1)}, u32[]{:S(2)}) copy-start(bf16[128,4096]{1,0:T(8,128)(2,1)} %tokens.1) | copy-start | bytes 3145732
  2.6 1.2 %copy-start.4 = (bf16[128,4096]{1,0:T(8,128)(2,1)S(1)}, bf16[128,4096]{1,0:T(8,128)(2,1)}, u32[]{:S(2)}) copy-start(bf16[128,4096]{1,0:T(8,128)(2,1)} %cot.1) | copy-start | bytes 3145732
  3.8 22.8 %copy-start = (bf16[1,2048,256]{2,1,0:T(8,128)(2,1)S(1)}, bf16[1,2048,256]{2,1,0:T(8,128)(2,1)}, u32[]{:S(2)}) copy-start(bf16[1,2048,256]{2,1,0:T(8,128)(2,1)} %refs_2_.1) | copy-start | bytes 3145732
  3.8 22.8 %copy-start.1 = (bf16[1,2048,256]{2,1,0:T(8,128)(2,1)S(1)}, bf16[1,2048,256]{2,1,0:T(8,128)(2,1)}, u32[]{:S(2)}) copy-start(bf16[1,2048,256]{2,1,0:T(8,128)(2,1)} %refs_3_.1) | copy-start | bytes 3145732
  4.7 6.3 %collective-permute-start = (bf16[8,2048]{1,0:T(8,128)(2,1)S(1)}, bf16[8,2048]{1,0:T(8,128)(2,1)S(1)}, u32[]{:S(2)}, u32[]{:S(2)}) collective-permute-start(bf16[8,2048]{1,0:T(8,128)(2,1)S(1)} %get-tuple-element.32), channel_id=1, source_target_pairs={{0,8},{1,9},{2,10},{3,11},{4,12},{5,13},{6,14},{7,15},{8,0},{9,1},... | collective-permute-start | bytes 98312 | tf_op jit(solution)/shard_map/ppermute | solution.py:226
  8.8 3.9 %collective-permute-start.1 = (bf16[8,2048]{1,0:T(8,128)(2,1)S(1)}, bf16[8,2048]{1,0:T(8,128)(2,1)S(1)}, u32[]{:S(2)}, u32[]{:S(2)}) collective-permute-start(bf16[8,2048]{1,0:T(8,128)(2,1)S(1)} %get-tuple-element.33), channel_id=1, source_target_pairs={{0,16},{1,17},{2,18},{3,19},{4,20},{5,21},{6,22},{7,23},{8,24},{9,... | collective-permute-start | bytes 98312 | tf_op jit(solution)/shard_map/ppermute | solution.py:226
  10.3 5.7 %collective-permute-start.2 = (bf16[8,2048]{1,0:T(8,128)(2,1)S(1)}, bf16[8,2048]{1,0:T(8,128)(2,1)S(1)}, u32[]{:S(2)}, u32[]{:S(2)}) collective-permute-start(bf16[8,2048]{1,0:T(8,128)(2,1)S(1)} %get-tuple-element.34), channel_id=1, source_target_pairs={{0,24},{1,25},{2,26},{3,27},{4,28},{5,29},{6,30},{7,31},{8,16},{9,... | collective-permute-start | bytes 98312 | tf_op jit(solution)/shard_map/ppermute | solution.py:226
  16.2 6.4 %collective-permute-start.4 = (bf16[32,2048]{1,0:T(8,128)(2,1)S(1)}, bf16[32,2048]{1,0:T(8,128)(2,1)S(1)}, u32[]{:S(2)}, u32[]{:S(2)}) collective-permute-start(bf16[32,2048]{1,0:T(8,128)(2,1)S(1)} %shard_map.111.refs_0_), channel_id=1, source_target_pairs={{0,2},{1,3},{2,0},{3,1},{4,6},{5,7},{6,4},{7,5},{8,10},{9,11},{10,... | collective-permute-start | bytes 393224 | tf_op jit(solution)/shard_map/ppermute | solution.py:226
  17.8 5.0 %collective-permute-start.6 = (bf16[32,2048]{1,0:T(8,128)(2,1)S(1)}, bf16[32,2048]{1,0:T(8,128)(2,1)S(1)}, u32[]{:S(2)}, u32[]{:S(2)}) collective-permute-start(bf16[32,2048]{1,0:T(8,128)(2,1)S(1)} %shard_map.111.refs_0_), channel_id=1, source_target_pairs={{0,4},{1,5},{2,6},{3,7},{4,0},{5,1},{6,2},{7,3},{8,12},{9,13},{10,... | collective-permute-start | bytes 393224 | tf_op jit(solution)/shard_map/ppermute | solution.py:226
  19.4 5.9 %collective-permute-start.8 = (bf16[32,2048]{1,0:T(8,128)(2,1)S(1)}, bf16[32,2048]{1,0:T(8,128)(2,1)S(1)}, u32[]{:S(2)}, u32[]{:S(2)}) collective-permute-start(bf16[32,2048]{1,0:T(8,128)(2,1)S(1)} %shard_map.111.refs_0_), channel_id=1, source_target_pairs={{0,6},{1,7},{2,4},{3,5},{4,2},{5,3},{6,0},{7,1},{8,14},{9,15},{10,... | collective-permute-start | bytes 393224 | tf_op jit(solution)/shard_map/ppermute | solution.py:226
  19.8 5.5 %collective-permute-start.3 = (bf16[32,2048]{1,0:T(8,128)(2,1)S(1)}, bf16[32,2048]{1,0:T(8,128)(2,1)S(1)}, u32[]{:S(2)}, u32[]{:S(2)}) collective-permute-start(bf16[32,2048]{1,0:T(8,128)(2,1)S(1)} %shard_map.111.refs_0_), channel_id=1, source_target_pairs={{0,1},{1,0},{2,3},{3,2},{4,5},{5,4},{6,7},{7,6},{8,9},{9,8},{10,11... | collective-permute-start | bytes 393224 | tf_op jit(solution)/shard_map/ppermute | solution.py:226
  22.6 2.6 %collective-permute-start.5 = (bf16[32,2048]{1,0:T(8,128)(2,1)S(1)}, bf16[32,2048]{1,0:T(8,128)(2,1)S(1)}, u32[]{:S(2)}, u32[]{:S(2)}) collective-permute-start(bf16[32,2048]{1,0:T(8,128)(2,1)S(1)} %collective-permute-done.4.refs_2_), channel_id=1, source_target_pairs={{0,1},{1,0},{2,3},{3,2},{4,5},{5,4},{6,7},{7,6},{8,9},{9,8},{10,11... | collective-permute-start | bytes 393224 | tf_op jit(solution)/shard_map/ppermute | solution.py:226
  22.8 2.5 %collective-permute-start.7 = (bf16[32,2048]{1,0:T(8,128)(2,1)S(1)}, bf16[32,2048]{1,0:T(8,128)(2,1)S(1)}, u32[]{:S(2)}, u32[]{:S(2)}) collective-permute-start(bf16[32,2048]{1,0:T(8,128)(2,1)S(1)} %collective-permute-done.6.refs_4_), channel_id=1, source_target_pairs={{0,1},{1,0},{2,3},{3,2},{4,5},{5,4},{6,7},{7,6},{8,9},{9,8},{10,11... | collective-permute-start | bytes 393224 | tf_op jit(solution)/shard_map/ppermute | solution.py:226
  25.2 1.3 %collective-permute-start.9 = (bf16[32,2048]{1,0:T(8,128)(2,1)S(1)}, bf16[32,2048]{1,0:T(8,128)(2,1)S(1)}, u32[]{:S(2)}, u32[]{:S(2)}) collective-permute-start(bf16[32,2048]{1,0:T(8,128)(2,1)S(1)} %collective-permute-done.8.refs_6_), channel_id=1, source_target_pairs={{0,1},{1,0},{2,3},{3,2},{4,5},{5,4},{6,7},{7,6},{8,9},{9,8},{10,11... | collective-permute-start | bytes 393224 | tf_op jit(solution)/shard_map/ppermute | solution.py:226
  26.6 1.2 %copy-start.2 = (bf16[1,2048,256]{2,1,0:T(8,128)(2,1)S(1)}, bf16[1,2048,256]{2,1,0:T(8,128)(2,1)}, u32[]{:S(2)}) copy-start(bf16[1,2048,256]{2,1,0:T(8,128)(2,1)} %refs_4_.1) | copy-start | bytes 3145732
  28.4 7.0 %collective-permute-start.10 = (bf16[128,768]{1,0:T(8,128)(2,1)S(1)}, bf16[128,768]{1,0:T(8,128)(2,1)S(1)}, u32[]{:S(2)}, u32[]{:S(2)}) collective-permute-start(bf16[128,768]{1,0:T(8,128)(2,1)S(1)} %get-tuple-element.36), channel_id=1, source_target_pairs={{0,16},{1,17},{2,18},{3,19},{4,20},{5,21},{6,22},{7,23},{8,24},{9,... | collective-permute-start | bytes 589832 | tf_op jit(solution)/shard_map/ppermute | solution.py:226
  36.6 2.0 %collective-permute-start.11 = (bf16[128,2048]{1,0:T(8,128)(2,1)S(1)}, bf16[128,2048]{1,0:T(8,128)(2,1)S(1)}, u32[]{:S(2)}, u32[]{:S(2)}) collective-permute-start(bf16[128,2048]{1,0:T(8,128)(2,1)S(1)} %get-tuple-element.38), channel_id=1, source_target_pairs={{0,1},{1,0},{2,3},{3,2},{4,5},{5,4},{6,7},{7,6},{8,9},{9,8},{10,11... | collective-permute-start | bytes 1572872 | tf_op jit(solution)/shard_map/ppermute | solution.py:226
  38.7 5.6 %collective-permute-start.12 = (bf16[32,2048]{1,0:T(8,128)(2,1)S(1)}, bf16[32,2048]{1,0:T(8,128)(2,1)S(1)}, u32[]{:S(2)}, u32[]{:S(2)}) collective-permute-start(bf16[32,2048]{1,0:T(8,128)(2,1)S(1)} %get-tuple-element.40), channel_id=1, source_target_pairs={{0,2},{1,3},{2,0},{3,1},{4,6},{5,7},{6,4},{7,5},{8,10},{9,11},{10,... | collective-permute-start | bytes 393224 | tf_op jit(solution)/shard_map/ppermute | solution.py:226
  39.2 6.4 %collective-permute-start.13 = (bf16[32,2048]{1,0:T(8,128)(2,1)S(1)}, bf16[32,2048]{1,0:T(8,128)(2,1)S(1)}, u32[]{:S(2)}, u32[]{:S(2)}) collective-permute-start(bf16[32,2048]{1,0:T(8,128)(2,1)S(1)} %get-tuple-element.41), channel_id=1, source_target_pairs={{0,4},{1,5},{2,6},{3,7},{4,0},{5,1},{6,2},{7,3},{8,12},{9,13},{10,... | collective-permute-start | bytes 393224 | tf_op jit(solution)/shard_map/ppermute | solution.py:226
  40.7 7.6 %collective-permute-start.14 = (bf16[32,2048]{1,0:T(8,128)(2,1)S(1)}, bf16[32,2048]{1,0:T(8,128)(2,1)S(1)}, u32[]{:S(2)}, u32[]{:S(2)}) collective-permute-start(bf16[32,2048]{1,0:T(8,128)(2,1)S(1)} %get-tuple-element.42), channel_id=1, source_target_pairs={{0,6},{1,7},{2,4},{3,5},{4,2},{5,3},{6,0},{7,1},{8,14},{9,15},{10,... | collective-permute-start | bytes 393224 | tf_op jit(solution)/shard_map/ppermute | solution.py:226
  48.5 6.8 %collective-permute-start.15 = (bf16[8,2048]{1,0:T(8,128)(2,1)S(1)}, bf16[8,2048]{1,0:T(8,128)(2,1)S(1)}, u32[]{:S(2)}, u32[]{:S(2)}) collective-permute-start(bf16[8,2048]{1,0:T(8,128)(2,1)S(1)} %get-tuple-element.44), channel_id=1, source_target_pairs={{0,8},{1,9},{2,10},{3,11},{4,12},{5,13},{6,14},{7,15},{8,0},{9,1},... | collective-permute-start | bytes 98312 | tf_op jit(solution)/shard_map/ppermute | solution.py:226
  49.1 6.2 %collective-permute-start.16 = (bf16[8,2048]{1,0:T(8,128)(2,1)S(1)}, bf16[8,2048]{1,0:T(8,128)(2,1)S(1)}, u32[]{:S(2)}, u32[]{:S(2)}) collective-permute-start(bf16[8,2048]{1,0:T(8,128)(2,1)S(1)} %get-tuple-element.45), channel_id=1, source_target_pairs={{0,16},{1,17},{2,18},{3,19},{4,20},{5,21},{6,22},{7,23},{8,24},{9,... | collective-permute-start | bytes 98312 | tf_op jit(solution)/shard_map/ppermute | solution.py:226
  49.7 6.1 %collective-permute-start.17 = (bf16[8,2048]{1,0:T(8,128)(2,1)S(1)}, bf16[8,2048]{1,0:T(8,128)(2,1)S(1)}, u32[]{:S(2)}, u32[]{:S(2)}) collective-permute-start(bf16[8,2048]{1,0:T(8,128)(2,1)S(1)} %get-tuple-element.46), channel_id=1, source_target_pairs={{0,24},{1,25},{2,26},{3,27},{4,28},{5,29},{6,30},{7,31},{8,16},{9,... | collective-permute-start | bytes 98312 | tf_op jit(solution)/shard_map/ppermute | solution.py:226

commit v2 on v1

v2 whole, which is shorter than its diff:
```python
import functools
import math

import jax
import jax.numpy as jnp
from jax import lax
from jax.experimental import pallas as pl
from jax.experimental.pallas import tpu as pltpu
from jax.sharding import PartitionSpec as P

SPLIT = 8
BF = jnp.bfloat16
F32 = jnp.float32
AXES = ("dp", "expert")
NT = (((1,), (1,)), ((), ()))
TN = (((0,), (0,)), ((), ()))
ANY = pl.BlockSpec(memory_space=pl.ANY)
HBM = pl.BlockSpec(memory_space=pltpu.HBM)
SMEM = pl.BlockSpec(memory_space=pltpu.SMEM)
VMEM = pl.BlockSpec(memory_space=pltpu.VMEM)


def mm(a, b, dims=None):
    if dims is None:
        return jnp.dot(a, b, preferred_element_type=F32)
    return lax.dot_general(a, b, dims, preferred_element_type=F32)


def in_hbm(x):
    return pltpu.with_memory_space_constraint(x, pltpu.HBM)


def size(x):
    return math.prod(x.shape) * jnp.dtype(x.dtype).itemsize


def call(
    body,
    out_shape,
    args,
    in_specs=None,
    out_specs=None,
    scratch=(),
    extra=0,
    after=(),
    mark=False,
    cost=None,
):
    n_in, n_out = len(args), len(out_shape)
    used = sum(map(size, args)) + sum(map(size, out_shape)) + extra
    in_specs = in_specs or [VMEM] * n_in
    out_specs = out_specs or [VMEM] * n_out

    def whole(*refs):
        ins, rest = refs[:n_in], refs[n_in + len(after) :]
        outs, rest = rest[:n_out], rest[n_out:]
        if mark:
            rest[0][...] = jnp.zeros_like(rest[0])
            rest = rest[1:]
        body(*ins, *outs, *rest)

    return pl.pallas_call(
        whole,
        out_shape=[*out_shape, *[jax.ShapeDtypeStruct((8, 128), F32)] * mark],
        in_specs=[*in_specs, *[ANY] * len(after)],
        out_specs=[*out_specs, *[VMEM] * mark],
        scratch_shapes=list(scratch),
        compiler_params=pltpu.CompilerParams(vmem_limit_bytes=min(2 * used + (4 << 20), 56 << 20)),
        cost_estimate=cost,
    )(*args, *after)


def slot_values(read, count, slots, expert, experts, axis):
    shape = (count, 1) if axis == 0 else (1, count)
    place = lax.broadcasted_iota(jnp.int32, shape, axis)
    value = None
    for k in range(experts):
        e = lax.rem(expert + k, experts)
        for j in range(2 * slots):
            here = read(e, j % slots)
            if value is None:
                value = jnp.full(shape, here)
            else:
                value = jnp.where(place == k * 2 * slots + j, here, value)
    return value


def own_expert(experts):
    return lax.div(lax.axis_index("expert"), SPLIT)


def gather_body(n_dp, experts, slots, routes_in, gates_in, tokens, cot, *refs):
    *outs, both, routes, gates, sems = refs
    batch = lax.axis_index("dp")
    expert = own_expert(experts)
    count = 2 * slots * experts
    block = tokens.shape[0]
    half = tokens.shape[1] // n_dp
    moves = [(routes_in, routes), (gates_in, gates)]
    for dx in range(n_dp):
        at = pl.ds(pl.multiple_of(lax.rem(batch + dx, n_dp) * half, 128), half)
        for i, src in enumerate((tokens, cot)):
            moves.append((src.at[:, at], both.at[dx, pl.ds(i * block, block)]))
    copies = [pltpu.make_async_copy(*move, sems.at[i]) for i, move in enumerate(moves)]
    for copy in copies:
        copy.start()
    for copy in copies[:2]:
        copy.wait()
    pos = slot_values(lambda e, s: routes[e, s], count, slots, expert, experts, 0)
    gate = slot_values(lambda e, s: gates[e, s], count, slots, expert, experts, 0)
    is_token = lax.rem(lax.broadcasted_iota(jnp.int32, (count, 1), 0), 2 * slots) < slots
    scale = jnp.where(is_token, 1.0, gate)
    row = jnp.where(is_token, pos, pos + block)
    hit = lax.broadcasted_iota(jnp.int32, (count, 2 * block), 1) == row
    pick = jnp.where(hit, 1.0, 0.0).astype(BF)
    for dx in range(n_dp):
        for copy in copies[2 + 2 * dx : 4 + 2 * dx]:
            copy.wait()
        rows = (mm(pick, both[dx]) * scale).astype(BF)
        for k in range(experts):
            outs[dx * experts + k][...] = rows[k * 2 * slots : (k + 1) * 2 * slots]


def row_map(n_dp, ks, slots, batch, to_block):
    each = 2 * slots
    total = each * n_dp * ks
    r = lax.broadcasted_iota(jnp.int32, (total, 1), 0)
    if to_block:
        kind, rest = lax.div(r, total // 2), lax.rem(r, total // 2)
        b, rest = lax.div(rest, ks * slots), lax.rem(rest, ks * slots)
        k, s = lax.div(rest, slots), lax.rem(rest, slots)
        dx = lax.rem(batch - b + n_dp, n_dp)
        source = (dx * ks + k) * each + kind * slots + s
    else:
        m, j = lax.div(r, each), lax.rem(r, each)
        dx, k = lax.div(m, ks), lax.rem(m, ks)
        kind, s = lax.div(j, slots), lax.rem(j, slots)
        b = lax.rem(batch - dx + n_dp, n_dp)
        source = kind * (total // 2) + (b * ks + k) * slots + s
    pick = lax.broadcasted_iota(jnp.int32, (total, total), 1) == source
    return jnp.where(pick, 1.0, 0.0).astype(BF)


def arrange_body(n_dp, experts, slots, order, *refs):
    *msgs, out, wide = refs
    each = 2 * slots
    for m, msg in zip(order, msgs):
        wide[m * each : (m + 1) * each, :] = msg[...].astype(F32)
    pick = row_map(n_dp, experts, slots, lax.axis_index("dp"), True)
    out[...] = mm(pick, wide[...].astype(BF)).astype(BF)


def load_body(src, dst, sem):
    copy = pltpu.make_async_copy(src, dst, sem)
    copy.start()
    copy.wait()


def forward_body(*refs):
    *pieces, wg, wu, wd, xs, ys, part, part_sent = refs
    n = pieces[0].shape[0] // 2
    hid = wg.shape[2]
    for q, piece in enumerate(pieces):
        xs[q * n : (q + 1) * n, :] = piece[:n, :]
        ys[q * n : (q + 1) * n, :] = piece[n:, :]
    for i, (rows, w) in enumerate(((xs, wg), (xs, wu), (ys, wd))):
        got = mm(rows[...], w[0])
        part[:, i * hid : (i + 1) * hid] = got
        part_sent[:, i * hid : (i + 1) * hid] = got.astype(BF)


def backward_body(n_recv, *refs):
    part, *rest = refs
    recv, rest = rest[:n_recv], rest[n_recv:]
    wg, wu, wd, rows_h, rows_a, rows_b, own, sib = rest
    hid = wg.shape[2]
    total = part[...]
    for other in recv:
        total = total + other[...].astype(F32)
    g, u, q = total[:, :hid], total[:, hid : 2 * hid], total[:, 2 * hid :]
    sig = jax.nn.sigmoid(g)
    h = (g * sig * u).astype(BF)
    a = (q * u * sig * (1.0 + g * (1.0 - sig))).astype(BF)
    b = (q * g * sig).astype(BF)
    rows_h[...] = h
    rows_a[...] = a
    rows_b[...] = b
    p = mm(h, wd[0], NT).astype(BF)
    e = (mm(a, wg[0], NT) + mm(b, wu[0], NT)).astype(BF)
    n = part.shape[0] // SPLIT
    for piece in range(SPLIT):
        out = own if piece % 2 == 0 else sib
        at = (piece // 2) * 2 * n
        out[at : at + n, :] = p[piece * n : (piece + 1) * n]
        out[at + n : at + 2 * n, :] = e[piece * n : (piece + 1) * n]


def pair_sum_body(own, got, *outs):
    n = own.shape[0] // len(outs)
    for j, out in enumerate(outs):
        at = slice(j * n, (j + 1) * n)
        out[...] = (own[at, :].astype(F32) + got[at, :].astype(F32)).astype(BF)


def return_body(n_dp, ks, slots, n_in, order, *refs):
    ins, outs = refs[:n_in], refs[n_in:]
    each = 2 * slots
    value = ins[0][...].astype(F32)
    for other in ins[1:]:
        value = value + other[...].astype(F32)
    pick = row_map(n_dp, ks, slots, lax.axis_index("dp"), False)
    rows = mm(pick, value.astype(BF)).astype(BF)
    for m, out in zip(order, outs):
        out[...] = rows[m * each : (m + 1) * each]


def home_body(n_dp, experts, order, put_out, put_grad, scale, *refs):
    msgs, outs, (layer_half, grad_half, wide, sems) = refs[:-6], refs[-6:-4], refs[-4:]
    msgs = dict(zip(order, msgs))
    batch = lax.axis_index("dp")
    each = msgs[0].shape[0]
    half = layer_half.shape[2]
    copies = []
    for dx in range(n_dp):
        for k in range(experts):
            wide[k * each : (k + 1) * each, :] = msgs[dx * experts + k][...].astype(F32)
        at = pl.ds(pl.multiple_of(lax.rem(batch + dx, n_dp) * half, 128), half)
        value = wide[...] * scale[...]
        high = value.astype(BF)
        low = (value - high.astype(F32)).astype(BF)
        grad_half[dx] = mm(put_grad[...], high).astype(BF)
        copies.append(pltpu.make_async_copy(grad_half.at[dx], outs[1].at[:, at], sems.at[2 * dx]))
        copies[-1].start()
        layer_half[dx] = (mm(put_out[...], high) + mm(put_out[...], low)).astype(BF)
        copies.append(
            pltpu.make_async_copy(layer_half.at[dx], outs[0].at[:, at], sems.at[2 * dx + 1])
        )
        copies[-1].start()
    for copy in copies:
        copy.wait()


def grads_body(experts, slots, routes, gates, xs, ys, rows_a, rows_b, rows_h, *refs):
    *outs, put_out, put_grad, scale, held, sems = refs
    copies = []
    for i, (rows, w) in enumerate(((xs, rows_a), (xs, rows_b), (ys, rows_h))):
        held[i] = mm(rows[...], w[...], TN).astype(BF)
        copies.append(pltpu.make_async_copy(held.at[i], outs[i].at[0], sems.at[i]))
        copies[-1].start()
    expert = own_expert(experts)
    each = 2 * slots
    count = each * experts
    block = put_out.shape[0]
    pos = slot_values(lambda e, s: routes[e, s], count, slots, expert, experts, 1)
    gate = slot_values(lambda e, s: gates[e, s], count, slots, expert, experts, 0)
    is_out = lax.rem(lax.broadcasted_iota(jnp.int32, (count, 1), 0), each) < slots
    is_out_lane = lax.rem(lax.broadcasted_iota(jnp.int32, (1, count), 1), each) < slots
    scale[...] = jnp.where(is_out, gate, 1.0)
    hit = lax.broadcasted_iota(jnp.int32, (block, count), 0) == pos
    put_out[...] = jnp.where(hit & is_out_lane, 1.0, 0.0).astype(BF)
    put_grad[...] = jnp.where(hit & ~is_out_lane, 1.0, 0.0).astype(BF)
    for copy in copies:
        copy.wait()


def shards(n_dp, n_exp, tokens, routes, gate_values, wg, wu, wd, cot):
    block, width = tokens.shape
    experts = routes.shape[1]
    slots = routes.shape[2]
    hid = wg.shape[2]
    half = width // n_dp
    each = 2 * slots
    n_msg = n_dp * experts
    sds = jax.ShapeDtypeStruct

    def home_perm(dx, k, sign):
        return [
            (
                d * n_exp + i,
                (d + sign * dx) % n_dp * n_exp + (i // SPLIT + sign * k) % experts * SPLIT + i % SPLIT,
            )
            for d in range(n_dp)
            for i in range(n_exp)
        ]

    def part_perm(q):
        return [(d * n_exp + i, d * n_exp + (i ^ q)) for d in range(n_dp) for i in range(n_exp)]

    def batch_perm(dx):
        return [
            (d * n_exp + i, (d + dx) % n_dp * n_exp + i) for d in range(n_dp) for i in range(n_exp)
        ]

    def send(x, perm):
        return lax.ppermute(x, AXES, perm)

    kinds = [(dx, k) for dx in range(n_dp) for k in range(experts)]
    order = sorted(range(n_msg), key=lambda m: (kinds[m][1] == 0, kinds[m][0] == 0, m))
    small = [sds((each, half), BF)] * n_msg
    msgs = call(
        functools.partial(gather_body, n_dp, experts, slots),
        small,
        [in_hbm(x) for x in (routes[0], gate_values[0], tokens, cot)],
        in_specs=[HBM] * 4,
        scratch=[
            pltpu.VMEM((n_dp, 2 * block, half), BF),
            pltpu.SMEM((experts, slots), jnp.int32),
            pltpu.SMEM((experts, slots), F32),
            pltpu.SemaphoreType.DMA((2 + 2 * n_dp,)),
        ],
    )
    got = dict(zip(kinds, msgs))
    for kind in kinds[1:]:
        got[kind] = send(got[kind], home_perm(*kind, 1))
    down, mark = call(
        load_body,
        [sds(wd.shape, BF)],
        [in_hbm(wd)],
        in_specs=[HBM],
        scratch=[pltpu.SemaphoreType.DMA],
        mark=True,
    )
    rows = each * n_msg
    n_rows = rows // 2 * SPLIT
    (piece,) = call(
        functools.partial(arrange_body, n_dp, experts, slots, order),
        [sds((rows, half), BF)],
        [got[kinds[m]] for m in order],
        scratch=[pltpu.VMEM((rows, half), F32)],
        extra=rows * half * 8,
        after=[mark],
    )
    pieces = [None] * SPLIT
    for q in range(0, SPLIT, 2):
        pieces[q] = piece if q == 0 else send(piece, part_perm(q))
        pieces[q + 1] = send(pieces[q], part_perm(1))
    xs, ys, part, part_sent = call(
        forward_body,
        [
            sds((n_rows, half), BF),
            sds((n_rows, half), BF),
            sds((n_rows, 3 * hid), F32),
            sds((n_rows, 3 * hid), BF),
        ],
        (*pieces, wg, wu, down),
    )
    recv = [send(part_sent, batch_perm(dx)) for dx in range(1, n_dp)]
    rows_h, rows_a, rows_b, own, sib = call(
        functools.partial(backward_body, n_dp - 1),
        [sds((n_rows, hid), BF)] * 3 + [sds((n_rows, half), BF)] * 2,
        (part, *recv, wg, wu, down),
        extra=n_rows * half * 12,
    )
    sums = call(
        pair_sum_body, [sds((rows, half), BF)] * (SPLIT // 2), (own, send(sib, part_perm(1)))
    )
    back = [sums[0]] + [send(sums[j], part_perm(2 * j)) for j in range(1, SPLIT // 2)]
    count = each * experts
    *grads, put_out, put_grad, scale, mark = call(
        functools.partial(grads_body, experts, slots),
        [sds((1, half, hid), BF)] * 3 + [sds((block, count), BF)] * 2 + [sds((count, 1), F32)],
        (routes[0], gate_values[0], xs, ys, rows_a, rows_b, rows_h),
        in_specs=[SMEM] * 2 + [VMEM] * 5,
        out_specs=[HBM] * 3 + [VMEM] * 3,
        scratch=[pltpu.VMEM((3, half, hid), BF), pltpu.SemaphoreType.DMA((3,))],
        extra=n_rows * half * 4 + half * hid * 12,
        mark=True,
        cost=pl.CostEstimate(
            flops=6 * n_rows * half * hid, bytes_accessed=6 * half * hid, transcendentals=0
        ),
    )
    msgs = call(
        functools.partial(return_body, n_dp, experts, slots, len(back), order),
        [sds((each, half), BF)] * n_msg,
        back,
        extra=rows * half * 8,
        after=[mark],
    )
    got = {kinds[m]: msg for m, msg in zip(order, msgs)}
    for kind in kinds[1:]:
        got[kind] = send(got[kind], home_perm(*kind, -1))
    layer_out, token_grad = call(
        functools.partial(home_body, n_dp, experts, order),
        [sds((block, width), BF)] * 2,
        (put_out, put_grad, scale, *[got[kinds[m]] for m in order]),
        out_specs=[HBM] * 2,
        scratch=[pltpu.VMEM((n_dp, block, half), BF)] * 2
        + [pltpu.VMEM((count, half), F32), pltpu.SemaphoreType.DMA((2 * n_dp,))],
        extra=block * half * 16 + count * half * 4,
    )
    return layer_out, token_grad, *grads


def solution(mesh):
    rows = P(AXES, None)
    slots = P(AXES, None, None)
    weights = P("expert", "dp", None)
    return jax.shard_map(
        functools.partial(shards, mesh.shape["dp"], mesh.shape["expert"]),
        mesh=mesh,
        in_specs=(rows, slots, slots, weights, weights, weights, rows),
        out_specs=(rows, rows, weights, weights, weights),
        check_vma=False,
    )
```

time: 58.7 us -> 51.8 us (0.88)
  waiting for transfers between devices: 26.8 us -> 21.7 us
  local copies, waits for them, and re-layouts: 4.36 us -> 0.69 us
  Pallas kernels: 8.26 us -> 10.1 us
    ppermute x18, waiting for transfers between devices: 26.8 us -> 21.7 us  [send(): return lax.ppermute(x, AXES, perm)]
    unnamed x14 -> x8, local copies, waits for them, and re-layouts: 4.36 us -> 0.69 us
    pallas_call x8 -> x9, Pallas kernels: 8.26 us -> 10.1 us  [call(): pl.pallas_call(whole, out_shape=[*out_shape, *[jax.ShapeDtypeStruct((8, 1...]
  transfers between devices with their start and end apart: 18 -> 18, of which waited for: 13 -> 14; matrix products, arithmetic and copies ran while one was open for 0% -> 0% of each run, Pallas kernels for 4% -> 8%
where the time goes in v2:
time: 51.8 us; the launch traced here: 51.6 us
  waiting for transfers between devices  21.7 us (42%)
  starting transfers between devices  18.3 us (35%)
  Pallas kernels  10.1 us (19%)
  between operations  0.74 us (1%)
  local copies, waits for them, and re-layouts  0.69 us (1%)
    ppermute x18, waiting for transfers between devices, send(): return lax.ppermute(x, AXES, perm)  21.7 us
    ppermute x18, starting transfers between devices, send(): return lax.ppermute(x, AXES, perm)  18.3 us
    pallas_call x9, Pallas kernels, call(): pl.pallas_call(whole, out_shape=[*out_shape, *[jax.ShapeDtypeStruct((8, 1...  10.1 us
  transfers between devices with their start and end apart: 18, of which 14 were waited for; matrix products, arithmetic and copies ran while one was open for 0% of the time, Pallas kernels for 8%

profile of v2, /device:TPU:0, one launch (start us, length us, event | category | flops | bytes accessed | tf_op | source)
XLA Modules:
  0.0 51.6 jit_solution(12622962037733180878)
XLA Ops:
  0.6 1.9 %shard_map.110 = (bf16[8,2048]{1,0:T(8,128)(2,1)S(1)}, bf16[8,2048]{1,0:T(8,128)(2,1)S(1)}, bf16[8,2048]{1,0:T(8,128)(2,1)S(1)}, bf16[8,2048]{1,0:T(8,128)(2,1)S(1)}) custom-call(s32[2,4]{1,0:T(2,128)} %bitcast.2, f32[2,4]{1,0:T(2,128)} %bitcast.4, bf16[128,4096]{1,0:T(8,128)(2,1)} %refs_2_.2, bf16[128,4096]{1,0:T(8,128)(2,1)} %refs_3_.2), custom_call_target="tpu_custom_call" | custom-call | tf_op jit(solution)/shard_map/pallas_call | solution.py:62
  2.6 0.0 copy-start
  2.6 5.0 %collective-permute-start = (bf16[8,2048]{1,0:T(8,128)(2,1)S(1)}, bf16[8,2048]{1,0:T(8,128)(2,1)S(1)}, u32[]{:S(2)}, u32[]{:S(2)}) collective-permute-start(bf16[8,2048]{1,0:T(8,128)(2,1)S(1)} %get-tuple-element.37), channel_id=1, source_target_pairs={{0,24},{1,25},{2,26},{3,27},{4,28},{5,29},{6,30},{7,31},{8,16},{9,... | collective-permute-start | bytes 98312 | tf_op jit(solution)/shard_map/ppermute | solution.py:295
  7.6 0.3 collective-permute-start.1
  8.0 0.3 collective-permute-start.2
  8.3 1.2 %shard_map.111 = (bf16[1,2048,256]{2,1,0:T(8,128)(2,1)S(1)}, f32[8,128]{1,0:T(8,128)S(1)}) custom-call(bf16[1,2048,256]{2,1,0:T(8,128)(2,1)} %refs_0_.1), custom_call_target="tpu_custom_call" | custom-call | tf_op jit(solution)/shard_map/pallas_call | solution.py:62
  9.5 0.4 collective-permute-done.refs_0_
  9.9 2.6 %collective-permute-done.1.refs_1_ = bf16[8,2048]{1,0:T(8,128)(2,1)S(1)} collective-permute-done((bf16[8,2048]{1,0:T(8,128)(2,1)S(1)}, bf16[8,2048]{1,0:T(8,128)(2,1)S(1)}, u32[]{:S(2)}, u32[]{:S(2)}) %collective-permute-start.1) | collective-permute-done | bytes 32800 | tf_op jit(solution)/shard_map/ppermute | solution.py:295
  12.4 0.0 collective-permute-done.2.refs_2_
  12.4 0.2 shard_map.112.refs_0_
  12.6 2.6 %collective-permute-start.8 = (bf16[32,2048]{1,0:T(8,128)(2,1)S(1)}, bf16[32,2048]{1,0:T(8,128)(2,1)S(1)}, u32[]{:S(2)}, u32[]{:S(2)}) collective-permute-start(bf16[32,2048]{1,0:T(8,128)(2,1)S(1)} %shard_map.112.refs_0_), channel_id=1, source_target_pairs={{0,6},{1,7},{2,4},{3,5},{4,2},{5,3},{6,0},{7,1},{8,14},{9,15},{10,... | collective-permute-start | bytes 393224 | tf_op jit(solution)/shard_map/ppermute | solution.py:295
  15.2 0.4 collective-permute-start.6
  15.7 0.5 collective-permute-start.4
  16.2 0.0 collective-permute-start.3
  16.2 2.9 %collective-permute-done.8.refs_6_ = bf16[32,2048]{1,0:T(8,128)(2,1)S(1)} collective-permute-done((bf16[32,2048]{1,0:T(8,128)(2,1)S(1)}, bf16[32,2048]{1,0:T(8,128)(2,1)S(1)}, u32[]{:S(2)}, u32[]{:S(2)}) %collective-permute-start.8) | collective-permute-done | bytes 131104 | tf_op jit(solution)/shard_map/ppermute | solution.py:295
  19.1 0.0 collective-permute-start.9
  19.1 1.3 %collective-permute-done.6.refs_4_ = bf16[32,2048]{1,0:T(8,128)(2,1)S(1)} collective-permute-done((bf16[32,2048]{1,0:T(8,128)(2,1)S(1)}, bf16[32,2048]{1,0:T(8,128)(2,1)S(1)}, u32[]{:S(2)}, u32[]{:S(2)}) %collective-permute-start.6) | collective-permute-done | bytes 131104 | tf_op jit(solution)/shard_map/ppermute | solution.py:295
  20.4 0.0 collective-permute-start.7
  20.4 0.2 collective-permute-done.4.refs_2_
  20.6 0.3 collective-permute-start.5
  21.0 0.0 collective-permute-done.3.refs_1_
  21.0 0.0 collective-permute-done.9.refs_7_
  21.0 0.8 %collective-permute-done.7.refs_5_ = bf16[32,2048]{1,0:T(8,128)(2,1)S(1)} collective-permute-done((bf16[32,2048]{1,0:T(8,128)(2,1)S(1)}, bf16[32,2048]{1,0:T(8,128)(2,1)S(1)}, u32[]{:S(2)}, u32[]{:S(2)}) %collective-permute-start.7) | collective-permute-done | bytes 131104 | tf_op jit(solution)/shard_map/ppermute | solution.py:295
  21.8 0.2 collective-permute-done.5.refs_3_
  22.0 0.0 copy-done
  22.0 0.6 %shard_map.113 = (bf16[128,2048]{1,0:T(8,128)(2,1)S(1)}, bf16[128,2048]{1,0:T(8,128)(2,1)S(1)}, f32[128,768]{1,0:T(8,128)S(1)}, bf16[128,768]{1,0:T(8,128)(2,1)S(1)}) custom-call(bf16[32,2048]{1,0:T(8,128)(2,1)S(1)} %shard_map.112.refs_0_, bf16[32,2048]{1,0:T(8,128)(2,1)S(1)} %collective-permute-done.3.refs_1_, ...), custom_call_target="tpu_custom_call" | custom-call | tf_op jit(solution)/shard_map/pallas_call | solution.py:62
  22.6 0.7 %collective-permute-start.10 = (bf16[128,768]{1,0:T(8,128)(2,1)S(1)}, bf16[128,768]{1,0:T(8,128)(2,1)S(1)}, u32[]{:S(2)}, u32[]{:S(2)}) collective-permute-start(bf16[128,768]{1,0:T(8,128)(2,1)S(1)} %get-tuple-element.46), channel_id=1, source_target_pairs={{0,16},{1,17},{2,18},{3,19},{4,20},{5,21},{6,22},{7,23},{8,24},{9,... | collective-permute-start | bytes 589832 | tf_op jit(solution)/shard_map/ppermute | solution.py:295
  23.3 6.5 %collective-permute-done.10.refs_1_ = bf16[128,768]{1,0:T(8,128)(2,1)S(1)} collective-permute-done((bf16[128,768]{1,0:T(8,128)(2,1)S(1)}, bf16[128,768]{1,0:T(8,128)(2,1)S(1)}, u32[]{:S(2)}, u32[]{:S(2)}) %collective-permute-start.10) | collective-permute-done | bytes 196640 | tf_op jit(solution)/shard_map/ppermute | solution.py:295
  29.8 1.1 %shard_map.114 = (bf16[128,256]{1,0:T(8,128)(2,1)S(1)}, bf16[128,256]{1,0:T(8,128)(2,1)S(1)}, bf16[128,256]{1,0:T(8,128)(2,1)S(1)}, bf16[128,2048]{1,0:T(8,128)(2,1)S(1)}, bf16[128,2048]{1,0:T(8,128)(2,1)S(1)}) custom-call(f32[128,768]{1,0:T(8,128)S(1)} %get-tuple-element.45.refs_0_, bf16[128,768]{1,0:T(8,128)(2,1)S(1)} %collective-permute-done.10.refs_1_, ...), custom_call_target="tpu_custom_call" | custom-call | tf_op jit(solution)/shard_map/pallas_call | solution.py:62
  30.9 0.1 collective-permute-start.11
  31.0 1.9 %collective-permute-done.11.refs_1_ = bf16[128,2048]{1,0:T(8,128)(2,1)S(1)} collective-permute-done((bf16[128,2048]{1,0:T(8,128)(2,1)S(1)}, bf16[128,2048]{1,0:T(8,128)(2,1)S(1)}, u32[]{:S(2)}, u32[]{:S(2)}) %collective-permute-start.11) | collective-permute-done | bytes 524320 | tf_op jit(solution)/shard_map/ppermute | solution.py:295
  32.9 0.1 shard_map.116
  33.0 1.2 %collective-permute-start.12 = (bf16[32,2048]{1,0:T(8,128)(2,1)S(1)}, bf16[32,2048]{1,0:T(8,128)(2,1)S(1)}, u32[]{:S(2)}, u32[]{:S(2)}) collective-permute-start(bf16[32,2048]{1,0:T(8,128)(2,1)S(1)} %get-tuple-element.56), channel_id=1, source_target_pairs={{0,2},{1,3},{2,0},{3,1},{4,6},{5,7},{6,4},{7,5},{8,10},{9,11},{10,... | collective-permute-start | bytes 393224 | tf_op jit(solution)/shard_map/ppermute | solution.py:295
  34.2 1.4 %collective-permute-start.13 = (bf16[32,2048]{1,0:T(8,128)(2,1)S(1)}, bf16[32,2048]{1,0:T(8,128)(2,1)S(1)}, u32[]{:S(2)}, u32[]{:S(2)}) collective-permute-start(bf16[32,2048]{1,0:T(8,128)(2,1)S(1)} %get-tuple-element.57), channel_id=1, source_target_pairs={{0,4},{1,5},{2,6},{3,7},{4,0},{5,1},{6,2},{7,3},{8,12},{9,13},{10,... | collective-permute-start | bytes 393224 | tf_op jit(solution)/shard_map/ppermute | solution.py:295
  35.6 1.0 %collective-permute-start.14 = (bf16[32,2048]{1,0:T(8,128)(2,1)S(1)}, bf16[32,2048]{1,0:T(8,128)(2,1)S(1)}, u32[]{:S(2)}, u32[]{:S(2)}) collective-permute-start(bf16[32,2048]{1,0:T(8,128)(2,1)S(1)} %get-tuple-element.58), channel_id=1, source_target_pairs={{0,6},{1,7},{2,4},{3,5},{4,2},{5,3},{6,0},{7,1},{8,14},{9,15},{10,... | collective-permute-start | bytes 393224 | tf_op jit(solution)/shard_map/ppermute | solution.py:295
  36.6 0.7 %copy-done.2 = s32[1,2,4]{2,1,0:T(2,128)S(1)} copy-done((s32[1,2,4]{2,1,0:T(2,128)S(1)}, s32[1,2,4]{2,1,0:T(2,128)}, u32[]{:S(2)}) %copy-start.2) | copy-done | bytes 56
  37.3 2.9 %shard_map.115 = (bf16[1,2048,256]{2,1,0:T(8,128)(2,1)}, bf16[1,2048,256]{2,1,0:T(8,128)(2,1)}, bf16[1,2048,256]{2,1,0:T(8,128)(2,1)}, bf16[128,16]{1,0:T(8,128)...) custom-call(s32[2,4]{1,0:T(2,128)S(1)} %bitcast.3, f32[2,4]{1,0:T(2,128)S(1)} %bitcast.5, ...), custom_call_target="tpu_custom_call" | custom-call | flops 402653184 | bytes 3145728 | tf_op jit(solution)/shard_map/pallas_call | solution.py:62
  40.2 0.0 collective-permute-done.12.refs_1_
  40.2 0.4 collective-permute-done.13.refs_2_
  40.6 2.0 %collective-permute-done.14.refs_3_ = bf16[32,2048]{1,0:T(8,128)(2,1)S(1)} collective-permute-done((bf16[32,2048]{1,0:T(8,128)(2,1)S(1)}, bf16[32,2048]{1,0:T(8,128)(2,1)S(1)}, u32[]{:S(2)}, u32[]{:S(2)}) %collective-permute-start.14) | collective-permute-done | bytes 131104 | tf_op jit(solution)/shard_map/ppermute | solution.py:295
  42.6 0.2 shard_map.117
  42.8 2.0 %collective-permute-start.15 = (bf16[8,2048]{1,0:T(8,128)(2,1)S(1)}, bf16[8,2048]{1,0:T(8,128)(2,1)S(1)}, u32[]{:S(2)}, u32[]{:S(2)}) collective-permute-start(bf16[8,2048]{1,0:T(8,128)(2,1)S(1)} %get-tuple-element.60), channel_id=1, source_target_pairs={{0,24},{1,25},{2,26},{3,27},{4,28},{5,29},{6,30},{7,31},{8,16},{9,... | collective-permute-start | bytes 98312 | tf_op jit(solution)/shard_map/ppermute | solution.py:295
  44.8 1.1 %collective-permute-start.16 = (bf16[8,2048]{1,0:T(8,128)(2,1)S(1)}, bf16[8,2048]{1,0:T(8,128)(2,1)S(1)}, u32[]{:S(2)}, u32[]{:S(2)}) collective-permute-start(bf16[8,2048]{1,0:T(8,128)(2,1)S(1)} %get-tuple-element.61), channel_id=1, source_target_pairs={{0,8},{1,9},{2,10},{3,11},{4,12},{5,13},{6,14},{7,15},{8,0},{9,1},... | collective-permute-start | bytes 98312 | tf_op jit(solution)/shard_map/ppermute | solution.py:295
  45.9 1.4 %collective-permute-start.17 = (bf16[8,2048]{1,0:T(8,128)(2,1)S(1)}, bf16[8,2048]{1,0:T(8,128)(2,1)S(1)}, u32[]{:S(2)}, u32[]{:S(2)}) collective-permute-start(bf16[8,2048]{1,0:T(8,128)(2,1)S(1)} %get-tuple-element.62), channel_id=1, source_target_pairs={{0,16},{1,17},{2,18},{3,19},{4,20},{5,21},{6,22},{7,23},{8,24},{9,... | collective-permute-start | bytes 98312 | tf_op jit(solution)/shard_map/ppermute | solution.py:295
  47.3 1.5 %collective-permute-done.15.refs_3_ = bf16[8,2048]{1,0:T(8,128)(2,1)S(1)} collective-permute-done((bf16[8,2048]{1,0:T(8,128)(2,1)S(1)}, bf16[8,2048]{1,0:T(8,128)(2,1)S(1)}, u32[]{:S(2)}, u32[]{:S(2)}) %collective-permute-start.15) | collective-permute-done | bytes 32800 | tf_op jit(solution)/shard_map/ppermute | solution.py:295
  48.8 0.8 %collective-permute-done.16.refs_4_ = bf16[8,2048]{1,0:T(8,128)(2,1)S(1)} collective-permute-done((bf16[8,2048]{1,0:T(8,128)(2,1)S(1)}, bf16[8,2048]{1,0:T(8,128)(2,1)S(1)}, u32[]{:S(2)}, u32[]{:S(2)}) %collective-permute-start.16) | collective-permute-done | bytes 32800 | tf_op jit(solution)/shard_map/ppermute | solution.py:295
  49.6 0.2 collective-permute-done.17.refs_5_
  49.8 1.8 %shard_map.118 = (bf16[128,4096]{1,0:T(8,128)(2,1)}, bf16[128,4096]{1,0:T(8,128)(2,1)}) custom-call(bf16[128,16]{1,0:T(8,128)(2,1)S(1)} %get-tuple-element.50.refs_0_, bf16[128,16]{1,0:T(8,128)(2,1)S(1)} %get-tuple-element.51.refs_1_, f32[16,1]{1,0:T(8,128)S(1)} %get-tuple-element.52.refs_2_, bf16[8,2048]{1,0:T(8,128)(2,1)S(1)} %collective-permute-done.15.refs_3_, ...), custom_call_target="tpu_custom_call" | custom-call | tf_op jit(solution)/shard_map/pallas_call | solution.py:62
  (5 shorter events, 0.0 us)
Async XLA Ops:
  0.6 21.4 %copy-start.1 = (bf16[1,2048,256]{2,1,0:T(8,128)(2,1)S(1)}, bf16[1,2048,256]{2,1,0:T(8,128)(2,1)}, u32[]{:S(2)}) copy-start(bf16[1,2048,256]{2,1,0:T(8,128)(2,1)} %refs_3_.3) | copy-start | bytes 3145732
  2.6 19.4 %copy-start = (bf16[1,2048,256]{2,1,0:T(8,128)(2,1)S(1)}, bf16[1,2048,256]{2,1,0:T(8,128)(2,1)}, u32[]{:S(2)}) copy-start(bf16[1,2048,256]{2,1,0:T(8,128)(2,1)} %refs_2_.3) | copy-start | bytes 3145732
  2.6 7.3 %collective-permute-start = (bf16[8,2048]{1,0:T(8,128)(2,1)S(1)}, bf16[8,2048]{1,0:T(8,128)(2,1)S(1)}, u32[]{:S(2)}, u32[]{:S(2)}) collective-permute-start(bf16[8,2048]{1,0:T(8,128)(2,1)S(1)} %get-tuple-element.37), channel_id=1, source_target_pairs={{0,24},{1,25},{2,26},{3,27},{4,28},{5,29},{6,30},{7,31},{8,16},{9,... | collective-permute-start | bytes 98312 | tf_op jit(solution)/shard_map/ppermute | solution.py:295
  7.6 4.8 %collective-permute-start.1 = (bf16[8,2048]{1,0:T(8,128)(2,1)S(1)}, bf16[8,2048]{1,0:T(8,128)(2,1)S(1)}, u32[]{:S(2)}, u32[]{:S(2)}) collective-permute-start(bf16[8,2048]{1,0:T(8,128)(2,1)S(1)} %get-tuple-element.38), channel_id=1, source_target_pairs={{0,8},{1,9},{2,10},{3,11},{4,12},{5,13},{6,14},{7,15},{8,0},{9,1},... | collective-permute-start | bytes 98312 | tf_op jit(solution)/shard_map/ppermute | solution.py:295
  8.0 4.5 %collective-permute-start.2 = (bf16[8,2048]{1,0:T(8,128)(2,1)S(1)}, bf16[8,2048]{1,0:T(8,128)(2,1)S(1)}, u32[]{:S(2)}, u32[]{:S(2)}) collective-permute-start(bf16[8,2048]{1,0:T(8,128)(2,1)S(1)} %get-tuple-element.39), channel_id=1, source_target_pairs={{0,16},{1,17},{2,18},{3,19},{4,20},{5,21},{6,22},{7,23},{8,24},{9,... | collective-permute-start | bytes 98312 | tf_op jit(solution)/shard_map/ppermute | solution.py:295
  12.6 6.5 %collective-permute-start.8 = (bf16[32,2048]{1,0:T(8,128)(2,1)S(1)}, bf16[32,2048]{1,0:T(8,128)(2,1)S(1)}, u32[]{:S(2)}, u32[]{:S(2)}) collective-permute-start(bf16[32,2048]{1,0:T(8,128)(2,1)S(1)} %shard_map.112.refs_0_), channel_id=1, source_target_pairs={{0,6},{1,7},{2,4},{3,5},{4,2},{5,3},{6,0},{7,1},{8,14},{9,15},{10,... | collective-permute-start | bytes 393224 | tf_op jit(solution)/shard_map/ppermute | solution.py:295
  15.2 5.2 %collective-permute-start.6 = (bf16[32,2048]{1,0:T(8,128)(2,1)S(1)}, bf16[32,2048]{1,0:T(8,128)(2,1)S(1)}, u32[]{:S(2)}, u32[]{:S(2)}) collective-permute-start(bf16[32,2048]{1,0:T(8,128)(2,1)S(1)} %shard_map.112.refs_0_), channel_id=1, source_target_pairs={{0,4},{1,5},{2,6},{3,7},{4,0},{5,1},{6,2},{7,3},{8,12},{9,13},{10,... | collective-permute-start | bytes 393224 | tf_op jit(solution)/shard_map/ppermute | solution.py:295
  15.7 5.0 %collective-permute-start.4 = (bf16[32,2048]{1,0:T(8,128)(2,1)S(1)}, bf16[32,2048]{1,0:T(8,128)(2,1)S(1)}, u32[]{:S(2)}, u32[]{:S(2)}) collective-permute-start(bf16[32,2048]{1,0:T(8,128)(2,1)S(1)} %shard_map.112.refs_0_), channel_id=1, source_target_pairs={{0,2},{1,3},{2,0},{3,1},{4,6},{5,7},{6,4},{7,5},{8,10},{9,11},{10,... | collective-permute-start | bytes 393224 | tf_op jit(solution)/shard_map/ppermute | solution.py:295
  16.2 4.8 %collective-permute-start.3 = (bf16[32,2048]{1,0:T(8,128)(2,1)S(1)}, bf16[32,2048]{1,0:T(8,128)(2,1)S(1)}, u32[]{:S(2)}, u32[]{:S(2)}) collective-permute-start(bf16[32,2048]{1,0:T(8,128)(2,1)S(1)} %shard_map.112.refs_0_), channel_id=1, source_target_pairs={{0,1},{1,0},{2,3},{3,2},{4,5},{5,4},{6,7},{7,6},{8,9},{9,8},{10,11... | collective-permute-start | bytes 393224 | tf_op jit(solution)/shard_map/ppermute | solution.py:295
  19.1 1.9 %collective-permute-start.9 = (bf16[32,2048]{1,0:T(8,128)(2,1)S(1)}, bf16[32,2048]{1,0:T(8,128)(2,1)S(1)}, u32[]{:S(2)}, u32[]{:S(2)}) collective-permute-start(bf16[32,2048]{1,0:T(8,128)(2,1)S(1)} %collective-permute-done.8.refs_6_), channel_id=1, source_target_pairs={{0,1},{1,0},{2,3},{3,2},{4,5},{5,4},{6,7},{7,6},{8,9},{9,8},{10,11... | collective-permute-start | bytes 393224 | tf_op jit(solution)/shard_map/ppermute | solution.py:295
  20.4 1.3 %collective-permute-start.7 = (bf16[32,2048]{1,0:T(8,128)(2,1)S(1)}, bf16[32,2048]{1,0:T(8,128)(2,1)S(1)}, u32[]{:S(2)}, u32[]{:S(2)}) collective-permute-start(bf16[32,2048]{1,0:T(8,128)(2,1)S(1)} %collective-permute-done.6.refs_4_), channel_id=1, source_target_pairs={{0,1},{1,0},{2,3},{3,2},{4,5},{5,4},{6,7},{7,6},{8,9},{9,8},{10,11... | collective-permute-start | bytes 393224 | tf_op jit(solution)/shard_map/ppermute | solution.py:295
  20.6 1.3 %collective-permute-start.5 = (bf16[32,2048]{1,0:T(8,128)(2,1)S(1)}, bf16[32,2048]{1,0:T(8,128)(2,1)S(1)}, u32[]{:S(2)}, u32[]{:S(2)}) collective-permute-start(bf16[32,2048]{1,0:T(8,128)(2,1)S(1)} %collective-permute-done.4.refs_2_), channel_id=1, source_target_pairs={{0,1},{1,0},{2,3},{3,2},{4,5},{5,4},{6,7},{7,6},{8,9},{9,8},{10,11... | collective-permute-start | bytes 393224 | tf_op jit(solution)/shard_map/ppermute | solution.py:295
  22.6 7.2 %collective-permute-start.10 = (bf16[128,768]{1,0:T(8,128)(2,1)S(1)}, bf16[128,768]{1,0:T(8,128)(2,1)S(1)}, u32[]{:S(2)}, u32[]{:S(2)}) collective-permute-start(bf16[128,768]{1,0:T(8,128)(2,1)S(1)} %get-tuple-element.46), channel_id=1, source_target_pairs={{0,16},{1,17},{2,18},{3,19},{4,20},{5,21},{6,22},{7,23},{8,24},{9,... | collective-permute-start | bytes 589832 | tf_op jit(solution)/shard_map/ppermute | solution.py:295
  30.9 2.0 %collective-permute-start.11 = (bf16[128,2048]{1,0:T(8,128)(2,1)S(1)}, bf16[128,2048]{1,0:T(8,128)(2,1)S(1)}, u32[]{:S(2)}, u32[]{:S(2)}) collective-permute-start(bf16[128,2048]{1,0:T(8,128)(2,1)S(1)} %get-tuple-element.54), channel_id=1, source_target_pairs={{0,1},{1,0},{2,3},{3,2},{4,5},{5,4},{6,7},{7,6},{8,9},{9,8},{10,11... | collective-permute-start | bytes 1572872 | tf_op jit(solution)/shard_map/ppermute | solution.py:295
  32.9 3.7 %copy-start.3 = (f32[1,2,4]{2,1,0:T(2,128)S(1)}, f32[1,2,4]{2,1,0:T(2,128)}, u32[]{:S(2)}) copy-start(f32[1,2,4]{2,1,0:T(2,128)} %param.9) | copy-start | bytes 100
  33.0 7.2 %collective-permute-start.12 = (bf16[32,2048]{1,0:T(8,128)(2,1)S(1)}, bf16[32,2048]{1,0:T(8,128)(2,1)S(1)}, u32[]{:S(2)}, u32[]{:S(2)}) collective-permute-start(bf16[32,2048]{1,0:T(8,128)(2,1)S(1)} %get-tuple-element.56), channel_id=1, source_target_pairs={{0,2},{1,3},{2,0},{3,1},{4,6},{5,7},{6,4},{7,5},{8,10},{9,11},{10,... | collective-permute-start | bytes 393224 | tf_op jit(solution)/shard_map/ppermute | solution.py:295
  34.2 6.4 %collective-permute-start.13 = (bf16[32,2048]{1,0:T(8,128)(2,1)S(1)}, bf16[32,2048]{1,0:T(8,128)(2,1)S(1)}, u32[]{:S(2)}, u32[]{:S(2)}) collective-permute-start(bf16[32,2048]{1,0:T(8,128)(2,1)S(1)} %get-tuple-element.57), channel_id=1, source_target_pairs={{0,4},{1,5},{2,6},{3,7},{4,0},{5,1},{6,2},{7,3},{8,12},{9,13},{10,... | collective-permute-start | bytes 393224 | tf_op jit(solution)/shard_map/ppermute | solution.py:295
  35.6 7.0 %collective-permute-start.14 = (bf16[32,2048]{1,0:T(8,128)(2,1)S(1)}, bf16[32,2048]{1,0:T(8,128)(2,1)S(1)}, u32[]{:S(2)}, u32[]{:S(2)}) collective-permute-start(bf16[32,2048]{1,0:T(8,128)(2,1)S(1)} %get-tuple-element.58), channel_id=1, source_target_pairs={{0,6},{1,7},{2,4},{3,5},{4,2},{5,3},{6,0},{7,1},{8,14},{9,15},{10,... | collective-permute-start | bytes 393224 | tf_op jit(solution)/shard_map/ppermute | solution.py:295
  36.6 0.7 %copy-start.2 = (s32[1,2,4]{2,1,0:T(2,128)S(1)}, s32[1,2,4]{2,1,0:T(2,128)}, u32[]{:S(2)}) copy-start(s32[1,2,4]{2,1,0:T(2,128)} %param.8) | copy-start | bytes 100
  42.8 6.0 %collective-permute-start.15 = (bf16[8,2048]{1,0:T(8,128)(2,1)S(1)}, bf16[8,2048]{1,0:T(8,128)(2,1)S(1)}, u32[]{:S(2)}, u32[]{:S(2)}) collective-permute-start(bf16[8,2048]{1,0:T(8,128)(2,1)S(1)} %get-tuple-element.60), channel_id=1, source_target_pairs={{0,24},{1,25},{2,26},{3,27},{4,28},{5,29},{6,30},{7,31},{8,16},{9,... | collective-permute-start | bytes 98312 | tf_op jit(solution)/shard_map/ppermute | solution.py:295
  44.8 4.8 %collective-permute-start.16 = (bf16[8,2048]{1,0:T(8,128)(2,1)S(1)}, bf16[8,2048]{1,0:T(8,128)(2,1)S(1)}, u32[]{:S(2)}, u32[]{:S(2)}) collective-permute-start(bf16[8,2048]{1,0:T(8,128)(2,1)S(1)} %get-tuple-element.61), channel_id=1, source_target_pairs={{0,8},{1,9},{2,10},{3,11},{4,12},{5,13},{6,14},{7,15},{8,0},{9,1},... | collective-permute-start | bytes 98312 | tf_op jit(solution)/shard_map/ppermute | solution.py:295
  45.9 3.9 %collective-permute-start.17 = (bf16[8,2048]{1,0:T(8,128)(2,1)S(1)}, bf16[8,2048]{1,0:T(8,128)(2,1)S(1)}, u32[]{:S(2)}, u32[]{:S(2)}) collective-permute-start(bf16[8,2048]{1,0:T(8,128)(2,1)S(1)} %get-tuple-element.62), channel_id=1, source_target_pairs={{0,16},{1,17},{2,18},{3,19},{4,20},{5,21},{6,22},{7,23},{8,24},{9,... | collective-permute-start | bytes 98312 | tf_op jit(solution)/shard_map/ppermute | solution.py:295

commit v3 on v2

--- a/solution.py
+++ b/solution.py
@@ -16,7 +16,6 @@
 TN = (((0,), (0,)), ((), ()))
 ANY = pl.BlockSpec(memory_space=pl.ANY)
 HBM = pl.BlockSpec(memory_space=pltpu.HBM)
-SMEM = pl.BlockSpec(memory_space=pltpu.SMEM)
 VMEM = pl.BlockSpec(memory_space=pltpu.VMEM)
 
 
@@ -150,26 +149,41 @@
     out[...] = mm(pick, wide[...].astype(BF)).astype(BF)
 
 
-def load_body(src, dst, sem):
-    copy = pltpu.make_async_copy(src, dst, sem)
-    copy.start()
-    copy.wait()
+def load_body(experts, slots, src, routes_in, gates_in, dst, put_out, put_grad, scale, routes, gates, sems):
+    moves = ((src, dst), (routes_in, routes), (gates_in, gates))
+    copies = [pltpu.make_async_copy(*move, sems.at[i]) for i, move in enumerate(moves)]
+    for copy in copies:
+        copy.start()
+    for copy in copies[1:]:
+        copy.wait()
+    expert = own_expert(experts)
+    each = 2 * slots
+    count = each * experts
+    block = put_out.shape[0]
+    pos = slot_values(lambda e, s: routes[e, s], count, slots, expert, experts, 1)
+    gate = slot_values(lambda e, s: gates[e, s], count, slots, expert, experts, 0)
+    is_out = lax.rem(lax.broadcasted_iota(jnp.int32, (count, 1), 0), each) < slots
+    is_out_lane = lax.rem(lax.broadcasted_iota(jnp.int32, (1, count), 1), each) < slots
+    scale[...] = jnp.where(is_out, gate, 1.0)
+    hit = lax.broadcasted_iota(jnp.int32, (block, count), 0) == pos
+    put_out[...] = jnp.where(hit & is_out_lane, 1.0, 0.0).astype(BF)
+    put_grad[...] = jnp.where(hit & ~is_out_lane, 1.0, 0.0).astype(BF)
+    copies[0].wait()
 
 
 def forward_body(*refs):
-    *pieces, wg, wu, wd, xs, ys, part, part_sent = refs
+    *pieces, wg, wu, wd, part, part_sent = refs
     n = pieces[0].shape[0] // 2
     hid = wg.shape[2]
-    for q, piece in enumerate(pieces):
-        xs[q * n : (q + 1) * n, :] = piece[:n, :]
-        ys[q * n : (q + 1) * n, :] = piece[n:, :]
+    xs = jnp.concatenate([piece[:n, :] for piece in pieces], axis=0)
+    ys = jnp.concatenate([piece[n:, :] for piece in pieces], axis=0)
     for i, (rows, w) in enumerate(((xs, wg), (xs, wu), (ys, wd))):
-        got = mm(rows[...], w[0])
+        got = mm(rows, w[0])
         part[:, i * hid : (i + 1) * hid] = got
         part_sent[:, i * hid : (i + 1) * hid] = got.astype(BF)
 
 
-def backward_body(n_recv, *refs):
+def backward_body(n_pieces, n_recv, *refs):
     part, *rest = refs
     recv, rest = rest[:n_recv], rest[n_recv:]
     wg, wu, wd, rows_h, rows_a, rows_b, own, sib = rest
@@ -187,12 +201,11 @@
     rows_b[...] = b
     p = mm(h, wd[0], NT).astype(BF)
     e = (mm(a, wg[0], NT) + mm(b, wu[0], NT)).astype(BF)
-    n = part.shape[0] // SPLIT
-    for piece in range(SPLIT):
-        out = own if piece % 2 == 0 else sib
-        at = (piece // 2) * 2 * n
-        out[at : at + n, :] = p[piece * n : (piece + 1) * n]
-        out[at + n : at + 2 * n, :] = e[piece * n : (piece + 1) * n]
+    n = part.shape[0] // n_pieces
+    for i in range(n_pieces):
+        out, at = (own, i) if 2 * i < n_pieces else (sib, i - n_pieces // 2)
+        out[2 * at * n : (2 * at + 1) * n, :] = p[i * n : (i + 1) * n]
+        out[(2 * at + 1) * n : (2 * at + 2) * n, :] = e[i * n : (i + 1) * n]
 
 
 def pair_sum_body(own, got, *outs):
@@ -240,25 +253,24 @@
         copy.wait()
 
 
-def grads_body(experts, slots, routes, gates, xs, ys, rows_a, rows_b, rows_h, *refs):
-    *outs, put_out, put_grad, scale, held, sems = refs
+def grads_body(*refs):
+    pieces, lefts, (*outs, xs, ys, w, held, sems) = (
+        refs[:SPLIT],
+        refs[SPLIT : SPLIT + 6],
+        refs[SPLIT + 6 :],
+    )
+    n = pieces[0].shape[0] // 2
+    for i, piece in enumerate(pieces):
+        xs[i * n : (i + 1) * n, :] = piece[:n, :]
+        ys[i * n : (i + 1) * n, :] = piece[n:, :]
     copies = []
-    for i, (rows, w) in enumerate(((xs, rows_a), (xs, rows_b), (ys, rows_h))):
+    for i, rows in enumerate((xs, xs, ys)):
+        for j in range(2):
+            left = lefts[3 * j + i]
+            w[j * left.shape[0] : (j + 1) * left.shape[0], :] = left[...]
         held[i] = mm(rows[...], w[...], TN).astype(BF)
         copies.append(pltpu.make_async_copy(held.at[i], outs[i].at[0], sems.at[i]))
         copies[-1].start()
-    expert = own_expert(experts)
-    each = 2 * slots
-    count = each * experts
-    block = put_out.shape[0]
-    pos = slot_values(lambda e, s: routes[e, s], count, slots, expert, experts, 1)
-    gate = slot_values(lambda e, s: gates[e, s], count, slots, expert, experts, 0)
-    is_out = lax.rem(lax.broadcasted_iota(jnp.int32, (count, 1), 0), each) < slots
-    is_out_lane = lax.rem(lax.broadcasted_iota(jnp.int32, (1, count), 1), each) < slots
-    scale[...] = jnp.where(is_out, gate, 1.0)
-    hit = lax.broadcasted_iota(jnp.int32, (block, count), 0) == pos
-    put_out[...] = jnp.where(hit & is_out_lane, 1.0, 0.0).astype(BF)
-    put_grad[...] = jnp.where(hit & ~is_out_lane, 1.0, 0.0).astype(BF)
     for copy in copies:
         copy.wait()
 
@@ -312,12 +324,14 @@
     got = dict(zip(kinds, msgs))
     for kind in kinds[1:]:
         got[kind] = send(got[kind], home_perm(*kind, 1))
-    down, mark = call(
-        load_body,
-        [sds(wd.shape, BF)],
-        [in_hbm(wd)],
-        in_specs=[HBM],
-        scratch=[pltpu.SemaphoreType.DMA],
+    count = each * experts
+    small = [pltpu.SMEM((experts, slots), jnp.int32), pltpu.SMEM((experts, slots), F32)]
+    down, put_out, put_grad, scale, mark = call(
+        functools.partial(load_body, experts, slots),
+        [sds(wd.shape, BF)] + [sds((block, count), BF)] * 2 + [sds((count, 1), F32)],
+        [in_hbm(x) for x in (wd, routes[0], gate_values[0])],
+        in_specs=[HBM] * 3,
+        scratch=[*small, pltpu.SemaphoreType.DMA((3,))],
         mark=True,
     )
     rows = each * n_msg
@@ -330,40 +344,53 @@
         extra=rows * half * 8,
         after=[mark],
     )
-    pieces = [None] * SPLIT
-    for q in range(0, SPLIT, 2):
-        pieces[q] = piece if q == 0 else send(piece, part_perm(q))
-        pieces[q + 1] = send(pieces[q], part_perm(1))
-    xs, ys, part, part_sent = call(
-        forward_body,
-        [
-            sds((n_rows, half), BF),
-            sds((n_rows, half), BF),
-            sds((n_rows, 3 * hid), F32),
-            sds((n_rows, 3 * hid), BF),
+    own_pieces = [piece] + [send(piece, part_perm(q)) for q in range(2, SPLIT, 2)]
+    sib_pieces = [send(p, part_perm(1)) for p in own_pieces]
+    chips = SPLIT // 2
+    halves = [(0, chips - 1), tuple(range(1, chips - 1))]
+    ordered = [[own_pieces[j] for j in js] + [sib_pieces[j] for j in js] for js in halves]
+    mark, parts, recv = (), [], []
+    for i, pieces in enumerate(ordered):
+        n = len(pieces) * rows // 2
+        part, part_sent, *mark = call(
+            forward_body,
+            [sds((n, 3 * hid), F32), sds((n, 3 * hid), BF)],
+            (*pieces, wg, wu, down),
+            extra=2 * n * half * 2 + n * hid * 4,
+            after=mark,
+            mark=i == 0,
+        )
+        parts.append(part)
+        recv.append([send(part_sent, batch_perm(dx)) for dx in range(1, n_dp)])
+    lefts, sums, mark = [], {}, ()
+    for i, js in enumerate(halves):
+        n = parts[i].shape[0]
+        rows_h, rows_a, rows_b, own, sib, *mark = call(
+            functools.partial(backward_body, 2 * len(js), n_dp - 1),
+            [sds((n, hid), BF)] * 3 + [sds((n, half), BF)] * 2,
+            (parts[i], *recv[i], wg, wu, down),
+            extra=n * half * 12,
+            after=mark,
+            mark=i == 0,
+        )
+        lefts += [rows_a, rows_b, rows_h]
+        got = call(
+            pair_sum_body, [sds((rows, half), BF)] * len(js), (own, send(sib, part_perm(1)))
+        )
+        sums.update(zip(js, got))
+    back = [sums[0]] + [send(sums[j], part_perm(2 * j)) for js in halves for j in js if j]
+    *grads, mark = call(
+        grads_body,
+        [sds((1, half, hid), BF)] * 3,
+        (*ordered[0], *ordered[1], *lefts),
+        out_specs=[HBM] * 3,
+        scratch=[pltpu.VMEM((n_rows, half), BF)] * 2
+        + [
+            pltpu.VMEM((n_rows, hid), BF),
+            pltpu.VMEM((3, half, hid), BF),
+            pltpu.SemaphoreType.DMA((3,)),
         ],
-        (*pieces, wg, wu, down),
-    )
-    recv = [send(part_sent, batch_perm(dx)) for dx in range(1, n_dp)]
-    rows_h, rows_a, rows_b, own, sib = call(
-        functools.partial(backward_body, n_dp - 1),
-        [sds((n_rows, hid), BF)] * 3 + [sds((n_rows, half), BF)] * 2,
-        (part, *recv, wg, wu, down),
-        extra=n_rows * half * 12,
-    )
-    sums = call(
-        pair_sum_body, [sds((rows, half), BF)] * (SPLIT // 2), (own, send(sib, part_perm(1)))
-    )
-    back = [sums[0]] + [send(sums[j], part_perm(2 * j)) for j in range(1, SPLIT // 2)]
-    count = each * experts
-    *grads, put_out, put_grad, scale, mark = call(
-        functools.partial(grads_body, experts, slots),
-        [sds((1, half, hid), BF)] * 3 + [sds((block, count), BF)] * 2 + [sds((count, 1), F32)],
-        (routes[0], gate_values[0], xs, ys, rows_a, rows_b, rows_h),
-        in_specs=[SMEM] * 2 + [VMEM] * 5,
-        out_specs=[HBM] * 3 + [VMEM] * 3,
-        scratch=[pltpu.VMEM((3, half, hid), BF), pltpu.SemaphoreType.DMA((3,))],
-        extra=n_rows * half * 4 + half * hid * 12,
+        extra=n_rows * half * 8 + half * hid * 12,
         mark=True,
         cost=pl.CostEstimate(
             flops=6 * n_rows * half * hid, bytes_accessed=6 * half * hid, transcendentals=0

time: 51.8 us -> 49 us (0.946)
  waiting for transfers between devices: 21.7 us -> 16.2 us
  starting transfers between devices: 18.3 us -> 20.5 us
  Pallas kernels: 10.1 us -> 11.3 us
  local copies, waits for them, and re-layouts: 0.69 us -> 0.01 us
    ppermute x18 -> x20, waiting for transfers between devices: 21.7 us -> 16.2 us  [send(): return lax.ppermute(x, AXES, perm)]
    ppermute x18 -> x20, starting transfers between devices: 18.3 us -> 20.5 us  [send(): return lax.ppermute(x, AXES, perm)]
    pallas_call x9 -> x12, Pallas kernels: 10.1 us -> 11.3 us  [call(): pl.pallas_call(whole, out_shape=[*out_shape, *[jax.ShapeDtypeStruct((8, 1...]
    unnamed x8 -> x4, local copies, waits for them, and re-layouts: 0.69 us -> 0.01 us
  transfers between devices with their start and end apart: 18 -> 20, of which waited for: 14 -> 11; matrix products, arithmetic and copies ran while one was open for 0% -> 0% of each run, Pallas kernels for 8% -> 15%
where the time goes in v3:
time: 49 us; the launch traced here: 48.8 us
  starting transfers between devices  20.5 us (42%)
  waiting for transfers between devices  16.2 us (33%)
  Pallas kernels  11.3 us (23%)
  between operations  0.75 us (2%)
    ppermute x20, starting transfers between devices, send(): return lax.ppermute(x, AXES, perm)  20.5 us
    ppermute x20, waiting for transfers between devices, send(): return lax.ppermute(x, AXES, perm)  16.2 us
    pallas_call x12, Pallas kernels, call(): pl.pallas_call(whole, out_shape=[*out_shape, *[jax.ShapeDtypeStruct((8, 1...  11.3 us
  transfers between devices with their start and end apart: 20, of which 11 were waited for; matrix products, arithmetic and copies ran while one was open for 0% of the time, Pallas kernels for 15%

profile of v3, /device:TPU:0, one launch (start us, length us, event | category | flops | bytes accessed | tf_op | source)
XLA Modules:
  0.0 48.8 jit_solution(9836215060728464424)
XLA Ops:
  0.6 1.9 %shard_map.111 = (bf16[8,2048]{1,0:T(8,128)(2,1)S(1)}, bf16[8,2048]{1,0:T(8,128)(2,1)S(1)}, bf16[8,2048]{1,0:T(8,128)(2,1)S(1)}, bf16[8,2048]{1,0:T(8,128)(2,1)S(1)}) custom-call(s32[2,4]{1,0:T(2,128)} %bitcast.2, f32[2,4]{1,0:T(2,128)} %bitcast.4, bf16[128,4096]{1,0:T(8,128)(2,1)} %refs_2_.3, bf16[128,4096]{1,0:T(8,128)(2,1)} %refs_3_.3), custom_call_target="tpu_custom_call" | custom-call | tf_op jit(solution)/shard_map/pallas_call | solution.py:61
  2.6 0.0 copy-start
  2.6 5.0 %collective-permute-start = (bf16[8,2048]{1,0:T(8,128)(2,1)S(1)}, bf16[8,2048]{1,0:T(8,128)(2,1)S(1)}, u32[]{:S(2)}, u32[]{:S(2)}) collective-permute-start(bf16[8,2048]{1,0:T(8,128)(2,1)S(1)} %get-tuple-element.47), channel_id=1, source_target_pairs={{0,24},{1,25},{2,26},{3,27},{4,28},{5,29},{6,30},{7,31},{8,16},{9,... | collective-permute-start | bytes 98312 | tf_op jit(solution)/shard_map/ppermute | solution.py:307
  7.6 0.3 collective-permute-start.1
  8.0 0.3 collective-permute-start.2
  8.3 1.3 %shard_map.110 = (bf16[1,2048,256]{2,1,0:T(8,128)(2,1)S(1)}, bf16[128,16]{1,0:T(8,128)(2,1)S(1)}, bf16[128,16]{1,0:T(8,128)(2,1)S(1)}, f32[16,1]{1,0:T(8,128)S(1)}, f32[8,128]{1,0:T(8,128)S(1)}) custom-call(bf16[1,2048,256]{2,1,0:T(8,128)(2,1)} %refs_0_.1, s32[2,4]{1,0:T(2,128)} %bitcast.3, f32[2,4]{1,0:T(2,128)} %bitcast.5), custom_call_target="tpu_custom_call" | custom-call | tf_op jit(solution)/shard_map/pallas_call | solution.py:61
  9.5 0.3 collective-permute-done.refs_0_
  9.9 2.6 %collective-permute-done.1.refs_1_ = bf16[8,2048]{1,0:T(8,128)(2,1)S(1)} collective-permute-done((bf16[8,2048]{1,0:T(8,128)(2,1)S(1)}, bf16[8,2048]{1,0:T(8,128)(2,1)S(1)}, u32[]{:S(2)}, u32[]{:S(2)}) %collective-permute-start.1) | collective-permute-done | bytes 32800 | tf_op jit(solution)/shard_map/ppermute | solution.py:307
  12.4 0.2 shard_map.112.refs_0_
  12.6 2.6 %collective-permute-start.3 = (bf16[32,2048]{1,0:T(8,128)(2,1)S(1)}, bf16[32,2048]{1,0:T(8,128)(2,1)S(1)}, u32[]{:S(2)}, u32[]{:S(2)}) collective-permute-start(bf16[32,2048]{1,0:T(8,128)(2,1)S(1)} %shard_map.112.refs_0_), channel_id=1, source_target_pairs={{0,6},{1,7},{2,4},{3,5},{4,2},{5,3},{6,0},{7,1},{8,14},{9,15},{10,... | collective-permute-start | bytes 393224 | tf_op jit(solution)/shard_map/ppermute | solution.py:307
  15.2 0.4 collective-permute-start.10
  15.7 0.5 %collective-permute-start.9 = (bf16[32,2048]{1,0:T(8,128)(2,1)S(1)}, bf16[32,2048]{1,0:T(8,128)(2,1)S(1)}, u32[]{:S(2)}, u32[]{:S(2)}) collective-permute-start(bf16[32,2048]{1,0:T(8,128)(2,1)S(1)} %shard_map.112.refs_0_), channel_id=1, source_target_pairs={{0,2},{1,3},{2,0},{3,1},{4,6},{5,7},{6,4},{7,5},{8,10},{9,11},{10,... | collective-permute-start | bytes 393224 | tf_op jit(solution)/shard_map/ppermute | solution.py:307
  16.2 0.0 collective-permute-start.4
  16.2 2.9 %collective-permute-done.3.refs_1_ = bf16[32,2048]{1,0:T(8,128)(2,1)S(1)} collective-permute-done((bf16[32,2048]{1,0:T(8,128)(2,1)S(1)}, bf16[32,2048]{1,0:T(8,128)(2,1)S(1)}, u32[]{:S(2)}, u32[]{:S(2)}) %collective-permute-start.3) | collective-permute-done | bytes 131104 | tf_op jit(solution)/shard_map/ppermute | solution.py:307
  19.1 0.0 collective-permute-start.5
  19.1 1.3 %collective-permute-done.10.refs_1_.refs_5_ = bf16[32,2048]{1,0:T(8,128)(2,1)S(1)} collective-permute-done((bf16[32,2048]{1,0:T(8,128)(2,1)S(1)}, bf16[32,2048]{1,0:T(8,128)(2,1)S(1)}, u32[]{:S(2)}, u32[]{:S(2)}) %collective-permute-start.10) | collective-permute-done | bytes 131104 | tf_op jit(solution)/shard_map/ppermute | solution.py:307
  20.4 0.0 collective-permute-start.12
  20.4 0.2 collective-permute-done.9.refs_0_.refs_4_
  20.6 0.3 collective-permute-start.11
  21.0 0.7 %shard_map.113 = (f32[64,768]{1,0:T(8,128)S(1)}, bf16[64,768]{1,0:T(8,128)(2,1)S(1)}, f32[8,128]{1,0:T(8,128)S(1)}) custom-call(bf16[32,2048]{1,0:T(8,128)(2,1)S(1)} %shard_map.112.refs_0_, bf16[32,2048]{1,0:T(8,128)(2,1)S(1)} %collective-permute-done.3.refs_1_, bf16[32,2048]{1,0:T(8,128)(2,1)S(1)} %collective-permute-done.4.refs_2_, ...), custom_call_target="tpu_custom_call" | custom-call | tf_op jit(solution)/shard_map/pallas_call | solution.py:61
  21.7 0.7 %collective-permute-start.6 = (bf16[64,768]{1,0:T(8,128)(2,1)S(1)}, bf16[64,768]{1,0:T(8,128)(2,1)S(1)}, u32[]{:S(2)}, u32[]{:S(2)}) collective-permute-start(bf16[64,768]{1,0:T(8,128)(2,1)S(1)} %get-tuple-element.54), channel_id=1, source_target_pairs={{0,16},{1,17},{2,18},{3,19},{4,20},{5,21},{6,22},{7,23},{8,24},{9,... | collective-permute-start | bytes 294920 | tf_op jit(solution)/shard_map/ppermute | solution.py:307
  22.3 0.0 collective-permute-done.12.refs_3_.refs_7_
  22.3 0.0 collective-permute-done.11.refs_2_.refs_6_
  22.3 0.7 %shard_map.116 = (f32[64,768]{1,0:T(8,128)S(1)}, bf16[64,768]{1,0:T(8,128)(2,1)S(1)}) custom-call(bf16[32,2048]{1,0:T(8,128)(2,1)S(1)} %collective-permute-done.9.refs_0_.refs_4_, bf16[32,2048]{1,0:T(8,128)(2,1)S(1)} %collective-permute-done.10.refs_1_.refs_5_, bf16[32,2048]{1,0:T(8,128)(2,1)S(1)} %collective-permute-done.11.refs_2_.refs_6_, ...), custom_call_target="tpu_custom_call" | custom-call | tf_op jit(solution)/shard_map/pallas_call | solution.py:61
  23.0 1.5 %collective-permute-start.13 = (bf16[64,768]{1,0:T(8,128)(2,1)S(1)}, bf16[64,768]{1,0:T(8,128)(2,1)S(1)}, u32[]{:S(2)}, u32[]{:S(2)}) collective-permute-start(bf16[64,768]{1,0:T(8,128)(2,1)S(1)} %get-tuple-element.61), channel_id=1, source_target_pairs={{0,16},{1,17},{2,18},{3,19},{4,20},{5,21},{6,22},{7,23},{8,24},{9,... | collective-permute-start | bytes 294920 | tf_op jit(solution)/shard_map/ppermute | solution.py:307
  24.5 2.9 %collective-permute-done.6.refs_1_ = bf16[64,768]{1,0:T(8,128)(2,1)S(1)} collective-permute-done((bf16[64,768]{1,0:T(8,128)(2,1)S(1)}, bf16[64,768]{1,0:T(8,128)(2,1)S(1)}, u32[]{:S(2)}, u32[]{:S(2)}) %collective-permute-start.6) | collective-permute-done | bytes 98336 | tf_op jit(solution)/shard_map/ppermute | solution.py:307
  27.3 1.1 %shard_map.114 = (bf16[64,256]{1,0:T(8,128)(2,1)S(1)}, bf16[64,256]{1,0:T(8,128)(2,1)S(1)}, bf16[64,256]{1,0:T(8,128)(2,1)S(1)}, bf16[64,2048]{1,0:T(8,128)(2,1)...) custom-call(f32[64,768]{1,0:T(8,128)S(1)} %get-tuple-element.53.refs_0_, ...), custom_call_target="tpu_custom_call" | custom-call | tf_op jit(solution)/shard_map/pallas_call | solution.py:61
  28.4 0.1 collective-permute-start.7
  28.5 0.2 collective-permute-done.13.refs_1_
  28.7 1.1 %shard_map.117 = (bf16[64,256]{1,0:T(8,128)(2,1)S(1)}, bf16[64,256]{1,0:T(8,128)(2,1)S(1)}, bf16[64,256]{1,0:T(8,128)(2,1)S(1)}, bf16[64,2048]{1,0:T(8,128)(2,1)S(1)}, bf16[64,2048]{1,0:T(8,128)(2,1)S(1)}) custom-call(f32[64,768]{1,0:T(8,128)S(1)} %get-tuple-element.60.refs_0_, bf16[64,768]{1,0:T(8,128)(2,1)S(1)} %collective-permute-done.13.refs_1_, ...), custom_call_target="tpu_custom_call" | custom-call | tf_op jit(solution)/shard_map/pallas_call | solution.py:61
  29.8 0.4 collective-permute-start.14
  30.1 0.0 collective-permute-done.7.refs_1_
  30.1 0.1 shard_map.115
  30.2 1.9 %collective-permute-start.8 = (bf16[32,2048]{1,0:T(8,128)(2,1)S(1)}, bf16[32,2048]{1,0:T(8,128)(2,1)S(1)}, u32[]{:S(2)}, u32[]{:S(2)}) collective-permute-start(bf16[32,2048]{1,0:T(8,128)(2,1)S(1)} %get-tuple-element.58), channel_id=1, source_target_pairs={{0,6},{1,7},{2,4},{3,5},{4,2},{5,3},{6,0},{7,1},{8,14},{9,15},{10,... | collective-permute-start | bytes 393224 | tf_op jit(solution)/shard_map/ppermute | solution.py:307
  32.1 0.0 collective-permute-done.14.refs_1_
  32.1 0.1 shard_map.118
  32.2 1.1 %collective-permute-start.15 = (bf16[32,2048]{1,0:T(8,128)(2,1)S(1)}, bf16[32,2048]{1,0:T(8,128)(2,1)S(1)}, u32[]{:S(2)}, u32[]{:S(2)}) collective-permute-start(bf16[32,2048]{1,0:T(8,128)(2,1)S(1)} %get-tuple-element.65), channel_id=1, source_target_pairs={{0,2},{1,3},{2,0},{3,1},{4,6},{5,7},{6,4},{7,5},{8,10},{9,11},{10,... | collective-permute-start | bytes 393224 | tf_op jit(solution)/shard_map/ppermute | solution.py:307
  33.2 0.9 %collective-permute-start.16 = (bf16[32,2048]{1,0:T(8,128)(2,1)S(1)}, bf16[32,2048]{1,0:T(8,128)(2,1)S(1)}, u32[]{:S(2)}, u32[]{:S(2)}) collective-permute-start(bf16[32,2048]{1,0:T(8,128)(2,1)S(1)} %get-tuple-element.66), channel_id=1, source_target_pairs={{0,4},{1,5},{2,6},{3,7},{4,0},{5,1},{6,2},{7,3},{8,12},{9,13},{10,... | collective-permute-start | bytes 393224 | tf_op jit(solution)/shard_map/ppermute | solution.py:307
  34.2 2.4 %shard_map.119 = (bf16[1,2048,256]{2,1,0:T(8,128)(2,1)}, bf16[1,2048,256]{2,1,0:T(8,128)(2,1)}, bf16[1,2048,256]{2,1,0:T(8,128)(2,1)}, f32[8,128]{1,0:T(8,128)S(1)}) custom-call(bf16[32,2048]{1,0:T(8,128)(2,1)S(1)} %shard_map.112.refs_0_, bf16[32,2048]{1,0:T(8,128)(2,1)S(1)} %collective-permute-done.3.refs_1_, ...), custom_call_target="tpu_custom_call" | custom-call | flops 402653184 | bytes 3145728 | tf_op jit(solution)/shard_map/pallas_call | solution.py:61
  36.5 0.8 %collective-permute-done.8.refs_1_ = bf16[32,2048]{1,0:T(8,128)(2,1)S(1)} collective-permute-done((bf16[32,2048]{1,0:T(8,128)(2,1)S(1)}, bf16[32,2048]{1,0:T(8,128)(2,1)S(1)}, u32[]{:S(2)}, u32[]{:S(2)}) %collective-permute-start.8) | collective-permute-done | bytes 131104 | tf_op jit(solution)/shard_map/ppermute | solution.py:307
  37.3 2.3 %collective-permute-done.15.refs_2_ = bf16[32,2048]{1,0:T(8,128)(2,1)S(1)} collective-permute-done((bf16[32,2048]{1,0:T(8,128)(2,1)S(1)}, bf16[32,2048]{1,0:T(8,128)(2,1)S(1)}, u32[]{:S(2)}, u32[]{:S(2)}) %collective-permute-start.15) | collective-permute-done | bytes 131104 | tf_op jit(solution)/shard_map/ppermute | solution.py:307
  39.6 0.2 shard_map.120
  39.8 2.1 %collective-permute-start.17 = (bf16[8,2048]{1,0:T(8,128)(2,1)S(1)}, bf16[8,2048]{1,0:T(8,128)(2,1)S(1)}, u32[]{:S(2)}, u32[]{:S(2)}) collective-permute-start(bf16[8,2048]{1,0:T(8,128)(2,1)S(1)} %get-tuple-element.74), channel_id=1, source_target_pairs={{0,24},{1,25},{2,26},{3,27},{4,28},{5,29},{6,30},{7,31},{8,16},{9,... | collective-permute-start | bytes 98312 | tf_op jit(solution)/shard_map/ppermute | solution.py:307
  41.9 0.9 %collective-permute-start.18 = (bf16[8,2048]{1,0:T(8,128)(2,1)S(1)}, bf16[8,2048]{1,0:T(8,128)(2,1)S(1)}, u32[]{:S(2)}, u32[]{:S(2)}) collective-permute-start(bf16[8,2048]{1,0:T(8,128)(2,1)S(1)} %get-tuple-element.75), channel_id=1, source_target_pairs={{0,8},{1,9},{2,10},{3,11},{4,12},{5,13},{6,14},{7,15},{8,0},{9,1},... | collective-permute-start | bytes 98312 | tf_op jit(solution)/shard_map/ppermute | solution.py:307
  42.8 1.5 %collective-permute-start.19 = (bf16[8,2048]{1,0:T(8,128)(2,1)S(1)}, bf16[8,2048]{1,0:T(8,128)(2,1)S(1)}, u32[]{:S(2)}, u32[]{:S(2)}) collective-permute-start(bf16[8,2048]{1,0:T(8,128)(2,1)S(1)} %get-tuple-element.76), channel_id=1, source_target_pairs={{0,16},{1,17},{2,18},{3,19},{4,20},{5,21},{6,22},{7,23},{8,24},{9,... | collective-permute-start | bytes 98312 | tf_op jit(solution)/shard_map/ppermute | solution.py:307
  44.3 1.7 %collective-permute-done.17.refs_3_ = bf16[8,2048]{1,0:T(8,128)(2,1)S(1)} collective-permute-done((bf16[8,2048]{1,0:T(8,128)(2,1)S(1)}, bf16[8,2048]{1,0:T(8,128)(2,1)S(1)}, u32[]{:S(2)}, u32[]{:S(2)}) %collective-permute-start.17) | collective-permute-done | bytes 32800 | tf_op jit(solution)/shard_map/ppermute | solution.py:307
  45.9 1.0 %collective-permute-done.18.refs_4_ = bf16[8,2048]{1,0:T(8,128)(2,1)S(1)} collective-permute-done((bf16[8,2048]{1,0:T(8,128)(2,1)S(1)}, bf16[8,2048]{1,0:T(8,128)(2,1)S(1)}, u32[]{:S(2)}, u32[]{:S(2)}) %collective-permute-start.18) | collective-permute-done | bytes 32800 | tf_op jit(solution)/shard_map/ppermute | solution.py:307
  46.9 1.9 %shard_map.121 = (bf16[128,4096]{1,0:T(8,128)(2,1)}, bf16[128,4096]{1,0:T(8,128)(2,1)}) custom-call(bf16[128,16]{1,0:T(8,128)(2,1)S(1)} %get-tuple-element.44.refs_0_, bf16[128,16]{1,0:T(8,128)(2,1)S(1)} %get-tuple-element.45.refs_1_, f32[16,1]{1,0:T(8,128)S(1)} %get-tuple-element.46.refs_2_, bf16[8,2048]{1,0:T(8,128)(2,1)S(1)} %collective-permute-done.17.refs_3_, ...), custom_call_target="tpu_custom_call" | custom-call | tf_op jit(solution)/shard_map/pallas_call | solution.py:61
  (8 shorter events, 0.0 us)
Async XLA Ops:
  0.6 20.3 %copy-start.1 = (bf16[1,2048,256]{2,1,0:T(8,128)(2,1)S(1)}, bf16[1,2048,256]{2,1,0:T(8,128)(2,1)}, u32[]{:S(2)}) copy-start(bf16[1,2048,256]{2,1,0:T(8,128)(2,1)} %refs_3_.5) | copy-start | bytes 3145732
  2.6 18.4 %copy-start = (bf16[1,2048,256]{2,1,0:T(8,128)(2,1)S(1)}, bf16[1,2048,256]{2,1,0:T(8,128)(2,1)}, u32[]{:S(2)}) copy-start(bf16[1,2048,256]{2,1,0:T(8,128)(2,1)} %refs_2_.5) | copy-start | bytes 3145732
  2.6 7.3 %collective-permute-start = (bf16[8,2048]{1,0:T(8,128)(2,1)S(1)}, bf16[8,2048]{1,0:T(8,128)(2,1)S(1)}, u32[]{:S(2)}, u32[]{:S(2)}) collective-permute-start(bf16[8,2048]{1,0:T(8,128)(2,1)S(1)} %get-tuple-element.47), channel_id=1, source_target_pairs={{0,24},{1,25},{2,26},{3,27},{4,28},{5,29},{6,30},{7,31},{8,16},{9,... | collective-permute-start | bytes 98312 | tf_op jit(solution)/shard_map/ppermute | solution.py:307
  7.6 4.8 %collective-permute-start.1 = (bf16[8,2048]{1,0:T(8,128)(2,1)S(1)}, bf16[8,2048]{1,0:T(8,128)(2,1)S(1)}, u32[]{:S(2)}, u32[]{:S(2)}) collective-permute-start(bf16[8,2048]{1,0:T(8,128)(2,1)S(1)} %get-tuple-element.48), channel_id=1, source_target_pairs={{0,8},{1,9},{2,10},{3,11},{4,12},{5,13},{6,14},{7,15},{8,0},{9,1},... | collective-permute-start | bytes 98312 | tf_op jit(solution)/shard_map/ppermute | solution.py:307
  8.0 4.5 %collective-permute-start.2 = (bf16[8,2048]{1,0:T(8,128)(2,1)S(1)}, bf16[8,2048]{1,0:T(8,128)(2,1)S(1)}, u32[]{:S(2)}, u32[]{:S(2)}) collective-permute-start(bf16[8,2048]{1,0:T(8,128)(2,1)S(1)} %get-tuple-element.49), channel_id=1, source_target_pairs={{0,16},{1,17},{2,18},{3,19},{4,20},{5,21},{6,22},{7,23},{8,24},{9,... | collective-permute-start | bytes 98312 | tf_op jit(solution)/shard_map/ppermute | solution.py:307
  12.6 6.5 %collective-permute-start.3 = (bf16[32,2048]{1,0:T(8,128)(2,1)S(1)}, bf16[32,2048]{1,0:T(8,128)(2,1)S(1)}, u32[]{:S(2)}, u32[]{:S(2)}) collective-permute-start(bf16[32,2048]{1,0:T(8,128)(2,1)S(1)} %shard_map.112.refs_0_), channel_id=1, source_target_pairs={{0,6},{1,7},{2,4},{3,5},{4,2},{5,3},{6,0},{7,1},{8,14},{9,15},{10,... | collective-permute-start | bytes 393224 | tf_op jit(solution)/shard_map/ppermute | solution.py:307
  15.2 5.2 %collective-permute-start.10 = (bf16[32,2048]{1,0:T(8,128)(2,1)S(1)}, bf16[32,2048]{1,0:T(8,128)(2,1)S(1)}, u32[]{:S(2)}, u32[]{:S(2)}) collective-permute-start(bf16[32,2048]{1,0:T(8,128)(2,1)S(1)} %shard_map.112.refs_0_), channel_id=1, source_target_pairs={{0,4},{1,5},{2,6},{3,7},{4,0},{5,1},{6,2},{7,3},{8,12},{9,13},{10,... | collective-permute-start | bytes 393224 | tf_op jit(solution)/shard_map/ppermute | solution.py:307
  15.7 5.0 %collective-permute-start.9 = (bf16[32,2048]{1,0:T(8,128)(2,1)S(1)}, bf16[32,2048]{1,0:T(8,128)(2,1)S(1)}, u32[]{:S(2)}, u32[]{:S(2)}) collective-permute-start(bf16[32,2048]{1,0:T(8,128)(2,1)S(1)} %shard_map.112.refs_0_), channel_id=1, source_target_pairs={{0,2},{1,3},{2,0},{3,1},{4,6},{5,7},{6,4},{7,5},{8,10},{9,11},{10,... | collective-permute-start | bytes 393224 | tf_op jit(solution)/shard_map/ppermute | solution.py:307
  16.2 4.8 %collective-permute-start.4 = (bf16[32,2048]{1,0:T(8,128)(2,1)S(1)}, bf16[32,2048]{1,0:T(8,128)(2,1)S(1)}, u32[]{:S(2)}, u32[]{:S(2)}) collective-permute-start(bf16[32,2048]{1,0:T(8,128)(2,1)S(1)} %shard_map.112.refs_0_), channel_id=1, source_target_pairs={{0,1},{1,0},{2,3},{3,2},{4,5},{5,4},{6,7},{7,6},{8,9},{9,8},{10,11... | collective-permute-start | bytes 393224 | tf_op jit(solution)/shard_map/ppermute | solution.py:307
  19.1 1.9 %collective-permute-start.5 = (bf16[32,2048]{1,0:T(8,128)(2,1)S(1)}, bf16[32,2048]{1,0:T(8,128)(2,1)S(1)}, u32[]{:S(2)}, u32[]{:S(2)}) collective-permute-start(bf16[32,2048]{1,0:T(8,128)(2,1)S(1)} %collective-permute-done.3.refs_1_), channel_id=1, source_target_pairs={{0,1},{1,0},{2,3},{3,2},{4,5},{5,4},{6,7},{7,6},{8,9},{9,8},{10,11... | collective-permute-start | bytes 393224 | tf_op jit(solution)/shard_map/ppermute | solution.py:307
  20.4 1.9 %collective-permute-start.12 = (bf16[32,2048]{1,0:T(8,128)(2,1)S(1)}, bf16[32,2048]{1,0:T(8,128)(2,1)S(1)}, u32[]{:S(2)}, u32[]{:S(2)}) collective-permute-start(bf16[32,2048]{1,0:T(8,128)(2,1)S(1)} %collective-permute-done.10.refs_1_.refs_5_), channel_id=1, source_target_pairs={{0,1},{1,0},{2,3},{3,2},{4,5},{5,4},{6,7},{7,6},{8,9},{9,8},{10,11... | collective-permute-start | bytes 393224 | tf_op jit(solution)/shard_map/ppermute | solution.py:307
  20.6 1.7 %collective-permute-start.11 = (bf16[32,2048]{1,0:T(8,128)(2,1)S(1)}, bf16[32,2048]{1,0:T(8,128)(2,1)S(1)}, u32[]{:S(2)}, u32[]{:S(2)}) collective-permute-start(bf16[32,2048]{1,0:T(8,128)(2,1)S(1)} %collective-permute-done.9.refs_0_.refs_4_), channel_id=1, source_target_pairs={{0,1},{1,0},{2,3},{3,2},{4,5},{5,4},{6,7},{7,6},{8,9},{9,8},{10,11... | collective-permute-start | bytes 393224 | tf_op jit(solution)/shard_map/ppermute | solution.py:307
  21.7 5.7 %collective-permute-start.6 = (bf16[64,768]{1,0:T(8,128)(2,1)S(1)}, bf16[64,768]{1,0:T(8,128)(2,1)S(1)}, u32[]{:S(2)}, u32[]{:S(2)}) collective-permute-start(bf16[64,768]{1,0:T(8,128)(2,1)S(1)} %get-tuple-element.54), channel_id=1, source_target_pairs={{0,16},{1,17},{2,18},{3,19},{4,20},{5,21},{6,22},{7,23},{8,24},{9,... | collective-permute-start | bytes 294920 | tf_op jit(solution)/shard_map/ppermute | solution.py:307
  23.0 5.7 %collective-permute-start.13 = (bf16[64,768]{1,0:T(8,128)(2,1)S(1)}, bf16[64,768]{1,0:T(8,128)(2,1)S(1)}, u32[]{:S(2)}, u32[]{:S(2)}) collective-permute-start(bf16[64,768]{1,0:T(8,128)(2,1)S(1)} %get-tuple-element.61), channel_id=1, source_target_pairs={{0,16},{1,17},{2,18},{3,19},{4,20},{5,21},{6,22},{7,23},{8,24},{9,... | collective-permute-start | bytes 294920 | tf_op jit(solution)/shard_map/ppermute | solution.py:307
  28.4 1.7 %collective-permute-start.7 = (bf16[64,2048]{1,0:T(8,128)(2,1)S(1)}, bf16[64,2048]{1,0:T(8,128)(2,1)S(1)}, u32[]{:S(2)}, u32[]{:S(2)}) collective-permute-start(bf16[64,2048]{1,0:T(8,128)(2,1)S(1)} %get-tuple-element.56), channel_id=1, source_target_pairs={{0,1},{1,0},{2,3},{3,2},{4,5},{5,4},{6,7},{7,6},{8,9},{9,8},{10,11... | collective-permute-start | bytes 786440 | tf_op jit(solution)/shard_map/ppermute | solution.py:307
  29.8 2.3 %collective-permute-start.14 = (bf16[64,2048]{1,0:T(8,128)(2,1)S(1)}, bf16[64,2048]{1,0:T(8,128)(2,1)S(1)}, u32[]{:S(2)}, u32[]{:S(2)}) collective-permute-start(bf16[64,2048]{1,0:T(8,128)(2,1)S(1)} %get-tuple-element.64), channel_id=1, source_target_pairs={{0,1},{1,0},{2,3},{3,2},{4,5},{5,4},{6,7},{7,6},{8,9},{9,8},{10,11... | collective-permute-start | bytes 786440 | tf_op jit(solution)/shard_map/ppermute | solution.py:307
  30.2 7.1 %collective-permute-start.8 = (bf16[32,2048]{1,0:T(8,128)(2,1)S(1)}, bf16[32,2048]{1,0:T(8,128)(2,1)S(1)}, u32[]{:S(2)}, u32[]{:S(2)}) collective-permute-start(bf16[32,2048]{1,0:T(8,128)(2,1)S(1)} %get-tuple-element.58), channel_id=1, source_target_pairs={{0,6},{1,7},{2,4},{3,5},{4,2},{5,3},{6,0},{7,1},{8,14},{9,15},{10,... | collective-permute-start | bytes 393224 | tf_op jit(solution)/shard_map/ppermute | solution.py:307
  32.2 7.4 %collective-permute-start.15 = (bf16[32,2048]{1,0:T(8,128)(2,1)S(1)}, bf16[32,2048]{1,0:T(8,128)(2,1)S(1)}, u32[]{:S(2)}, u32[]{:S(2)}) collective-permute-start(bf16[32,2048]{1,0:T(8,128)(2,1)S(1)} %get-tuple-element.65), channel_id=1, source_target_pairs={{0,2},{1,3},{2,0},{3,1},{4,6},{5,7},{6,4},{7,5},{8,10},{9,11},{10,... | collective-permute-start | bytes 393224 | tf_op jit(solution)/shard_map/ppermute | solution.py:307
  33.2 6.4 %collective-permute-start.16 = (bf16[32,2048]{1,0:T(8,128)(2,1)S(1)}, bf16[32,2048]{1,0:T(8,128)(2,1)S(1)}, u32[]{:S(2)}, u32[]{:S(2)}) collective-permute-start(bf16[32,2048]{1,0:T(8,128)(2,1)S(1)} %get-tuple-element.66), channel_id=1, source_target_pairs={{0,4},{1,5},{2,6},{3,7},{4,0},{5,1},{6,2},{7,3},{8,12},{9,13},{10,... | collective-permute-start | bytes 393224 | tf_op jit(solution)/shard_map/ppermute | solution.py:307
  39.8 6.1 %collective-permute-start.17 = (bf16[8,2048]{1,0:T(8,128)(2,1)S(1)}, bf16[8,2048]{1,0:T(8,128)(2,1)S(1)}, u32[]{:S(2)}, u32[]{:S(2)}) collective-permute-start(bf16[8,2048]{1,0:T(8,128)(2,1)S(1)} %get-tuple-element.74), channel_id=1, source_target_pairs={{0,24},{1,25},{2,26},{3,27},{4,28},{5,29},{6,30},{7,31},{8,16},{9,... | collective-permute-start | bytes 98312 | tf_op jit(solution)/shard_map/ppermute | solution.py:307
  41.9 5.1 %collective-permute-start.18 = (bf16[8,2048]{1,0:T(8,128)(2,1)S(1)}, bf16[8,2048]{1,0:T(8,128)(2,1)S(1)}, u32[]{:S(2)}, u32[]{:S(2)}) collective-permute-start(bf16[8,2048]{1,0:T(8,128)(2,1)S(1)} %get-tuple-element.75), channel_id=1, source_target_pairs={{0,8},{1,9},{2,10},{3,11},{4,12},{5,13},{6,14},{7,15},{8,0},{9,1},... | collective-permute-start | bytes 98312 | tf_op jit(solution)/shard_map/ppermute | solution.py:307
  42.8 4.2 %collective-permute-start.19 = (bf16[8,2048]{1,0:T(8,128)(2,1)S(1)}, bf16[8,2048]{1,0:T(8,128)(2,1)S(1)}, u32[]{:S(2)}, u32[]{:S(2)}) collective-permute-start(bf16[8,2048]{1,0:T(8,128)(2,1)S(1)} %get-tuple-element.76), channel_id=1, source_target_pairs={{0,16},{1,17},{2,18},{3,19},{4,20},{5,21},{6,22},{7,23},{8,24},{9,... | collective-permute-start | bytes 98312 | tf_op jit(solution)/shard_map/ppermute | solution.py:307

commit v4 on v3

--- a/solution.py
+++ b/solution.py
@@ -12,7 +12,6 @@
 BF = jnp.bfloat16
 F32 = jnp.float32
 AXES = ("dp", "expert")
-NT = (((1,), (1,)), ((), ()))
 TN = (((0,), (0,)), ((), ()))
 ANY = pl.BlockSpec(memory_space=pl.ANY)
 HBM = pl.BlockSpec(memory_space=pltpu.HBM)
@@ -183,11 +182,20 @@
         part_sent[:, i * hid : (i + 1) * hid] = got.astype(BF)
 
 
+def hold_body(src, dst):
+    dst[...] = src[...]
+
+
+def flip_body(*refs):
+    for src, dst in zip(refs[:3], refs[3:]):
+        dst[...] = src[0].T
+
+
 def backward_body(n_pieces, n_recv, *refs):
     part, *rest = refs
     recv, rest = rest[:n_recv], rest[n_recv:]
     wg, wu, wd, rows_h, rows_a, rows_b, own, sib = rest
-    hid = wg.shape[2]
+    hid = wg.shape[0]
     total = part[...]
     for other in recv:
         total = total + other[...].astype(F32)
@@ -199,8 +207,8 @@
     rows_h[...] = h
     rows_a[...] = a
     rows_b[...] = b
-    p = mm(h, wd[0], NT).astype(BF)
-    e = (mm(a, wg[0], NT) + mm(b, wu[0], NT)).astype(BF)
+    p = mm(h, wd[...]).astype(BF)
+    e = (mm(a, wg[...]) + mm(b, wu[...])).astype(BF)
     n = part.shape[0] // n_pieces
     for i in range(n_pieces):
         out, at = (own, i) if 2 * i < n_pieces else (sib, i - n_pieces // 2)
@@ -345,6 +353,10 @@
         after=[mark],
     )
     own_pieces = [piece] + [send(piece, part_perm(q)) for q in range(2, SPLIT, 2)]
+    *flipped, last = call(
+        flip_body, [sds((hid, half), BF)] * 3, (wg, wu, down), extra=8 * hid * half, mark=True
+    )
+    (own_pieces[-1],) = call(hold_body, [sds((rows, half), BF)], [own_pieces[-1]], after=[last])
     sib_pieces = [send(p, part_perm(1)) for p in own_pieces]
     chips = SPLIT // 2
     halves = [(0, chips - 1), tuple(range(1, chips - 1))]
@@ -368,7 +380,7 @@
         rows_h, rows_a, rows_b, own, sib, *mark = call(
             functools.partial(backward_body, 2 * len(js), n_dp - 1),
             [sds((n, hid), BF)] * 3 + [sds((n, half), BF)] * 2,
-            (parts[i], *recv[i], wg, wu, down),
+            (parts[i], *recv[i], *flipped),
             extra=n * half * 12,
             after=mark,
             mark=i == 0,

time: 49 us -> 48.5 us (0.990)
  waiting for transfers between devices: 16.2 us -> 15.7 us
    ppermute x20, waiting for transfers between devices: 16.2 us -> 15.7 us  [send(): return lax.ppermute(x, AXES, perm)]
    pallas_call x12 -> x14, Pallas kernels: 11.3 us -> 11.5 us  [call(): pl.pallas_call(whole, out_shape=[*out_shape, *[jax.ShapeDtypeStruct((8, 1...]
  transfers between devices with their start and end apart: 20 -> 20, of which waited for: 11 -> 12; matrix products, arithmetic and copies ran while one was open for 0% -> 0% of each run, Pallas kernels for 15% -> 15%
where the time goes in v4:
time: 48.5 us; the launch traced here: 48.4 us
  starting transfers between devices  20.5 us (42%)
  waiting for transfers between devices  15.7 us (32%)
  Pallas kernels  11.5 us (24%)
  between operations  0.78 us (2%)
    ppermute x20, starting transfers between devices, send(): return lax.ppermute(x, AXES, perm)  20.5 us
    ppermute x20, waiting for transfers between devices, send(): return lax.ppermute(x, AXES, perm)  15.7 us
    pallas_call x14, Pallas kernels, call(): pl.pallas_call(whole, out_shape=[*out_shape, *[jax.ShapeDtypeStruct((8, 1...  11.5 us
  transfers between devices with their start and end apart: 20, of which 12 were waited for; matrix products, arithmetic and copies ran while one was open for 0% of the time, Pallas kernels for 15%

profile of v4, /device:TPU:0, one launch (start us, length us, event | category | flops | bytes accessed | tf_op | source)
XLA Modules:
  0.0 48.4 jit_solution(16621438364023604641)
XLA Ops:
  0.6 1.9 %shard_map.111 = (bf16[8,2048]{1,0:T(8,128)(2,1)S(1)}, bf16[8,2048]{1,0:T(8,128)(2,1)S(1)}, bf16[8,2048]{1,0:T(8,128)(2,1)S(1)}, bf16[8,2048]{1,0:T(8,128)(2,1)S(1)}) custom-call(s32[2,4]{1,0:T(2,128)} %bitcast.2, f32[2,4]{1,0:T(2,128)} %bitcast.4, bf16[128,4096]{1,0:T(8,128)(2,1)} %refs_2_.1, bf16[128,4096]{1,0:T(8,128)(2,1)} %refs_3_.1), custom_call_target="tpu_custom_call" | custom-call | tf_op jit(solution)/shard_map/pallas_call | solution.py:60
  2.6 0.0 copy-start
  2.6 5.0 %collective-permute-start = (bf16[8,2048]{1,0:T(8,128)(2,1)S(1)}, bf16[8,2048]{1,0:T(8,128)(2,1)S(1)}, u32[]{:S(2)}, u32[]{:S(2)}) collective-permute-start(bf16[8,2048]{1,0:T(8,128)(2,1)S(1)} %get-tuple-element.51), channel_id=1, source_target_pairs={{0,24},{1,25},{2,26},{3,27},{4,28},{5,29},{6,30},{7,31},{8,16},{9,... | collective-permute-start | bytes 98312 | tf_op jit(solution)/shard_map/ppermute | solution.py:315
  7.6 0.3 collective-permute-start.1
  8.0 0.3 collective-permute-start.2
  8.3 1.3 %shard_map.110 = (bf16[1,2048,256]{2,1,0:T(8,128)(2,1)S(1)}, bf16[128,16]{1,0:T(8,128)(2,1)S(1)}, bf16[128,16]{1,0:T(8,128)(2,1)S(1)}, f32[16,1]{1,0:T(8,128)S(1)}, f32[8,128]{1,0:T(8,128)S(1)}) custom-call(bf16[1,2048,256]{2,1,0:T(8,128)(2,1)} %refs_0_.2, s32[2,4]{1,0:T(2,128)} %bitcast.3, f32[2,4]{1,0:T(2,128)} %bitcast.5), custom_call_target="tpu_custom_call" | custom-call | tf_op jit(solution)/shard_map/pallas_call | solution.py:60
  9.5 0.3 collective-permute-done.refs_0_
  9.9 2.6 %collective-permute-done.1.refs_1_ = bf16[8,2048]{1,0:T(8,128)(2,1)S(1)} collective-permute-done((bf16[8,2048]{1,0:T(8,128)(2,1)S(1)}, bf16[8,2048]{1,0:T(8,128)(2,1)S(1)}, u32[]{:S(2)}, u32[]{:S(2)}) %collective-permute-start.1) | collective-permute-done | bytes 32800 | tf_op jit(solution)/shard_map/ppermute | solution.py:315
  12.4 0.2 shard_map.112.refs_0_
  12.6 2.6 %collective-permute-start.3 = (bf16[32,2048]{1,0:T(8,128)(2,1)S(1)}, bf16[32,2048]{1,0:T(8,128)(2,1)S(1)}, u32[]{:S(2)}, u32[]{:S(2)}) collective-permute-start(bf16[32,2048]{1,0:T(8,128)(2,1)S(1)} %shard_map.112.refs_0_), channel_id=1, source_target_pairs={{0,6},{1,7},{2,4},{3,5},{4,2},{5,3},{6,0},{7,1},{8,14},{9,15},{10,... | collective-permute-start | bytes 393224 | tf_op jit(solution)/shard_map/ppermute | solution.py:315
  15.2 0.4 collective-permute-start.10
  15.7 0.5 %collective-permute-start.9 = (bf16[32,2048]{1,0:T(8,128)(2,1)S(1)}, bf16[32,2048]{1,0:T(8,128)(2,1)S(1)}, u32[]{:S(2)}, u32[]{:S(2)}) collective-permute-start(bf16[32,2048]{1,0:T(8,128)(2,1)S(1)} %shard_map.112.refs_0_), channel_id=1, source_target_pairs={{0,2},{1,3},{2,0},{3,1},{4,6},{5,7},{6,4},{7,5},{8,10},{9,11},{10,... | collective-permute-start | bytes 393224 | tf_op jit(solution)/shard_map/ppermute | solution.py:315
  16.2 0.9 %shard_map.113 = (bf16[256,2048]{1,0:T(8,128)(2,1)S(1)}, bf16[256,2048]{1,0:T(8,128)(2,1)S(1)}, bf16[256,2048]{1,0:T(8,128)(2,1)S(1)}, f32[8,128]{1,0:T(8,128)S(1)}) custom-call(bf16[1,2048,256]{2,1,0:T(8,128)(2,1)S(1)} %copy-done, bf16[1,2048,256]{2,1,0:T(8,128)(2,1)S(1)} %copy-done.1, bf16[1,2048,256]{2,1,0:T(8,128)(2,1)S(1)} %get-tuple-element.56.refs_2_.refs_6_), custom_call_target="tpu_custom_call" | custom-call | tf_op jit(solution)/shard_map/pallas_call | solution.py:60
  17.1 0.1 collective-permute-start.4
  17.2 1.9 %collective-permute-done.3.refs_0_ = bf16[32,2048]{1,0:T(8,128)(2,1)S(1)} collective-permute-done((bf16[32,2048]{1,0:T(8,128)(2,1)S(1)}, bf16[32,2048]{1,0:T(8,128)(2,1)S(1)}, u32[]{:S(2)}, u32[]{:S(2)}) %collective-permute-start.3) | collective-permute-done | bytes 131104 | tf_op jit(solution)/shard_map/ppermute | solution.py:315
  19.1 0.1 collective-permute-start.5
  19.2 1.3 %collective-permute-done.10.refs_1_.refs_5_ = bf16[32,2048]{1,0:T(8,128)(2,1)S(1)} collective-permute-done((bf16[32,2048]{1,0:T(8,128)(2,1)S(1)}, bf16[32,2048]{1,0:T(8,128)(2,1)S(1)}, u32[]{:S(2)}, u32[]{:S(2)}) %collective-permute-start.10) | collective-permute-done | bytes 131104 | tf_op jit(solution)/shard_map/ppermute | solution.py:315
  20.4 0.0 collective-permute-start.12
  20.4 0.2 collective-permute-done.9.refs_0_.refs_4_
  20.6 0.3 collective-permute-start.11
  21.0 0.0 collective-permute-done.4.refs_2_
  21.0 0.7 %shard_map.115 = (f32[64,768]{1,0:T(8,128)S(1)}, bf16[64,768]{1,0:T(8,128)(2,1)S(1)}, f32[8,128]{1,0:T(8,128)S(1)}) custom-call(bf16[32,2048]{1,0:T(8,128)(2,1)S(1)} %shard_map.112.refs_0_, bf16[32,2048]{1,0:T(8,128)(2,1)S(1)} %shard_map.114.refs_1_, bf16[32,2048]{1,0:T(8,128)(2,1)S(1)} %collective-permute-done.4.refs_2_, ...), custom_call_target="tpu_custom_call" | custom-call | tf_op jit(solution)/shard_map/pallas_call | solution.py:60
  21.6 0.7 %collective-permute-start.6 = (bf16[64,768]{1,0:T(8,128)(2,1)S(1)}, bf16[64,768]{1,0:T(8,128)(2,1)S(1)}, u32[]{:S(2)}, u32[]{:S(2)}) collective-permute-start(bf16[64,768]{1,0:T(8,128)(2,1)S(1)} %get-tuple-element.59), channel_id=1, source_target_pairs={{0,16},{1,17},{2,18},{3,19},{4,20},{5,21},{6,22},{7,23},{8,24},{9,... | collective-permute-start | bytes 294920 | tf_op jit(solution)/shard_map/ppermute | solution.py:315
  22.3 0.0 collective-permute-done.12.refs_3_.refs_7_
  22.3 0.7 %shard_map.118 = (f32[64,768]{1,0:T(8,128)S(1)}, bf16[64,768]{1,0:T(8,128)(2,1)S(1)}) custom-call(bf16[32,2048]{1,0:T(8,128)(2,1)S(1)} %collective-permute-done.9.refs_0_.refs_4_, bf16[32,2048]{1,0:T(8,128)(2,1)S(1)} %collective-permute-done.10.refs_1_.refs_5_, bf16[32,2048]{1,0:T(8,128)(2,1)S(1)} %collective-permute-done.11.refs_2_.refs_6_, ...), custom_call_target="tpu_custom_call" | custom-call | tf_op jit(solution)/shard_map/pallas_call | solution.py:60
  23.0 1.5 %collective-permute-start.13 = (bf16[64,768]{1,0:T(8,128)(2,1)S(1)}, bf16[64,768]{1,0:T(8,128)(2,1)S(1)}, u32[]{:S(2)}, u32[]{:S(2)}) collective-permute-start(bf16[64,768]{1,0:T(8,128)(2,1)S(1)} %get-tuple-element.69), channel_id=1, source_target_pairs={{0,16},{1,17},{2,18},{3,19},{4,20},{5,21},{6,22},{7,23},{8,24},{9,... | collective-permute-start | bytes 294920 | tf_op jit(solution)/shard_map/ppermute | solution.py:315
  24.5 2.9 %collective-permute-done.6.refs_1_ = bf16[64,768]{1,0:T(8,128)(2,1)S(1)} collective-permute-done((bf16[64,768]{1,0:T(8,128)(2,1)S(1)}, bf16[64,768]{1,0:T(8,128)(2,1)S(1)}, u32[]{:S(2)}, u32[]{:S(2)}) %collective-permute-start.6) | collective-permute-done | bytes 98336 | tf_op jit(solution)/shard_map/ppermute | solution.py:315
  27.3 0.7 %shard_map.116 = (bf16[64,256]{1,0:T(8,128)(2,1)S(1)}, bf16[64,256]{1,0:T(8,128)(2,1)S(1)}, bf16[64,256]{1,0:T(8,128)(2,1)S(1)}, bf16[64,2048]{1,0:T(8,128)(2,1)...) custom-call(f32[64,768]{1,0:T(8,128)S(1)} %get-tuple-element.58.refs_0_, ...), custom_call_target="tpu_custom_call" | custom-call | tf_op jit(solution)/shard_map/pallas_call | solution.py:60
  28.0 0.1 collective-permute-start.7
  28.1 0.6 %collective-permute-done.13.refs_1_ = bf16[64,768]{1,0:T(8,128)(2,1)S(1)} collective-permute-done((bf16[64,768]{1,0:T(8,128)(2,1)S(1)}, bf16[64,768]{1,0:T(8,128)(2,1)S(1)}, u32[]{:S(2)}, u32[]{:S(2)}) %collective-permute-start.13) | collective-permute-done | bytes 98336 | tf_op jit(solution)/shard_map/ppermute | solution.py:315
  28.7 0.7 %shard_map.119 = (bf16[64,256]{1,0:T(8,128)(2,1)S(1)}, bf16[64,256]{1,0:T(8,128)(2,1)S(1)}, bf16[64,256]{1,0:T(8,128)(2,1)S(1)}, bf16[64,2048]{1,0:T(8,128)(2,1)S(1)}, bf16[64,2048]{1,0:T(8,128)(2,1)S(1)}) custom-call(f32[64,768]{1,0:T(8,128)S(1)} %get-tuple-element.68.refs_0_, bf16[64,768]{1,0:T(8,128)(2,1)S(1)} %collective-permute-done.13.refs_1_, ...), custom_call_target="tpu_custom_call" | custom-call | tf_op jit(solution)/shard_map/pallas_call | solution.py:60
  29.4 0.1 collective-permute-start.14
  29.4 0.2 collective-permute-done.7.refs_1_
  29.6 0.1 shard_map.117
  29.7 2.0 %collective-permute-start.8 = (bf16[32,2048]{1,0:T(8,128)(2,1)S(1)}, bf16[32,2048]{1,0:T(8,128)(2,1)S(1)}, u32[]{:S(2)}, u32[]{:S(2)}) collective-permute-start(bf16[32,2048]{1,0:T(8,128)(2,1)S(1)} %get-tuple-element.66), channel_id=1, source_target_pairs={{0,6},{1,7},{2,4},{3,5},{4,2},{5,3},{6,0},{7,1},{8,14},{9,15},{10,... | collective-permute-start | bytes 393224 | tf_op jit(solution)/shard_map/ppermute | solution.py:315
  31.7 0.1 shard_map.120
  31.8 1.0 %collective-permute-start.15 = (bf16[32,2048]{1,0:T(8,128)(2,1)S(1)}, bf16[32,2048]{1,0:T(8,128)(2,1)S(1)}, u32[]{:S(2)}, u32[]{:S(2)}) collective-permute-start(bf16[32,2048]{1,0:T(8,128)(2,1)S(1)} %get-tuple-element.73), channel_id=1, source_target_pairs={{0,2},{1,3},{2,0},{3,1},{4,6},{5,7},{6,4},{7,5},{8,10},{9,11},{10,... | collective-permute-start | bytes 393224 | tf_op jit(solution)/shard_map/ppermute | solution.py:315
  32.8 1.0 %collective-permute-start.16 = (bf16[32,2048]{1,0:T(8,128)(2,1)S(1)}, bf16[32,2048]{1,0:T(8,128)(2,1)S(1)}, u32[]{:S(2)}, u32[]{:S(2)}) collective-permute-start(bf16[32,2048]{1,0:T(8,128)(2,1)S(1)} %get-tuple-element.74), channel_id=1, source_target_pairs={{0,4},{1,5},{2,6},{3,7},{4,0},{5,1},{6,2},{7,3},{8,12},{9,13},{10,... | collective-permute-start | bytes 393224 | tf_op jit(solution)/shard_map/ppermute | solution.py:315
  33.8 2.4 %shard_map.121 = (bf16[1,2048,256]{2,1,0:T(8,128)(2,1)}, bf16[1,2048,256]{2,1,0:T(8,128)(2,1)}, bf16[1,2048,256]{2,1,0:T(8,128)(2,1)}, f32[8,128]{1,0:T(8,128)S(1)}) custom-call(bf16[32,2048]{1,0:T(8,128)(2,1)S(1)} %shard_map.112.refs_0_, bf16[32,2048]{1,0:T(8,128)(2,1)S(1)} %shard_map.114.refs_1_, bf16[32,2048]{1,0:T(8,128)(2,1)S(1)} %collective-permute-done.4.refs_2_, ...), custom_call_target="tpu_custom_call" | custom-call | flops 402653184 | bytes 3145728 | tf_op jit(solution)/shard_map/pallas_call | solution.py:60
  36.1 0.8 %collective-permute-done.8.refs_1_ = bf16[32,2048]{1,0:T(8,128)(2,1)S(1)} collective-permute-done((bf16[32,2048]{1,0:T(8,128)(2,1)S(1)}, bf16[32,2048]{1,0:T(8,128)(2,1)S(1)}, u32[]{:S(2)}, u32[]{:S(2)}) %collective-permute-start.8) | collective-permute-done | bytes 131104 | tf_op jit(solution)/shard_map/ppermute | solution.py:315
  36.9 2.3 %collective-permute-done.15.refs_2_ = bf16[32,2048]{1,0:T(8,128)(2,1)S(1)} collective-permute-done((bf16[32,2048]{1,0:T(8,128)(2,1)S(1)}, bf16[32,2048]{1,0:T(8,128)(2,1)S(1)}, u32[]{:S(2)}, u32[]{:S(2)}) %collective-permute-start.15) | collective-permute-done | bytes 131104 | tf_op jit(solution)/shard_map/ppermute | solution.py:315
  39.2 0.2 shard_map.122
  39.4 2.1 %collective-permute-start.17 = (bf16[8,2048]{1,0:T(8,128)(2,1)S(1)}, bf16[8,2048]{1,0:T(8,128)(2,1)S(1)}, u32[]{:S(2)}, u32[]{:S(2)}) collective-permute-start(bf16[8,2048]{1,0:T(8,128)(2,1)S(1)} %get-tuple-element.82), channel_id=1, source_target_pairs={{0,24},{1,25},{2,26},{3,27},{4,28},{5,29},{6,30},{7,31},{8,16},{9,... | collective-permute-start | bytes 98312 | tf_op jit(solution)/shard_map/ppermute | solution.py:315
  41.5 0.9 %collective-permute-start.18 = (bf16[8,2048]{1,0:T(8,128)(2,1)S(1)}, bf16[8,2048]{1,0:T(8,128)(2,1)S(1)}, u32[]{:S(2)}, u32[]{:S(2)}) collective-permute-start(bf16[8,2048]{1,0:T(8,128)(2,1)S(1)} %get-tuple-element.83), channel_id=1, source_target_pairs={{0,8},{1,9},{2,10},{3,11},{4,12},{5,13},{6,14},{7,15},{8,0},{9,1},... | collective-permute-start | bytes 98312 | tf_op jit(solution)/shard_map/ppermute | solution.py:315
  42.4 1.5 %collective-permute-start.19 = (bf16[8,2048]{1,0:T(8,128)(2,1)S(1)}, bf16[8,2048]{1,0:T(8,128)(2,1)S(1)}, u32[]{:S(2)}, u32[]{:S(2)}) collective-permute-start(bf16[8,2048]{1,0:T(8,128)(2,1)S(1)} %get-tuple-element.84), channel_id=1, source_target_pairs={{0,16},{1,17},{2,18},{3,19},{4,20},{5,21},{6,22},{7,23},{8,24},{9,... | collective-permute-start | bytes 98312 | tf_op jit(solution)/shard_map/ppermute | solution.py:315
  43.9 1.7 %collective-permute-done.17.refs_3_ = bf16[8,2048]{1,0:T(8,128)(2,1)S(1)} collective-permute-done((bf16[8,2048]{1,0:T(8,128)(2,1)S(1)}, bf16[8,2048]{1,0:T(8,128)(2,1)S(1)}, u32[]{:S(2)}, u32[]{:S(2)}) %collective-permute-start.17) | collective-permute-done | bytes 32800 | tf_op jit(solution)/shard_map/ppermute | solution.py:315
  45.5 1.0 %collective-permute-done.18.refs_4_ = bf16[8,2048]{1,0:T(8,128)(2,1)S(1)} collective-permute-done((bf16[8,2048]{1,0:T(8,128)(2,1)S(1)}, bf16[8,2048]{1,0:T(8,128)(2,1)S(1)}, u32[]{:S(2)}, u32[]{:S(2)}) %collective-permute-start.18) | collective-permute-done | bytes 32800 | tf_op jit(solution)/shard_map/ppermute | solution.py:315
  46.5 1.8 %shard_map.123 = (bf16[128,4096]{1,0:T(8,128)(2,1)}, bf16[128,4096]{1,0:T(8,128)(2,1)}) custom-call(bf16[128,16]{1,0:T(8,128)(2,1)S(1)} %get-tuple-element.48.refs_0_, bf16[128,16]{1,0:T(8,128)(2,1)S(1)} %get-tuple-element.49.refs_1_, f32[16,1]{1,0:T(8,128)S(1)} %get-tuple-element.50.refs_2_, bf16[8,2048]{1,0:T(8,128)(2,1)S(1)} %collective-permute-done.17.refs_3_, ...), custom_call_target="tpu_custom_call" | custom-call | tf_op jit(solution)/shard_map/pallas_call | solution.py:60
  (10 shorter events, 0.0 us)
Async XLA Ops:
  0.6 15.5 %copy-start.1 = (bf16[1,2048,256]{2,1,0:T(8,128)(2,1)S(1)}, bf16[1,2048,256]{2,1,0:T(8,128)(2,1)}, u32[]{:S(2)}) copy-start(bf16[1,2048,256]{2,1,0:T(8,128)(2,1)} %refs_5_.3) | copy-start | bytes 3145732
  2.6 13.6 %copy-start = (bf16[1,2048,256]{2,1,0:T(8,128)(2,1)S(1)}, bf16[1,2048,256]{2,1,0:T(8,128)(2,1)}, u32[]{:S(2)}) copy-start(bf16[1,2048,256]{2,1,0:T(8,128)(2,1)} %refs_4_.3) | copy-start | bytes 3145732
  2.6 7.3 %collective-permute-start = (bf16[8,2048]{1,0:T(8,128)(2,1)S(1)}, bf16[8,2048]{1,0:T(8,128)(2,1)S(1)}, u32[]{:S(2)}, u32[]{:S(2)}) collective-permute-start(bf16[8,2048]{1,0:T(8,128)(2,1)S(1)} %get-tuple-element.51), channel_id=1, source_target_pairs={{0,24},{1,25},{2,26},{3,27},{4,28},{5,29},{6,30},{7,31},{8,16},{9,... | collective-permute-start | bytes 98312 | tf_op jit(solution)/shard_map/ppermute | solution.py:315
  7.6 4.8 %collective-permute-start.1 = (bf16[8,2048]{1,0:T(8,128)(2,1)S(1)}, bf16[8,2048]{1,0:T(8,128)(2,1)S(1)}, u32[]{:S(2)}, u32[]{:S(2)}) collective-permute-start(bf16[8,2048]{1,0:T(8,128)(2,1)S(1)} %get-tuple-element.52), channel_id=1, source_target_pairs={{0,8},{1,9},{2,10},{3,11},{4,12},{5,13},{6,14},{7,15},{8,0},{9,1},... | collective-permute-start | bytes 98312 | tf_op jit(solution)/shard_map/ppermute | solution.py:315
  8.0 4.5 %collective-permute-start.2 = (bf16[8,2048]{1,0:T(8,128)(2,1)S(1)}, bf16[8,2048]{1,0:T(8,128)(2,1)S(1)}, u32[]{:S(2)}, u32[]{:S(2)}) collective-permute-start(bf16[8,2048]{1,0:T(8,128)(2,1)S(1)} %get-tuple-element.53), channel_id=1, source_target_pairs={{0,16},{1,17},{2,18},{3,19},{4,20},{5,21},{6,22},{7,23},{8,24},{9,... | collective-permute-start | bytes 98312 | tf_op jit(solution)/shard_map/ppermute | solution.py:315
  12.6 6.5 %collective-permute-start.3 = (bf16[32,2048]{1,0:T(8,128)(2,1)S(1)}, bf16[32,2048]{1,0:T(8,128)(2,1)S(1)}, u32[]{:S(2)}, u32[]{:S(2)}) collective-permute-start(bf16[32,2048]{1,0:T(8,128)(2,1)S(1)} %shard_map.112.refs_0_), channel_id=1, source_target_pairs={{0,6},{1,7},{2,4},{3,5},{4,2},{5,3},{6,0},{7,1},{8,14},{9,15},{10,... | collective-permute-start | bytes 393224 | tf_op jit(solution)/shard_map/ppermute | solution.py:315
  15.2 5.2 %collective-permute-start.10 = (bf16[32,2048]{1,0:T(8,128)(2,1)S(1)}, bf16[32,2048]{1,0:T(8,128)(2,1)S(1)}, u32[]{:S(2)}, u32[]{:S(2)}) collective-permute-start(bf16[32,2048]{1,0:T(8,128)(2,1)S(1)} %shard_map.112.refs_0_), channel_id=1, source_target_pairs={{0,4},{1,5},{2,6},{3,7},{4,0},{5,1},{6,2},{7,3},{8,12},{9,13},{10,... | collective-permute-start | bytes 393224 | tf_op jit(solution)/shard_map/ppermute | solution.py:315
  15.7 5.0 %collective-permute-start.9 = (bf16[32,2048]{1,0:T(8,128)(2,1)S(1)}, bf16[32,2048]{1,0:T(8,128)(2,1)S(1)}, u32[]{:S(2)}, u32[]{:S(2)}) collective-permute-start(bf16[32,2048]{1,0:T(8,128)(2,1)S(1)} %shard_map.112.refs_0_), channel_id=1, source_target_pairs={{0,2},{1,3},{2,0},{3,1},{4,6},{5,7},{6,4},{7,5},{8,10},{9,11},{10,... | collective-permute-start | bytes 393224 | tf_op jit(solution)/shard_map/ppermute | solution.py:315
  17.1 3.9 %collective-permute-start.4 = (bf16[32,2048]{1,0:T(8,128)(2,1)S(1)}, bf16[32,2048]{1,0:T(8,128)(2,1)S(1)}, u32[]{:S(2)}, u32[]{:S(2)}) collective-permute-start(bf16[32,2048]{1,0:T(8,128)(2,1)S(1)} %shard_map.112.refs_0_), channel_id=1, source_target_pairs={{0,1},{1,0},{2,3},{3,2},{4,5},{5,4},{6,7},{7,6},{8,9},{9,8},{10,11... | collective-permute-start | bytes 393224 | tf_op jit(solution)/shard_map/ppermute | solution.py:315
  19.1 1.9 %collective-permute-start.5 = (bf16[32,2048]{1,0:T(8,128)(2,1)S(1)}, bf16[32,2048]{1,0:T(8,128)(2,1)S(1)}, u32[]{:S(2)}, u32[]{:S(2)}) collective-permute-start(bf16[32,2048]{1,0:T(8,128)(2,1)S(1)} %shard_map.114.refs_1_), channel_id=1, source_target_pairs={{0,1},{1,0},{2,3},{3,2},{4,5},{5,4},{6,7},{7,6},{8,9},{9,8},{10,11... | collective-permute-start | bytes 393224 | tf_op jit(solution)/shard_map/ppermute | solution.py:315
  20.4 1.9 %collective-permute-start.12 = (bf16[32,2048]{1,0:T(8,128)(2,1)S(1)}, bf16[32,2048]{1,0:T(8,128)(2,1)S(1)}, u32[]{:S(2)}, u32[]{:S(2)}) collective-permute-start(bf16[32,2048]{1,0:T(8,128)(2,1)S(1)} %collective-permute-done.10.refs_1_.refs_5_), channel_id=1, source_target_pairs={{0,1},{1,0},{2,3},{3,2},{4,5},{5,4},{6,7},{7,6},{8,9},{9,8},{10,11... | collective-permute-start | bytes 393224 | tf_op jit(solution)/shard_map/ppermute | solution.py:315
  20.6 1.7 %collective-permute-start.11 = (bf16[32,2048]{1,0:T(8,128)(2,1)S(1)}, bf16[32,2048]{1,0:T(8,128)(2,1)S(1)}, u32[]{:S(2)}, u32[]{:S(2)}) collective-permute-start(bf16[32,2048]{1,0:T(8,128)(2,1)S(1)} %collective-permute-done.9.refs_0_.refs_4_), channel_id=1, source_target_pairs={{0,1},{1,0},{2,3},{3,2},{4,5},{5,4},{6,7},{7,6},{8,9},{9,8},{10,11... | collective-permute-start | bytes 393224 | tf_op jit(solution)/shard_map/ppermute | solution.py:315
  21.6 5.7 %collective-permute-start.6 = (bf16[64,768]{1,0:T(8,128)(2,1)S(1)}, bf16[64,768]{1,0:T(8,128)(2,1)S(1)}, u32[]{:S(2)}, u32[]{:S(2)}) collective-permute-start(bf16[64,768]{1,0:T(8,128)(2,1)S(1)} %get-tuple-element.59), channel_id=1, source_target_pairs={{0,16},{1,17},{2,18},{3,19},{4,20},{5,21},{6,22},{7,23},{8,24},{9,... | collective-permute-start | bytes 294920 | tf_op jit(solution)/shard_map/ppermute | solution.py:315
  23.0 5.7 %collective-permute-start.13 = (bf16[64,768]{1,0:T(8,128)(2,1)S(1)}, bf16[64,768]{1,0:T(8,128)(2,1)S(1)}, u32[]{:S(2)}, u32[]{:S(2)}) collective-permute-start(bf16[64,768]{1,0:T(8,128)(2,1)S(1)} %get-tuple-element.69), channel_id=1, source_target_pairs={{0,16},{1,17},{2,18},{3,19},{4,20},{5,21},{6,22},{7,23},{8,24},{9,... | collective-permute-start | bytes 294920 | tf_op jit(solution)/shard_map/ppermute | solution.py:315
  28.0 1.6 %collective-permute-start.7 = (bf16[64,2048]{1,0:T(8,128)(2,1)S(1)}, bf16[64,2048]{1,0:T(8,128)(2,1)S(1)}, u32[]{:S(2)}, u32[]{:S(2)}) collective-permute-start(bf16[64,2048]{1,0:T(8,128)(2,1)S(1)} %get-tuple-element.64), channel_id=1, source_target_pairs={{0,1},{1,0},{2,3},{3,2},{4,5},{5,4},{6,7},{7,6},{8,9},{9,8},{10,11... | collective-permute-start | bytes 786440 | tf_op jit(solution)/shard_map/ppermute | solution.py:315
  29.4 2.3 %collective-permute-start.14 = (bf16[64,2048]{1,0:T(8,128)(2,1)S(1)}, bf16[64,2048]{1,0:T(8,128)(2,1)S(1)}, u32[]{:S(2)}, u32[]{:S(2)}) collective-permute-start(bf16[64,2048]{1,0:T(8,128)(2,1)S(1)} %get-tuple-element.72), channel_id=1, source_target_pairs={{0,1},{1,0},{2,3},{3,2},{4,5},{5,4},{6,7},{7,6},{8,9},{9,8},{10,11... | collective-permute-start | bytes 786440 | tf_op jit(solution)/shard_map/ppermute | solution.py:315
  29.7 7.2 %collective-permute-start.8 = (bf16[32,2048]{1,0:T(8,128)(2,1)S(1)}, bf16[32,2048]{1,0:T(8,128)(2,1)S(1)}, u32[]{:S(2)}, u32[]{:S(2)}) collective-permute-start(bf16[32,2048]{1,0:T(8,128)(2,1)S(1)} %get-tuple-element.66), channel_id=1, source_target_pairs={{0,6},{1,7},{2,4},{3,5},{4,2},{5,3},{6,0},{7,1},{8,14},{9,15},{10,... | collective-permute-start | bytes 393224 | tf_op jit(solution)/shard_map/ppermute | solution.py:315
  31.8 7.4 %collective-permute-start.15 = (bf16[32,2048]{1,0:T(8,128)(2,1)S(1)}, bf16[32,2048]{1,0:T(8,128)(2,1)S(1)}, u32[]{:S(2)}, u32[]{:S(2)}) collective-permute-start(bf16[32,2048]{1,0:T(8,128)(2,1)S(1)} %get-tuple-element.73), channel_id=1, source_target_pairs={{0,2},{1,3},{2,0},{3,1},{4,6},{5,7},{6,4},{7,5},{8,10},{9,11},{10,... | collective-permute-start | bytes 393224 | tf_op jit(solution)/shard_map/ppermute | solution.py:315
  32.8 6.4 %collective-permute-start.16 = (bf16[32,2048]{1,0:T(8,128)(2,1)S(1)}, bf16[32,2048]{1,0:T(8,128)(2,1)S(1)}, u32[]{:S(2)}, u32[]{:S(2)}) collective-permute-start(bf16[32,2048]{1,0:T(8,128)(2,1)S(1)} %get-tuple-element.74), channel_id=1, source_target_pairs={{0,4},{1,5},{2,6},{3,7},{4,0},{5,1},{6,2},{7,3},{8,12},{9,13},{10,... | collective-permute-start | bytes 393224 | tf_op jit(solution)/shard_map/ppermute | solution.py:315
  39.4 6.1 %collective-permute-start.17 = (bf16[8,2048]{1,0:T(8,128)(2,1)S(1)}, bf16[8,2048]{1,0:T(8,128)(2,1)S(1)}, u32[]{:S(2)}, u32[]{:S(2)}) collective-permute-start(bf16[8,2048]{1,0:T(8,128)(2,1)S(1)} %get-tuple-element.82), channel_id=1, source_target_pairs={{0,24},{1,25},{2,26},{3,27},{4,28},{5,29},{6,30},{7,31},{8,16},{9,... | collective-permute-start | bytes 98312 | tf_op jit(solution)/shard_map/ppermute | solution.py:315
  41.5 5.1 %collective-permute-start.18 = (bf16[8,2048]{1,0:T(8,128)(2,1)S(1)}, bf16[8,2048]{1,0:T(8,128)(2,1)S(1)}, u32[]{:S(2)}, u32[]{:S(2)}) collective-permute-start(bf16[8,2048]{1,0:T(8,128)(2,1)S(1)} %get-tuple-element.83), channel_id=1, source_target_pairs={{0,8},{1,9},{2,10},{3,11},{4,12},{5,13},{6,14},{7,15},{8,0},{9,1},... | collective-permute-start | bytes 98312 | tf_op jit(solution)/shard_map/ppermute | solution.py:315
  42.4 4.2 %collective-permute-start.19 = (bf16[8,2048]{1,0:T(8,128)(2,1)S(1)}, bf16[8,2048]{1,0:T(8,128)(2,1)S(1)}, u32[]{:S(2)}, u32[]{:S(2)}) collective-permute-start(bf16[8,2048]{1,0:T(8,128)(2,1)S(1)} %get-tuple-element.84), channel_id=1, source_target_pairs={{0,16},{1,17},{2,18},{3,19},{4,20},{5,21},{6,22},{7,23},{8,24},{9,... | collective-permute-start | bytes 98312 | tf_op jit(solution)/shard_map/ppermute | solution.py:315

commit v5 on v4

--- a/solution.py
+++ b/solution.py
@@ -235,28 +235,34 @@
         out[...] = rows[m * each : (m + 1) * each]
 
 
-def home_body(n_dp, experts, order, put_out, put_grad, scale, *refs):
+def home_body(n_dp, experts, order, parts, put_out, put_grad, scale, *refs):
     msgs, outs, (layer_half, grad_half, wide, sems) = refs[:-6], refs[-6:-4], refs[-4:]
     msgs = dict(zip(order, msgs))
     batch = lax.axis_index("dp")
     each = msgs[0].shape[0]
     half = layer_half.shape[2]
+    step = half // parts
+    put_out, put_grad, scale = put_out[...], put_grad[...], scale[...]
+    put_both = jnp.concatenate([put_out, put_out], axis=1)
     copies = []
     for dx in range(n_dp):
         for k in range(experts):
             wide[k * each : (k + 1) * each, :] = msgs[dx * experts + k][...].astype(F32)
-        at = pl.ds(pl.multiple_of(lax.rem(batch + dx, n_dp) * half, 128), half)
-        value = wide[...] * scale[...]
-        high = value.astype(BF)
-        low = (value - high.astype(F32)).astype(BF)
-        grad_half[dx] = mm(put_grad[...], high).astype(BF)
-        copies.append(pltpu.make_async_copy(grad_half.at[dx], outs[1].at[:, at], sems.at[2 * dx]))
-        copies[-1].start()
-        layer_half[dx] = (mm(put_out[...], high) + mm(put_out[...], low)).astype(BF)
-        copies.append(
-            pltpu.make_async_copy(layer_half.at[dx], outs[0].at[:, at], sems.at[2 * dx + 1])
-        )
-        copies[-1].start()
+        first = lax.rem(batch + dx, n_dp) * half
+        for c in range(parts):
+            at = slice(c * step, (c + 1) * step)
+            value = wide[:, at] * scale
+            high = value.astype(BF)
+            low = (value - high.astype(F32)).astype(BF)
+            grad_half[dx, :, at] = mm(put_grad, high).astype(BF)
+            layer_half[dx, :, at] = mm(put_both, jnp.concatenate([high, low], axis=0)).astype(BF)
+            to = pl.ds(pl.multiple_of(first + c * step, 128), step)
+            for src, dst in ((grad_half, outs[1]), (layer_half, outs[0])):
+                copy = pltpu.make_async_copy(
+                    src.at[dx, :, pl.ds(c * step, step)], dst.at[:, to], sems.at[len(copies)]
+                )
+                copy.start()
+                copies.append(copy)
     for copy in copies:
         copy.wait()
 
@@ -418,13 +424,14 @@
     got = {kinds[m]: msg for m, msg in zip(order, msgs)}
     for kind in kinds[1:]:
         got[kind] = send(got[kind], home_perm(*kind, -1))
+    parts = 2
     layer_out, token_grad = call(
-        functools.partial(home_body, n_dp, experts, order),
+        functools.partial(home_body, n_dp, experts, order, parts),
         [sds((block, width), BF)] * 2,
         (put_out, put_grad, scale, *[got[kinds[m]] for m in order]),
         out_specs=[HBM] * 2,
         scratch=[pltpu.VMEM((n_dp, block, half), BF)] * 2
-        + [pltpu.VMEM((count, half), F32), pltpu.SemaphoreType.DMA((2 * n_dp,))],
+        + [pltpu.VMEM((count, half), F32), pltpu.SemaphoreType.DMA((2 * n_dp * parts,))],
         extra=block * half * 16 + count * half * 4,
     )
     return layer_out, token_grad, *grads

time: 48.5 us -> 48.3 us (level)
  no operation moved by 1% of the time
where the time goes in v5:
time: 48.3 us; the launch traced here: 48.2 us
  starting transfers between devices  20.5 us (42%)
  waiting for transfers between devices  15.7 us (33%)
  Pallas kernels  11.3 us (23%)
  between operations  0.78 us (2%)
    ppermute x20, starting transfers between devices, send(): return lax.ppermute(x, AXES, perm)  20.5 us
    ppermute x20, waiting for transfers between devices, send(): return lax.ppermute(x, AXES, perm)  15.7 us
    pallas_call x14, Pallas kernels, call(): pl.pallas_call(whole, out_shape=[*out_shape, *[jax.ShapeDtypeStruct((8, 1...  11.3 us
  transfers between devices with their start and end apart: 20, of which 12 were waited for; matrix products, arithmetic and copies ran while one was open for 0% of the time, Pallas kernels for 15%

profile of v5, /device:TPU:0, one launch (start us, length us, event | category | flops | bytes accessed | tf_op | source)
XLA Modules:
  0.0 48.2 jit_solution(18045922922386737650)
XLA Ops:
  0.6 1.9 %shard_map.111 = (bf16[8,2048]{1,0:T(8,128)(2,1)S(1)}, bf16[8,2048]{1,0:T(8,128)(2,1)S(1)}, bf16[8,2048]{1,0:T(8,128)(2,1)S(1)}, bf16[8,2048]{1,0:T(8,128)(2,1)S(1)}) custom-call(s32[2,4]{1,0:T(2,128)} %bitcast.2, f32[2,4]{1,0:T(2,128)} %bitcast.4, bf16[128,4096]{1,0:T(8,128)(2,1)} %refs_2_.1, bf16[128,4096]{1,0:T(8,128)(2,1)} %refs_3_.1), custom_call_target="tpu_custom_call" | custom-call | tf_op jit(solution)/shard_map/pallas_call | solution.py:60
  2.6 0.0 copy-start
  2.6 5.0 %collective-permute-start = (bf16[8,2048]{1,0:T(8,128)(2,1)S(1)}, bf16[8,2048]{1,0:T(8,128)(2,1)S(1)}, u32[]{:S(2)}, u32[]{:S(2)}) collective-permute-start(bf16[8,2048]{1,0:T(8,128)(2,1)S(1)} %get-tuple-element.51), channel_id=1, source_target_pairs={{0,24},{1,25},{2,26},{3,27},{4,28},{5,29},{6,30},{7,31},{8,16},{9,... | collective-permute-start | bytes 98312 | tf_op jit(solution)/shard_map/ppermute | solution.py:321
  7.6 0.3 collective-permute-start.1
  8.0 0.3 collective-permute-start.2
  8.3 1.3 %shard_map.110 = (bf16[1,2048,256]{2,1,0:T(8,128)(2,1)S(1)}, bf16[128,16]{1,0:T(8,128)(2,1)S(1)}, bf16[128,16]{1,0:T(8,128)(2,1)S(1)}, f32[16,1]{1,0:T(8,128)S(1)}, f32[8,128]{1,0:T(8,128)S(1)}) custom-call(bf16[1,2048,256]{2,1,0:T(8,128)(2,1)} %refs_0_.2, s32[2,4]{1,0:T(2,128)} %bitcast.3, f32[2,4]{1,0:T(2,128)} %bitcast.5), custom_call_target="tpu_custom_call" | custom-call | tf_op jit(solution)/shard_map/pallas_call | solution.py:60
  9.5 0.3 collective-permute-done.refs_0_
  9.9 2.6 %collective-permute-done.1.refs_1_ = bf16[8,2048]{1,0:T(8,128)(2,1)S(1)} collective-permute-done((bf16[8,2048]{1,0:T(8,128)(2,1)S(1)}, bf16[8,2048]{1,0:T(8,128)(2,1)S(1)}, u32[]{:S(2)}, u32[]{:S(2)}) %collective-permute-start.1) | collective-permute-done | bytes 32800 | tf_op jit(solution)/shard_map/ppermute | solution.py:321
  12.4 0.0 collective-permute-done.2.refs_2_
  12.4 0.2 shard_map.112.refs_0_
  12.6 2.6 %collective-permute-start.3 = (bf16[32,2048]{1,0:T(8,128)(2,1)S(1)}, bf16[32,2048]{1,0:T(8,128)(2,1)S(1)}, u32[]{:S(2)}, u32[]{:S(2)}) collective-permute-start(bf16[32,2048]{1,0:T(8,128)(2,1)S(1)} %shard_map.112.refs_0_), channel_id=1, source_target_pairs={{0,6},{1,7},{2,4},{3,5},{4,2},{5,3},{6,0},{7,1},{8,14},{9,15},{10,... | collective-permute-start | bytes 393224 | tf_op jit(solution)/shard_map/ppermute | solution.py:321
  15.2 0.4 collective-permute-start.10
  15.7 0.5 %collective-permute-start.9 = (bf16[32,2048]{1,0:T(8,128)(2,1)S(1)}, bf16[32,2048]{1,0:T(8,128)(2,1)S(1)}, u32[]{:S(2)}, u32[]{:S(2)}) collective-permute-start(bf16[32,2048]{1,0:T(8,128)(2,1)S(1)} %shard_map.112.refs_0_), channel_id=1, source_target_pairs={{0,2},{1,3},{2,0},{3,1},{4,6},{5,7},{6,4},{7,5},{8,10},{9,11},{10,... | collective-permute-start | bytes 393224 | tf_op jit(solution)/shard_map/ppermute | solution.py:321
  16.2 0.9 %shard_map.113 = (bf16[256,2048]{1,0:T(8,128)(2,1)S(1)}, bf16[256,2048]{1,0:T(8,128)(2,1)S(1)}, bf16[256,2048]{1,0:T(8,128)(2,1)S(1)}, f32[8,128]{1,0:T(8,128)S(1)}) custom-call(bf16[1,2048,256]{2,1,0:T(8,128)(2,1)S(1)} %copy-done, bf16[1,2048,256]{2,1,0:T(8,128)(2,1)S(1)} %copy-done.1, bf16[1,2048,256]{2,1,0:T(8,128)(2,1)S(1)} %get-tuple-element.56.refs_2_.refs_6_), custom_call_target="tpu_custom_call" | custom-call | tf_op jit(solution)/shard_map/pallas_call | solution.py:60
  17.1 0.1 collective-permute-start.4
  17.2 1.9 %collective-permute-done.3.refs_0_ = bf16[32,2048]{1,0:T(8,128)(2,1)S(1)} collective-permute-done((bf16[32,2048]{1,0:T(8,128)(2,1)S(1)}, bf16[32,2048]{1,0:T(8,128)(2,1)S(1)}, u32[]{:S(2)}, u32[]{:S(2)}) %collective-permute-start.3) | collective-permute-done | bytes 131104 | tf_op jit(solution)/shard_map/ppermute | solution.py:321
  19.1 0.1 collective-permute-start.5
  19.2 1.3 %collective-permute-done.10.refs_1_.refs_5_ = bf16[32,2048]{1,0:T(8,128)(2,1)S(1)} collective-permute-done((bf16[32,2048]{1,0:T(8,128)(2,1)S(1)}, bf16[32,2048]{1,0:T(8,128)(2,1)S(1)}, u32[]{:S(2)}, u32[]{:S(2)}) %collective-permute-start.10) | collective-permute-done | bytes 131104 | tf_op jit(solution)/shard_map/ppermute | solution.py:321
  20.4 0.0 collective-permute-start.12
  20.4 0.2 collective-permute-done.9.refs_0_.refs_4_
  20.6 0.3 collective-permute-start.11
  21.0 0.0 collective-permute-done.4.refs_2_
  21.0 0.7 %shard_map.115 = (f32[64,768]{1,0:T(8,128)S(1)}, bf16[64,768]{1,0:T(8,128)(2,1)S(1)}, f32[8,128]{1,0:T(8,128)S(1)}) custom-call(bf16[32,2048]{1,0:T(8,128)(2,1)S(1)} %shard_map.112.refs_0_, bf16[32,2048]{1,0:T(8,128)(2,1)S(1)} %shard_map.114.refs_1_, bf16[32,2048]{1,0:T(8,128)(2,1)S(1)} %collective-permute-done.4.refs_2_, ...), custom_call_target="tpu_custom_call" | custom-call | tf_op jit(solution)/shard_map/pallas_call | solution.py:60
  21.6 0.7 %collective-permute-start.6 = (bf16[64,768]{1,0:T(8,128)(2,1)S(1)}, bf16[64,768]{1,0:T(8,128)(2,1)S(1)}, u32[]{:S(2)}, u32[]{:S(2)}) collective-permute-start(bf16[64,768]{1,0:T(8,128)(2,1)S(1)} %get-tuple-element.59), channel_id=1, source_target_pairs={{0,16},{1,17},{2,18},{3,19},{4,20},{5,21},{6,22},{7,23},{8,24},{9,... | collective-permute-start | bytes 294920 | tf_op jit(solution)/shard_map/ppermute | solution.py:321
  22.3 0.7 %shard_map.118 = (f32[64,768]{1,0:T(8,128)S(1)}, bf16[64,768]{1,0:T(8,128)(2,1)S(1)}) custom-call(bf16[32,2048]{1,0:T(8,128)(2,1)S(1)} %collective-permute-done.9.refs_0_.refs_4_, bf16[32,2048]{1,0:T(8,128)(2,1)S(1)} %collective-permute-done.10.refs_1_.refs_5_, bf16[32,2048]{1,0:T(8,128)(2,1)S(1)} %collective-permute-done.11.refs_2_.refs_6_, ...), custom_call_target="tpu_custom_call" | custom-call | tf_op jit(solution)/shard_map/pallas_call | solution.py:60
  23.0 1.5 %collective-permute-start.13 = (bf16[64,768]{1,0:T(8,128)(2,1)S(1)}, bf16[64,768]{1,0:T(8,128)(2,1)S(1)}, u32[]{:S(2)}, u32[]{:S(2)}) collective-permute-start(bf16[64,768]{1,0:T(8,128)(2,1)S(1)} %get-tuple-element.69), channel_id=1, source_target_pairs={{0,16},{1,17},{2,18},{3,19},{4,20},{5,21},{6,22},{7,23},{8,24},{9,... | collective-permute-start | bytes 294920 | tf_op jit(solution)/shard_map/ppermute | solution.py:321
  24.5 2.9 %collective-permute-done.6.refs_1_ = bf16[64,768]{1,0:T(8,128)(2,1)S(1)} collective-permute-done((bf16[64,768]{1,0:T(8,128)(2,1)S(1)}, bf16[64,768]{1,0:T(8,128)(2,1)S(1)}, u32[]{:S(2)}, u32[]{:S(2)}) %collective-permute-start.6) | collective-permute-done | bytes 98336 | tf_op jit(solution)/shard_map/ppermute | solution.py:321
  27.3 0.7 %shard_map.116 = (bf16[64,256]{1,0:T(8,128)(2,1)S(1)}, bf16[64,256]{1,0:T(8,128)(2,1)S(1)}, bf16[64,256]{1,0:T(8,128)(2,1)S(1)}, bf16[64,2048]{1,0:T(8,128)(2,1)...) custom-call(f32[64,768]{1,0:T(8,128)S(1)} %get-tuple-element.58.refs_0_, ...), custom_call_target="tpu_custom_call" | custom-call | tf_op jit(solution)/shard_map/pallas_call | solution.py:60
  28.0 0.1 collective-permute-start.7
  28.1 0.6 %collective-permute-done.13.refs_1_ = bf16[64,768]{1,0:T(8,128)(2,1)S(1)} collective-permute-done((bf16[64,768]{1,0:T(8,128)(2,1)S(1)}, bf16[64,768]{1,0:T(8,128)(2,1)S(1)}, u32[]{:S(2)}, u32[]{:S(2)}) %collective-permute-start.13) | collective-permute-done | bytes 98336 | tf_op jit(solution)/shard_map/ppermute | solution.py:321
  28.7 0.7 %shard_map.119 = (bf16[64,256]{1,0:T(8,128)(2,1)S(1)}, bf16[64,256]{1,0:T(8,128)(2,1)S(1)}, bf16[64,256]{1,0:T(8,128)(2,1)S(1)}, bf16[64,2048]{1,0:T(8,128)(2,1)S(1)}, bf16[64,2048]{1,0:T(8,128)(2,1)S(1)}) custom-call(f32[64,768]{1,0:T(8,128)S(1)} %get-tuple-element.68.refs_0_, bf16[64,768]{1,0:T(8,128)(2,1)S(1)} %collective-permute-done.13.refs_1_, ...), custom_call_target="tpu_custom_call" | custom-call | tf_op jit(solution)/shard_map/pallas_call | solution.py:60
  29.4 0.1 collective-permute-start.14
  29.4 0.2 collective-permute-done.7.refs_1_
  29.6 0.1 shard_map.117
  29.7 2.0 %collective-permute-start.8 = (bf16[32,2048]{1,0:T(8,128)(2,1)S(1)}, bf16[32,2048]{1,0:T(8,128)(2,1)S(1)}, u32[]{:S(2)}, u32[]{:S(2)}) collective-permute-start(bf16[32,2048]{1,0:T(8,128)(2,1)S(1)} %get-tuple-element.66), channel_id=1, source_target_pairs={{0,6},{1,7},{2,4},{3,5},{4,2},{5,3},{6,0},{7,1},{8,14},{9,15},{10,... | collective-permute-start | bytes 393224 | tf_op jit(solution)/shard_map/ppermute | solution.py:321
  31.7 0.1 shard_map.120
  31.8 1.0 %collective-permute-start.15 = (bf16[32,2048]{1,0:T(8,128)(2,1)S(1)}, bf16[32,2048]{1,0:T(8,128)(2,1)S(1)}, u32[]{:S(2)}, u32[]{:S(2)}) collective-permute-start(bf16[32,2048]{1,0:T(8,128)(2,1)S(1)} %get-tuple-element.73), channel_id=1, source_target_pairs={{0,2},{1,3},{2,0},{3,1},{4,6},{5,7},{6,4},{7,5},{8,10},{9,11},{10,... | collective-permute-start | bytes 393224 | tf_op jit(solution)/shard_map/ppermute | solution.py:321
  32.8 1.0 %collective-permute-start.16 = (bf16[32,2048]{1,0:T(8,128)(2,1)S(1)}, bf16[32,2048]{1,0:T(8,128)(2,1)S(1)}, u32[]{:S(2)}, u32[]{:S(2)}) collective-permute-start(bf16[32,2048]{1,0:T(8,128)(2,1)S(1)} %get-tuple-element.74), channel_id=1, source_target_pairs={{0,4},{1,5},{2,6},{3,7},{4,0},{5,1},{6,2},{7,3},{8,12},{9,13},{10,... | collective-permute-start | bytes 393224 | tf_op jit(solution)/shard_map/ppermute | solution.py:321
  33.8 2.4 %shard_map.121 = (bf16[1,2048,256]{2,1,0:T(8,128)(2,1)}, bf16[1,2048,256]{2,1,0:T(8,128)(2,1)}, bf16[1,2048,256]{2,1,0:T(8,128)(2,1)}, f32[8,128]{1,0:T(8,128)S(1)}) custom-call(bf16[32,2048]{1,0:T(8,128)(2,1)S(1)} %shard_map.112.refs_0_, bf16[32,2048]{1,0:T(8,128)(2,1)S(1)} %shard_map.114.refs_1_, bf16[32,2048]{1,0:T(8,128)(2,1)S(1)} %collective-permute-done.4.refs_2_, ...), custom_call_target="tpu_custom_call" | custom-call | flops 402653184 | bytes 3145728 | tf_op jit(solution)/shard_map/pallas_call | solution.py:60
  36.1 0.8 %collective-permute-done.8.refs_1_ = bf16[32,2048]{1,0:T(8,128)(2,1)S(1)} collective-permute-done((bf16[32,2048]{1,0:T(8,128)(2,1)S(1)}, bf16[32,2048]{1,0:T(8,128)(2,1)S(1)}, u32[]{:S(2)}, u32[]{:S(2)}) %collective-permute-start.8) | collective-permute-done | bytes 131104 | tf_op jit(solution)/shard_map/ppermute | solution.py:321
  36.9 2.3 %collective-permute-done.15.refs_2_ = bf16[32,2048]{1,0:T(8,128)(2,1)S(1)} collective-permute-done((bf16[32,2048]{1,0:T(8,128)(2,1)S(1)}, bf16[32,2048]{1,0:T(8,128)(2,1)S(1)}, u32[]{:S(2)}, u32[]{:S(2)}) %collective-permute-start.15) | collective-permute-done | bytes 131104 | tf_op jit(solution)/shard_map/ppermute | solution.py:321
  39.2 0.2 shard_map.122
  39.4 2.1 %collective-permute-start.17 = (bf16[8,2048]{1,0:T(8,128)(2,1)S(1)}, bf16[8,2048]{1,0:T(8,128)(2,1)S(1)}, u32[]{:S(2)}, u32[]{:S(2)}) collective-permute-start(bf16[8,2048]{1,0:T(8,128)(2,1)S(1)} %get-tuple-element.82), channel_id=1, source_target_pairs={{0,24},{1,25},{2,26},{3,27},{4,28},{5,29},{6,30},{7,31},{8,16},{9,... | collective-permute-start | bytes 98312 | tf_op jit(solution)/shard_map/ppermute | solution.py:321
  41.5 0.9 %collective-permute-start.18 = (bf16[8,2048]{1,0:T(8,128)(2,1)S(1)}, bf16[8,2048]{1,0:T(8,128)(2,1)S(1)}, u32[]{:S(2)}, u32[]{:S(2)}) collective-permute-start(bf16[8,2048]{1,0:T(8,128)(2,1)S(1)} %get-tuple-element.83), channel_id=1, source_target_pairs={{0,8},{1,9},{2,10},{3,11},{4,12},{5,13},{6,14},{7,15},{8,0},{9,1},... | collective-permute-start | bytes 98312 | tf_op jit(solution)/shard_map/ppermute | solution.py:321
  42.4 1.5 %collective-permute-start.19 = (bf16[8,2048]{1,0:T(8,128)(2,1)S(1)}, bf16[8,2048]{1,0:T(8,128)(2,1)S(1)}, u32[]{:S(2)}, u32[]{:S(2)}) collective-permute-start(bf16[8,2048]{1,0:T(8,128)(2,1)S(1)} %get-tuple-element.84), channel_id=1, source_target_pairs={{0,16},{1,17},{2,18},{3,19},{4,20},{5,21},{6,22},{7,23},{8,24},{9,... | collective-permute-start | bytes 98312 | tf_op jit(solution)/shard_map/ppermute | solution.py:321
  43.9 1.7 %collective-permute-done.17.refs_3_ = bf16[8,2048]{1,0:T(8,128)(2,1)S(1)} collective-permute-done((bf16[8,2048]{1,0:T(8,128)(2,1)S(1)}, bf16[8,2048]{1,0:T(8,128)(2,1)S(1)}, u32[]{:S(2)}, u32[]{:S(2)}) %collective-permute-start.17) | collective-permute-done | bytes 32800 | tf_op jit(solution)/shard_map/ppermute | solution.py:321
  45.5 1.0 %collective-permute-done.18.refs_4_ = bf16[8,2048]{1,0:T(8,128)(2,1)S(1)} collective-permute-done((bf16[8,2048]{1,0:T(8,128)(2,1)S(1)}, bf16[8,2048]{1,0:T(8,128)(2,1)S(1)}, u32[]{:S(2)}, u32[]{:S(2)}) %collective-permute-start.18) | collective-permute-done | bytes 32800 | tf_op jit(solution)/shard_map/ppermute | solution.py:321
  46.5 1.7 %shard_map.123 = (bf16[128,4096]{1,0:T(8,128)(2,1)}, bf16[128,4096]{1,0:T(8,128)(2,1)}) custom-call(bf16[128,16]{1,0:T(8,128)(2,1)S(1)} %get-tuple-element.48.refs_0_, bf16[128,16]{1,0:T(8,128)(2,1)S(1)} %get-tuple-element.49.refs_1_, f32[16,1]{1,0:T(8,128)S(1)} %get-tuple-element.50.refs_2_, bf16[8,2048]{1,0:T(8,128)(2,1)S(1)} %collective-permute-done.17.refs_3_, ...), custom_call_target="tpu_custom_call" | custom-call | tf_op jit(solution)/shard_map/pallas_call | solution.py:60
  (10 shorter events, 0.0 us)
Async XLA Ops:
  0.6 15.5 %copy-start.1 = (bf16[1,2048,256]{2,1,0:T(8,128)(2,1)S(1)}, bf16[1,2048,256]{2,1,0:T(8,128)(2,1)}, u32[]{:S(2)}) copy-start(bf16[1,2048,256]{2,1,0:T(8,128)(2,1)} %refs_5_.3) | copy-start | bytes 3145732
  2.6 13.6 %copy-start = (bf16[1,2048,256]{2,1,0:T(8,128)(2,1)S(1)}, bf16[1,2048,256]{2,1,0:T(8,128)(2,1)}, u32[]{:S(2)}) copy-start(bf16[1,2048,256]{2,1,0:T(8,128)(2,1)} %refs_4_.3) | copy-start | bytes 3145732
  2.6 7.3 %collective-permute-start = (bf16[8,2048]{1,0:T(8,128)(2,1)S(1)}, bf16[8,2048]{1,0:T(8,128)(2,1)S(1)}, u32[]{:S(2)}, u32[]{:S(2)}) collective-permute-start(bf16[8,2048]{1,0:T(8,128)(2,1)S(1)} %get-tuple-element.51), channel_id=1, source_target_pairs={{0,24},{1,25},{2,26},{3,27},{4,28},{5,29},{6,30},{7,31},{8,16},{9,... | collective-permute-start | bytes 98312 | tf_op jit(solution)/shard_map/ppermute | solution.py:321
  7.6 4.8 %collective-permute-start.1 = (bf16[8,2048]{1,0:T(8,128)(2,1)S(1)}, bf16[8,2048]{1,0:T(8,128)(2,1)S(1)}, u32[]{:S(2)}, u32[]{:S(2)}) collective-permute-start(bf16[8,2048]{1,0:T(8,128)(2,1)S(1)} %get-tuple-element.52), channel_id=1, source_target_pairs={{0,8},{1,9},{2,10},{3,11},{4,12},{5,13},{6,14},{7,15},{8,0},{9,1},... | collective-permute-start | bytes 98312 | tf_op jit(solution)/shard_map/ppermute | solution.py:321
  8.0 4.5 %collective-permute-start.2 = (bf16[8,2048]{1,0:T(8,128)(2,1)S(1)}, bf16[8,2048]{1,0:T(8,128)(2,1)S(1)}, u32[]{:S(2)}, u32[]{:S(2)}) collective-permute-start(bf16[8,2048]{1,0:T(8,128)(2,1)S(1)} %get-tuple-element.53), channel_id=1, source_target_pairs={{0,16},{1,17},{2,18},{3,19},{4,20},{5,21},{6,22},{7,23},{8,24},{9,... | collective-permute-start | bytes 98312 | tf_op jit(solution)/shard_map/ppermute | solution.py:321
  12.6 6.5 %collective-permute-start.3 = (bf16[32,2048]{1,0:T(8,128)(2,1)S(1)}, bf16[32,2048]{1,0:T(8,128)(2,1)S(1)}, u32[]{:S(2)}, u32[]{:S(2)}) collective-permute-start(bf16[32,2048]{1,0:T(8,128)(2,1)S(1)} %shard_map.112.refs_0_), channel_id=1, source_target_pairs={{0,6},{1,7},{2,4},{3,5},{4,2},{5,3},{6,0},{7,1},{8,14},{9,15},{10,... | collective-permute-start | bytes 393224 | tf_op jit(solution)/shard_map/ppermute | solution.py:321
  15.2 5.2 %collective-permute-start.10 = (bf16[32,2048]{1,0:T(8,128)(2,1)S(1)}, bf16[32,2048]{1,0:T(8,128)(2,1)S(1)}, u32[]{:S(2)}, u32[]{:S(2)}) collective-permute-start(bf16[32,2048]{1,0:T(8,128)(2,1)S(1)} %shard_map.112.refs_0_), channel_id=1, source_target_pairs={{0,4},{1,5},{2,6},{3,7},{4,0},{5,1},{6,2},{7,3},{8,12},{9,13},{10,... | collective-permute-start | bytes 393224 | tf_op jit(solution)/shard_map/ppermute | solution.py:321
  15.7 5.0 %collective-permute-start.9 = (bf16[32,2048]{1,0:T(8,128)(2,1)S(1)}, bf16[32,2048]{1,0:T(8,128)(2,1)S(1)}, u32[]{:S(2)}, u32[]{:S(2)}) collective-permute-start(bf16[32,2048]{1,0:T(8,128)(2,1)S(1)} %shard_map.112.refs_0_), channel_id=1, source_target_pairs={{0,2},{1,3},{2,0},{3,1},{4,6},{5,7},{6,4},{7,5},{8,10},{9,11},{10,... | collective-permute-start | bytes 393224 | tf_op jit(solution)/shard_map/ppermute | solution.py:321
  17.1 3.9 %collective-permute-start.4 = (bf16[32,2048]{1,0:T(8,128)(2,1)S(1)}, bf16[32,2048]{1,0:T(8,128)(2,1)S(1)}, u32[]{:S(2)}, u32[]{:S(2)}) collective-permute-start(bf16[32,2048]{1,0:T(8,128)(2,1)S(1)} %shard_map.112.refs_0_), channel_id=1, source_target_pairs={{0,1},{1,0},{2,3},{3,2},{4,5},{5,4},{6,7},{7,6},{8,9},{9,8},{10,11... | collective-permute-start | bytes 393224 | tf_op jit(solution)/shard_map/ppermute | solution.py:321
  19.1 1.9 %collective-permute-start.5 = (bf16[32,2048]{1,0:T(8,128)(2,1)S(1)}, bf16[32,2048]{1,0:T(8,128)(2,1)S(1)}, u32[]{:S(2)}, u32[]{:S(2)}) collective-permute-start(bf16[32,2048]{1,0:T(8,128)(2,1)S(1)} %shard_map.114.refs_1_), channel_id=1, source_target_pairs={{0,1},{1,0},{2,3},{3,2},{4,5},{5,4},{6,7},{7,6},{8,9},{9,8},{10,11... | collective-permute-start | bytes 393224 | tf_op jit(solution)/shard_map/ppermute | solution.py:321
  20.4 1.9 %collective-permute-start.12 = (bf16[32,2048]{1,0:T(8,128)(2,1)S(1)}, bf16[32,2048]{1,0:T(8,128)(2,1)S(1)}, u32[]{:S(2)}, u32[]{:S(2)}) collective-permute-start(bf16[32,2048]{1,0:T(8,128)(2,1)S(1)} %collective-permute-done.10.refs_1_.refs_5_), channel_id=1, source_target_pairs={{0,1},{1,0},{2,3},{3,2},{4,5},{5,4},{6,7},{7,6},{8,9},{9,8},{10,11... | collective-permute-start | bytes 393224 | tf_op jit(solution)/shard_map/ppermute | solution.py:321
  20.6 1.7 %collective-permute-start.11 = (bf16[32,2048]{1,0:T(8,128)(2,1)S(1)}, bf16[32,2048]{1,0:T(8,128)(2,1)S(1)}, u32[]{:S(2)}, u32[]{:S(2)}) collective-permute-start(bf16[32,2048]{1,0:T(8,128)(2,1)S(1)} %collective-permute-done.9.refs_0_.refs_4_), channel_id=1, source_target_pairs={{0,1},{1,0},{2,3},{3,2},{4,5},{5,4},{6,7},{7,6},{8,9},{9,8},{10,11... | collective-permute-start | bytes 393224 | tf_op jit(solution)/shard_map/ppermute | solution.py:321
  21.6 5.7 %collective-permute-start.6 = (bf16[64,768]{1,0:T(8,128)(2,1)S(1)}, bf16[64,768]{1,0:T(8,128)(2,1)S(1)}, u32[]{:S(2)}, u32[]{:S(2)}) collective-permute-start(bf16[64,768]{1,0:T(8,128)(2,1)S(1)} %get-tuple-element.59), channel_id=1, source_target_pairs={{0,16},{1,17},{2,18},{3,19},{4,20},{5,21},{6,22},{7,23},{8,24},{9,... | collective-permute-start | bytes 294920 | tf_op jit(solution)/shard_map/ppermute | solution.py:321
  23.0 5.7 %collective-permute-start.13 = (bf16[64,768]{1,0:T(8,128)(2,1)S(1)}, bf16[64,768]{1,0:T(8,128)(2,1)S(1)}, u32[]{:S(2)}, u32[]{:S(2)}) collective-permute-start(bf16[64,768]{1,0:T(8,128)(2,1)S(1)} %get-tuple-element.69), channel_id=1, source_target_pairs={{0,16},{1,17},{2,18},{3,19},{4,20},{5,21},{6,22},{7,23},{8,24},{9,... | collective-permute-start | bytes 294920 | tf_op jit(solution)/shard_map/ppermute | solution.py:321
  28.0 1.6 %collective-permute-start.7 = (bf16[64,2048]{1,0:T(8,128)(2,1)S(1)}, bf16[64,2048]{1,0:T(8,128)(2,1)S(1)}, u32[]{:S(2)}, u32[]{:S(2)}) collective-permute-start(bf16[64,2048]{1,0:T(8,128)(2,1)S(1)} %get-tuple-element.64), channel_id=1, source_target_pairs={{0,1},{1,0},{2,3},{3,2},{4,5},{5,4},{6,7},{7,6},{8,9},{9,8},{10,11... | collective-permute-start | bytes 786440 | tf_op jit(solution)/shard_map/ppermute | solution.py:321
  29.4 2.3 %collective-permute-start.14 = (bf16[64,2048]{1,0:T(8,128)(2,1)S(1)}, bf16[64,2048]{1,0:T(8,128)(2,1)S(1)}, u32[]{:S(2)}, u32[]{:S(2)}) collective-permute-start(bf16[64,2048]{1,0:T(8,128)(2,1)S(1)} %get-tuple-element.72), channel_id=1, source_target_pairs={{0,1},{1,0},{2,3},{3,2},{4,5},{5,4},{6,7},{7,6},{8,9},{9,8},{10,11... | collective-permute-start | bytes 786440 | tf_op jit(solution)/shard_map/ppermute | solution.py:321
  29.7 7.2 %collective-permute-start.8 = (bf16[32,2048]{1,0:T(8,128)(2,1)S(1)}, bf16[32,2048]{1,0:T(8,128)(2,1)S(1)}, u32[]{:S(2)}, u32[]{:S(2)}) collective-permute-start(bf16[32,2048]{1,0:T(8,128)(2,1)S(1)} %get-tuple-element.66), channel_id=1, source_target_pairs={{0,6},{1,7},{2,4},{3,5},{4,2},{5,3},{6,0},{7,1},{8,14},{9,15},{10,... | collective-permute-start | bytes 393224 | tf_op jit(solution)/shard_map/ppermute | solution.py:321
  31.8 7.4 %collective-permute-start.15 = (bf16[32,2048]{1,0:T(8,128)(2,1)S(1)}, bf16[32,2048]{1,0:T(8,128)(2,1)S(1)}, u32[]{:S(2)}, u32[]{:S(2)}) collective-permute-start(bf16[32,2048]{1,0:T(8,128)(2,1)S(1)} %get-tuple-element.73), channel_id=1, source_target_pairs={{0,2},{1,3},{2,0},{3,1},{4,6},{5,7},{6,4},{7,5},{8,10},{9,11},{10,... | collective-permute-start | bytes 393224 | tf_op jit(solution)/shard_map/ppermute | solution.py:321
  32.8 6.4 %collective-permute-start.16 = (bf16[32,2048]{1,0:T(8,128)(2,1)S(1)}, bf16[32,2048]{1,0:T(8,128)(2,1)S(1)}, u32[]{:S(2)}, u32[]{:S(2)}) collective-permute-start(bf16[32,2048]{1,0:T(8,128)(2,1)S(1)} %get-tuple-element.74), channel_id=1, source_target_pairs={{0,4},{1,5},{2,6},{3,7},{4,0},{5,1},{6,2},{7,3},{8,12},{9,13},{10,... | collective-permute-start | bytes 393224 | tf_op jit(solution)/shard_map/ppermute | solution.py:321
  39.4 6.1 %collective-permute-start.17 = (bf16[8,2048]{1,0:T(8,128)(2,1)S(1)}, bf16[8,2048]{1,0:T(8,128)(2,1)S(1)}, u32[]{:S(2)}, u32[]{:S(2)}) collective-permute-start(bf16[8,2048]{1,0:T(8,128)(2,1)S(1)} %get-tuple-element.82), channel_id=1, source_target_pairs={{0,24},{1,25},{2,26},{3,27},{4,28},{5,29},{6,30},{7,31},{8,16},{9,... | collective-permute-start | bytes 98312 | tf_op jit(solution)/shard_map/ppermute | solution.py:321
  41.5 5.1 %collective-permute-start.18 = (bf16[8,2048]{1,0:T(8,128)(2,1)S(1)}, bf16[8,2048]{1,0:T(8,128)(2,1)S(1)}, u32[]{:S(2)}, u32[]{:S(2)}) collective-permute-start(bf16[8,2048]{1,0:T(8,128)(2,1)S(1)} %get-tuple-element.83), channel_id=1, source_target_pairs={{0,8},{1,9},{2,10},{3,11},{4,12},{5,13},{6,14},{7,15},{8,0},{9,1},... | collective-permute-start | bytes 98312 | tf_op jit(solution)/shard_map/ppermute | solution.py:321
  42.4 4.2 %collective-permute-start.19 = (bf16[8,2048]{1,0:T(8,128)(2,1)S(1)}, bf16[8,2048]{1,0:T(8,128)(2,1)S(1)}, u32[]{:S(2)}, u32[]{:S(2)}) collective-permute-start(bf16[8,2048]{1,0:T(8,128)(2,1)S(1)} %get-tuple-element.84), channel_id=1, source_target_pairs={{0,16},{1,17},{2,18},{3,19},{4,20},{5,21},{6,22},{7,23},{8,24},{9,... | collective-permute-start | bytes 98312 | tf_op jit(solution)/shard_map/ppermute | solution.py:321

commit v6 on v5

--- a/solution.py
+++ b/solution.py
@@ -186,8 +186,16 @@
     dst[...] = src[...]
 
 
-def flip_body(*refs):
-    for src, dst in zip(refs[:3], refs[3:]):
+def flip_body(wg_in, wu_in, wd, wg, wu, wg_t, wu_t, wd_t, sems):
+    copies = [
+        pltpu.make_async_copy(src, dst, sems.at[i])
+        for i, (src, dst) in enumerate(((wg_in, wg), (wu_in, wu)))
+    ]
+    for copy in copies:
+        copy.start()
+    wd_t[...] = wd[0].T
+    for copy, src, dst in zip(copies, (wg, wu), (wg_t, wu_t)):
+        copy.wait()
         dst[...] = src[0].T
 
 
@@ -359,8 +367,14 @@
         after=[mark],
     )
     own_pieces = [piece] + [send(piece, part_perm(q)) for q in range(2, SPLIT, 2)]
-    *flipped, last = call(
-        flip_body, [sds((hid, half), BF)] * 3, (wg, wu, down), extra=8 * hid * half, mark=True
+    gate, up, *flipped, last = call(
+        flip_body,
+        [sds(wg.shape, BF)] * 2 + [sds((hid, half), BF)] * 3,
+        (in_hbm(wg), in_hbm(wu), down),
+        in_specs=[HBM] * 2 + [VMEM],
+        scratch=[pltpu.SemaphoreType.DMA((2,))],
+        extra=8 * hid * half,
+        mark=True,
     )
     (own_pieces[-1],) = call(hold_body, [sds((rows, half), BF)], [own_pieces[-1]], after=[last])
     sib_pieces = [send(p, part_perm(1)) for p in own_pieces]
@@ -373,7 +387,7 @@
         part, part_sent, *mark = call(
             forward_body,
             [sds((n, 3 * hid), F32), sds((n, 3 * hid), BF)],
-            (*pieces, wg, wu, down),
+            (*pieces, gate, up, down),
             extra=2 * n * half * 2 + n * hid * 4,
             after=mark,
             mark=i == 0,

time: 48.3 us -> 48.3 us (level)
  waiting for transfers between devices: 15.7 us -> 14.6 us
  Pallas kernels: 11.3 us -> 12.2 us
    ppermute x20, waiting for transfers between devices: 15.7 us -> 14.6 us  [send(): return lax.ppermute(x, AXES, perm)]
    pallas_call x14, Pallas kernels: 11.3 us -> 12.2 us  [call(): pl.pallas_call(whole, out_shape=[*out_shape, *[jax.ShapeDtypeStruct((8, 1...]
  transfers between devices with their start and end apart: 20 -> 20, of which waited for: 12 -> 12; matrix products, arithmetic and copies ran while one was open for 0% -> 0% of each run, Pallas kernels for 15% -> 17%
where the time goes in v6:
time: 48.3 us; the launch traced here: 48.1 us
  starting transfers between devices  20.5 us (42%)
  waiting for transfers between devices  14.6 us (30%)
  Pallas kernels  12.2 us (25%)
  between operations  0.77 us (2%)
    ppermute x20, starting transfers between devices, send(): return lax.ppermute(x, AXES, perm)  20.5 us
    ppermute x20, waiting for transfers between devices, send(): return lax.ppermute(x, AXES, perm)  14.6 us
    pallas_call x14, Pallas kernels, call(): pl.pallas_call(whole, out_shape=[*out_shape, *[jax.ShapeDtypeStruct((8, 1...  12.2 us
  transfers between devices with their start and end apart: 20, of which 12 were waited for; matrix products, arithmetic and copies ran while one was open for 0% of the time, Pallas kernels for 17%

profile of v6, /device:TPU:0, one launch (start us, length us, event | category | flops | bytes accessed | tf_op | source)
XLA Modules:
  0.0 48.1 jit_solution(14214236828476738966)
XLA Ops:
  0.6 1.8 %shard_map.111 = (bf16[8,2048]{1,0:T(8,128)(2,1)S(1)}, bf16[8,2048]{1,0:T(8,128)(2,1)S(1)}, bf16[8,2048]{1,0:T(8,128)(2,1)S(1)}, bf16[8,2048]{1,0:T(8,128)(2,1)S(1)}) custom-call(s32[2,4]{1,0:T(2,128)} %bitcast.2, f32[2,4]{1,0:T(2,128)} %bitcast.4, bf16[128,4096]{1,0:T(8,128)(2,1)} %refs_2_.1, bf16[128,4096]{1,0:T(8,128)(2,1)} %refs_3_.1), custom_call_target="tpu_custom_call" | custom-call | tf_op jit(solution)/shard_map/pallas_call | solution.py:60
  2.5 5.0 %collective-permute-start = (bf16[8,2048]{1,0:T(8,128)(2,1)S(1)}, bf16[8,2048]{1,0:T(8,128)(2,1)S(1)}, u32[]{:S(2)}, u32[]{:S(2)}) collective-permute-start(bf16[8,2048]{1,0:T(8,128)(2,1)S(1)} %get-tuple-element.53), channel_id=1, source_target_pairs={{0,24},{1,25},{2,26},{3,27},{4,28},{5,29},{6,30},{7,31},{8,16},{9,... | collective-permute-start | bytes 98312 | tf_op jit(solution)/shard_map/ppermute | solution.py:329
  7.5 0.3 collective-permute-start.1
  7.8 0.3 collective-permute-start.2
  8.2 1.3 %shard_map.110 = (bf16[1,2048,256]{2,1,0:T(8,128)(2,1)S(1)}, bf16[128,16]{1,0:T(8,128)(2,1)S(1)}, bf16[128,16]{1,0:T(8,128)(2,1)S(1)}, f32[16,1]{1,0:T(8,128)S(1)}, f32[8,128]{1,0:T(8,128)S(1)}) custom-call(bf16[1,2048,256]{2,1,0:T(8,128)(2,1)} %refs_0_.2, s32[2,4]{1,0:T(2,128)} %bitcast.3, f32[2,4]{1,0:T(2,128)} %bitcast.5), custom_call_target="tpu_custom_call" | custom-call | tf_op jit(solution)/shard_map/pallas_call | solution.py:60
  9.4 0.3 collective-permute-done.refs_0_
  9.8 2.6 %collective-permute-done.1.refs_1_ = bf16[8,2048]{1,0:T(8,128)(2,1)S(1)} collective-permute-done((bf16[8,2048]{1,0:T(8,128)(2,1)S(1)}, bf16[8,2048]{1,0:T(8,128)(2,1)S(1)}, u32[]{:S(2)}, u32[]{:S(2)}) %collective-permute-start.1) | collective-permute-done | bytes 32800 | tf_op jit(solution)/shard_map/ppermute | solution.py:329
  12.3 0.2 shard_map.112.refs_0_
  12.5 2.6 %collective-permute-start.3 = (bf16[32,2048]{1,0:T(8,128)(2,1)S(1)}, bf16[32,2048]{1,0:T(8,128)(2,1)S(1)}, u32[]{:S(2)}, u32[]{:S(2)}) collective-permute-start(bf16[32,2048]{1,0:T(8,128)(2,1)S(1)} %shard_map.112.refs_0_), channel_id=1, source_target_pairs={{0,6},{1,7},{2,4},{3,5},{4,2},{5,3},{6,0},{7,1},{8,14},{9,15},{10,... | collective-permute-start | bytes 393224 | tf_op jit(solution)/shard_map/ppermute | solution.py:329
  15.1 0.4 collective-permute-start.10
  15.6 0.5 %collective-permute-start.9 = (bf16[32,2048]{1,0:T(8,128)(2,1)S(1)}, bf16[32,2048]{1,0:T(8,128)(2,1)S(1)}, u32[]{:S(2)}, u32[]{:S(2)}) collective-permute-start(bf16[32,2048]{1,0:T(8,128)(2,1)S(1)} %shard_map.112.refs_0_), channel_id=1, source_target_pairs={{0,2},{1,3},{2,0},{3,1},{4,6},{5,7},{6,4},{7,5},{8,10},{9,11},{10,... | collective-permute-start | bytes 393224 | tf_op jit(solution)/shard_map/ppermute | solution.py:329
  16.1 1.9 %shard_map.113 = (bf16[1,2048,256]{2,1,0:T(8,128)(2,1)S(1)}, bf16[1,2048,256]{2,1,0:T(8,128)(2,1)S(1)}, bf16[256,2048]{1,0:T(8,128)(2,1)S(1)}, bf16[256,2048]{1,...) custom-call(bf16[1,2048,256]{2,1,0:T(8,128)(2,1)} %refs_0_.3, bf16[1,2048,256]{2,1,0:T(8,128)(2,1)} %refs_1_.1, ...), custom_call_target="tpu_custom_call" | custom-call | tf_op jit(solution)/shard_map/pallas_call | solution.py:60
  18.0 0.1 collective-permute-start.4
  18.1 0.9 %collective-permute-done.3.refs_0_ = bf16[32,2048]{1,0:T(8,128)(2,1)S(1)} collective-permute-done((bf16[32,2048]{1,0:T(8,128)(2,1)S(1)}, bf16[32,2048]{1,0:T(8,128)(2,1)S(1)}, u32[]{:S(2)}, u32[]{:S(2)}) %collective-permute-start.3) | collective-permute-done | bytes 131104 | tf_op jit(solution)/shard_map/ppermute | solution.py:329
  19.0 0.1 collective-permute-start.5
  19.1 1.3 %collective-permute-done.10.refs_1_.refs_5_ = bf16[32,2048]{1,0:T(8,128)(2,1)S(1)} collective-permute-done((bf16[32,2048]{1,0:T(8,128)(2,1)S(1)}, bf16[32,2048]{1,0:T(8,128)(2,1)S(1)}, u32[]{:S(2)}, u32[]{:S(2)}) %collective-permute-start.10) | collective-permute-done | bytes 131104 | tf_op jit(solution)/shard_map/ppermute | solution.py:329
  20.3 0.0 collective-permute-start.12
  20.3 0.2 collective-permute-done.9.refs_0_.refs_4_
  20.5 0.3 collective-permute-start.11
  20.9 0.0 collective-permute-done.4.refs_2_
  20.9 0.7 %shard_map.115 = (f32[64,768]{1,0:T(8,128)S(1)}, bf16[64,768]{1,0:T(8,128)(2,1)S(1)}, f32[8,128]{1,0:T(8,128)S(1)}) custom-call(bf16[32,2048]{1,0:T(8,128)(2,1)S(1)} %shard_map.112.refs_0_, bf16[32,2048]{1,0:T(8,128)(2,1)S(1)} %shard_map.114.refs_1_, bf16[32,2048]{1,0:T(8,128)(2,1)S(1)} %collective-permute-done.4.refs_2_, ...), custom_call_target="tpu_custom_call" | custom-call | tf_op jit(solution)/shard_map/pallas_call | solution.py:60
  21.5 0.7 %collective-permute-start.6 = (bf16[64,768]{1,0:T(8,128)(2,1)S(1)}, bf16[64,768]{1,0:T(8,128)(2,1)S(1)}, u32[]{:S(2)}, u32[]{:S(2)}) collective-permute-start(bf16[64,768]{1,0:T(8,128)(2,1)S(1)} %get-tuple-element.63), channel_id=1, source_target_pairs={{0,16},{1,17},{2,18},{3,19},{4,20},{5,21},{6,22},{7,23},{8,24},{9,... | collective-permute-start | bytes 294920 | tf_op jit(solution)/shard_map/ppermute | solution.py:329
  22.2 0.0 collective-permute-done.12.refs_3_.refs_7_
  22.2 0.0 collective-permute-done.11.refs_2_.refs_6_
  22.2 0.7 %shard_map.118 = (f32[64,768]{1,0:T(8,128)S(1)}, bf16[64,768]{1,0:T(8,128)(2,1)S(1)}) custom-call(bf16[32,2048]{1,0:T(8,128)(2,1)S(1)} %collective-permute-done.9.refs_0_.refs_4_, bf16[32,2048]{1,0:T(8,128)(2,1)S(1)} %collective-permute-done.10.refs_1_.refs_5_, bf16[32,2048]{1,0:T(8,128)(2,1)S(1)} %collective-permute-done.11.refs_2_.refs_6_, ...), custom_call_target="tpu_custom_call" | custom-call | tf_op jit(solution)/shard_map/pallas_call | solution.py:60
  22.9 1.5 %collective-permute-start.13 = (bf16[64,768]{1,0:T(8,128)(2,1)S(1)}, bf16[64,768]{1,0:T(8,128)(2,1)S(1)}, u32[]{:S(2)}, u32[]{:S(2)}) collective-permute-start(bf16[64,768]{1,0:T(8,128)(2,1)S(1)} %get-tuple-element.73), channel_id=1, source_target_pairs={{0,16},{1,17},{2,18},{3,19},{4,20},{5,21},{6,22},{7,23},{8,24},{9,... | collective-permute-start | bytes 294920 | tf_op jit(solution)/shard_map/ppermute | solution.py:329
  24.4 2.9 %collective-permute-done.6.refs_1_ = bf16[64,768]{1,0:T(8,128)(2,1)S(1)} collective-permute-done((bf16[64,768]{1,0:T(8,128)(2,1)S(1)}, bf16[64,768]{1,0:T(8,128)(2,1)S(1)}, u32[]{:S(2)}, u32[]{:S(2)}) %collective-permute-start.6) | collective-permute-done | bytes 98336 | tf_op jit(solution)/shard_map/ppermute | solution.py:329
  27.2 0.7 %shard_map.116 = (bf16[64,256]{1,0:T(8,128)(2,1)S(1)}, bf16[64,256]{1,0:T(8,128)(2,1)S(1)}, bf16[64,256]{1,0:T(8,128)(2,1)S(1)}, bf16[64,2048]{1,0:T(8,128)(2,1)...) custom-call(f32[64,768]{1,0:T(8,128)S(1)} %get-tuple-element.62.refs_0_, ...), custom_call_target="tpu_custom_call" | custom-call | tf_op jit(solution)/shard_map/pallas_call | solution.py:60
  27.9 0.1 collective-permute-start.7
  28.0 0.6 %collective-permute-done.13.refs_1_ = bf16[64,768]{1,0:T(8,128)(2,1)S(1)} collective-permute-done((bf16[64,768]{1,0:T(8,128)(2,1)S(1)}, bf16[64,768]{1,0:T(8,128)(2,1)S(1)}, u32[]{:S(2)}, u32[]{:S(2)}) %collective-permute-start.13) | collective-permute-done | bytes 98336 | tf_op jit(solution)/shard_map/ppermute | solution.py:329
  28.6 0.7 %shard_map.119 = (bf16[64,256]{1,0:T(8,128)(2,1)S(1)}, bf16[64,256]{1,0:T(8,128)(2,1)S(1)}, bf16[64,256]{1,0:T(8,128)(2,1)S(1)}, bf16[64,2048]{1,0:T(8,128)(2,1)S(1)}, bf16[64,2048]{1,0:T(8,128)(2,1)S(1)}) custom-call(f32[64,768]{1,0:T(8,128)S(1)} %get-tuple-element.72.refs_0_, bf16[64,768]{1,0:T(8,128)(2,1)S(1)} %collective-permute-done.13.refs_1_, ...), custom_call_target="tpu_custom_call" | custom-call | tf_op jit(solution)/shard_map/pallas_call | solution.py:60
  29.3 0.1 collective-permute-start.14
  29.3 0.2 collective-permute-done.7.refs_1_
  29.5 0.1 shard_map.117
  29.6 2.0 %collective-permute-start.8 = (bf16[32,2048]{1,0:T(8,128)(2,1)S(1)}, bf16[32,2048]{1,0:T(8,128)(2,1)S(1)}, u32[]{:S(2)}, u32[]{:S(2)}) collective-permute-start(bf16[32,2048]{1,0:T(8,128)(2,1)S(1)} %get-tuple-element.70), channel_id=1, source_target_pairs={{0,6},{1,7},{2,4},{3,5},{4,2},{5,3},{6,0},{7,1},{8,14},{9,15},{10,... | collective-permute-start | bytes 393224 | tf_op jit(solution)/shard_map/ppermute | solution.py:329
  31.6 0.1 shard_map.120
  31.7 1.0 %collective-permute-start.15 = (bf16[32,2048]{1,0:T(8,128)(2,1)S(1)}, bf16[32,2048]{1,0:T(8,128)(2,1)S(1)}, u32[]{:S(2)}, u32[]{:S(2)}) collective-permute-start(bf16[32,2048]{1,0:T(8,128)(2,1)S(1)} %get-tuple-element.77), channel_id=1, source_target_pairs={{0,2},{1,3},{2,0},{3,1},{4,6},{5,7},{6,4},{7,5},{8,10},{9,11},{10,... | collective-permute-start | bytes 393224 | tf_op jit(solution)/shard_map/ppermute | solution.py:329
  32.7 1.0 %collective-permute-start.16 = (bf16[32,2048]{1,0:T(8,128)(2,1)S(1)}, bf16[32,2048]{1,0:T(8,128)(2,1)S(1)}, u32[]{:S(2)}, u32[]{:S(2)}) collective-permute-start(bf16[32,2048]{1,0:T(8,128)(2,1)S(1)} %get-tuple-element.78), channel_id=1, source_target_pairs={{0,4},{1,5},{2,6},{3,7},{4,0},{5,1},{6,2},{7,3},{8,12},{9,13},{10,... | collective-permute-start | bytes 393224 | tf_op jit(solution)/shard_map/ppermute | solution.py:329
  33.7 2.4 %shard_map.121 = (bf16[1,2048,256]{2,1,0:T(8,128)(2,1)}, bf16[1,2048,256]{2,1,0:T(8,128)(2,1)}, bf16[1,2048,256]{2,1,0:T(8,128)(2,1)}, f32[8,128]{1,0:T(8,128)S(1)}) custom-call(bf16[32,2048]{1,0:T(8,128)(2,1)S(1)} %shard_map.112.refs_0_, bf16[32,2048]{1,0:T(8,128)(2,1)S(1)} %shard_map.114.refs_1_, bf16[32,2048]{1,0:T(8,128)(2,1)S(1)} %collective-permute-done.4.refs_2_, ...), custom_call_target="tpu_custom_call" | custom-call | flops 402653184 | bytes 3145728 | tf_op jit(solution)/shard_map/pallas_call | solution.py:60
  36.0 0.8 %collective-permute-done.8.refs_1_ = bf16[32,2048]{1,0:T(8,128)(2,1)S(1)} collective-permute-done((bf16[32,2048]{1,0:T(8,128)(2,1)S(1)}, bf16[32,2048]{1,0:T(8,128)(2,1)S(1)}, u32[]{:S(2)}, u32[]{:S(2)}) %collective-permute-start.8) | collective-permute-done | bytes 131104 | tf_op jit(solution)/shard_map/ppermute | solution.py:329
  36.8 2.3 %collective-permute-done.15.refs_2_ = bf16[32,2048]{1,0:T(8,128)(2,1)S(1)} collective-permute-done((bf16[32,2048]{1,0:T(8,128)(2,1)S(1)}, bf16[32,2048]{1,0:T(8,128)(2,1)S(1)}, u32[]{:S(2)}, u32[]{:S(2)}) %collective-permute-start.15) | collective-permute-done | bytes 131104 | tf_op jit(solution)/shard_map/ppermute | solution.py:329
  39.1 0.2 shard_map.122
  39.3 2.1 %collective-permute-start.17 = (bf16[8,2048]{1,0:T(8,128)(2,1)S(1)}, bf16[8,2048]{1,0:T(8,128)(2,1)S(1)}, u32[]{:S(2)}, u32[]{:S(2)}) collective-permute-start(bf16[8,2048]{1,0:T(8,128)(2,1)S(1)} %get-tuple-element.86), channel_id=1, source_target_pairs={{0,24},{1,25},{2,26},{3,27},{4,28},{5,29},{6,30},{7,31},{8,16},{9,... | collective-permute-start | bytes 98312 | tf_op jit(solution)/shard_map/ppermute | solution.py:329
  41.4 0.9 %collective-permute-start.18 = (bf16[8,2048]{1,0:T(8,128)(2,1)S(1)}, bf16[8,2048]{1,0:T(8,128)(2,1)S(1)}, u32[]{:S(2)}, u32[]{:S(2)}) collective-permute-start(bf16[8,2048]{1,0:T(8,128)(2,1)S(1)} %get-tuple-element.87), channel_id=1, source_target_pairs={{0,8},{1,9},{2,10},{3,11},{4,12},{5,13},{6,14},{7,15},{8,0},{9,1},... | collective-permute-start | bytes 98312 | tf_op jit(solution)/shard_map/ppermute | solution.py:329
  42.3 1.5 %collective-permute-start.19 = (bf16[8,2048]{1,0:T(8,128)(2,1)S(1)}, bf16[8,2048]{1,0:T(8,128)(2,1)S(1)}, u32[]{:S(2)}, u32[]{:S(2)}) collective-permute-start(bf16[8,2048]{1,0:T(8,128)(2,1)S(1)} %get-tuple-element.88), channel_id=1, source_target_pairs={{0,16},{1,17},{2,18},{3,19},{4,20},{5,21},{6,22},{7,23},{8,24},{9,... | collective-permute-start | bytes 98312 | tf_op jit(solution)/shard_map/ppermute | solution.py:329
  43.7 1.7 %collective-permute-done.17.refs_3_ = bf16[8,2048]{1,0:T(8,128)(2,1)S(1)} collective-permute-done((bf16[8,2048]{1,0:T(8,128)(2,1)S(1)}, bf16[8,2048]{1,0:T(8,128)(2,1)S(1)}, u32[]{:S(2)}, u32[]{:S(2)}) %collective-permute-start.17) | collective-permute-done | bytes 32800 | tf_op jit(solution)/shard_map/ppermute | solution.py:329
  45.4 1.0 %collective-permute-done.18.refs_4_ = bf16[8,2048]{1,0:T(8,128)(2,1)S(1)} collective-permute-done((bf16[8,2048]{1,0:T(8,128)(2,1)S(1)}, bf16[8,2048]{1,0:T(8,128)(2,1)S(1)}, u32[]{:S(2)}, u32[]{:S(2)}) %collective-permute-start.18) | collective-permute-done | bytes 32800 | tf_op jit(solution)/shard_map/ppermute | solution.py:329
  46.4 1.7 %shard_map.123 = (bf16[128,4096]{1,0:T(8,128)(2,1)}, bf16[128,4096]{1,0:T(8,128)(2,1)}) custom-call(bf16[128,16]{1,0:T(8,128)(2,1)S(1)} %get-tuple-element.50.refs_0_, bf16[128,16]{1,0:T(8,128)(2,1)S(1)} %get-tuple-element.51.refs_1_, f32[16,1]{1,0:T(8,128)S(1)} %get-tuple-element.52.refs_2_, bf16[8,2048]{1,0:T(8,128)(2,1)S(1)} %collective-permute-done.17.refs_3_, ...), custom_call_target="tpu_custom_call" | custom-call | tf_op jit(solution)/shard_map/pallas_call | solution.py:60
  (6 shorter events, 0.0 us)
Async XLA Ops:
  2.5 7.3 %collective-permute-start = (bf16[8,2048]{1,0:T(8,128)(2,1)S(1)}, bf16[8,2048]{1,0:T(8,128)(2,1)S(1)}, u32[]{:S(2)}, u32[]{:S(2)}) collective-permute-start(bf16[8,2048]{1,0:T(8,128)(2,1)S(1)} %get-tuple-element.53), channel_id=1, source_target_pairs={{0,24},{1,25},{2,26},{3,27},{4,28},{5,29},{6,30},{7,31},{8,16},{9,... | collective-permute-start | bytes 98312 | tf_op jit(solution)/shard_map/ppermute | solution.py:329
  7.5 4.8 %collective-permute-start.1 = (bf16[8,2048]{1,0:T(8,128)(2,1)S(1)}, bf16[8,2048]{1,0:T(8,128)(2,1)S(1)}, u32[]{:S(2)}, u32[]{:S(2)}) collective-permute-start(bf16[8,2048]{1,0:T(8,128)(2,1)S(1)} %get-tuple-element.54), channel_id=1, source_target_pairs={{0,8},{1,9},{2,10},{3,11},{4,12},{5,13},{6,14},{7,15},{8,0},{9,1},... | collective-permute-start | bytes 98312 | tf_op jit(solution)/shard_map/ppermute | solution.py:329
  7.8 4.5 %collective-permute-start.2 = (bf16[8,2048]{1,0:T(8,128)(2,1)S(1)}, bf16[8,2048]{1,0:T(8,128)(2,1)S(1)}, u32[]{:S(2)}, u32[]{:S(2)}) collective-permute-start(bf16[8,2048]{1,0:T(8,128)(2,1)S(1)} %get-tuple-element.55), channel_id=1, source_target_pairs={{0,16},{1,17},{2,18},{3,19},{4,20},{5,21},{6,22},{7,23},{8,24},{9,... | collective-permute-start | bytes 98312 | tf_op jit(solution)/shard_map/ppermute | solution.py:329
  12.5 6.5 %collective-permute-start.3 = (bf16[32,2048]{1,0:T(8,128)(2,1)S(1)}, bf16[32,2048]{1,0:T(8,128)(2,1)S(1)}, u32[]{:S(2)}, u32[]{:S(2)}) collective-permute-start(bf16[32,2048]{1,0:T(8,128)(2,1)S(1)} %shard_map.112.refs_0_), channel_id=1, source_target_pairs={{0,6},{1,7},{2,4},{3,5},{4,2},{5,3},{6,0},{7,1},{8,14},{9,15},{10,... | collective-permute-start | bytes 393224 | tf_op jit(solution)/shard_map/ppermute | solution.py:329
  15.1 5.2 %collective-permute-start.10 = (bf16[32,2048]{1,0:T(8,128)(2,1)S(1)}, bf16[32,2048]{1,0:T(8,128)(2,1)S(1)}, u32[]{:S(2)}, u32[]{:S(2)}) collective-permute-start(bf16[32,2048]{1,0:T(8,128)(2,1)S(1)} %shard_map.112.refs_0_), channel_id=1, source_target_pairs={{0,4},{1,5},{2,6},{3,7},{4,0},{5,1},{6,2},{7,3},{8,12},{9,13},{10,... | collective-permute-start | bytes 393224 | tf_op jit(solution)/shard_map/ppermute | solution.py:329
  15.6 5.0 %collective-permute-start.9 = (bf16[32,2048]{1,0:T(8,128)(2,1)S(1)}, bf16[32,2048]{1,0:T(8,128)(2,1)S(1)}, u32[]{:S(2)}, u32[]{:S(2)}) collective-permute-start(bf16[32,2048]{1,0:T(8,128)(2,1)S(1)} %shard_map.112.refs_0_), channel_id=1, source_target_pairs={{0,2},{1,3},{2,0},{3,1},{4,6},{5,7},{6,4},{7,5},{8,10},{9,11},{10,... | collective-permute-start | bytes 393224 | tf_op jit(solution)/shard_map/ppermute | solution.py:329
  18.0 2.8 %collective-permute-start.4 = (bf16[32,2048]{1,0:T(8,128)(2,1)S(1)}, bf16[32,2048]{1,0:T(8,128)(2,1)S(1)}, u32[]{:S(2)}, u32[]{:S(2)}) collective-permute-start(bf16[32,2048]{1,0:T(8,128)(2,1)S(1)} %shard_map.112.refs_0_), channel_id=1, source_target_pairs={{0,1},{1,0},{2,3},{3,2},{4,5},{5,4},{6,7},{7,6},{8,9},{9,8},{10,11... | collective-permute-start | bytes 393224 | tf_op jit(solution)/shard_map/ppermute | solution.py:329
  19.0 1.9 %collective-permute-start.5 = (bf16[32,2048]{1,0:T(8,128)(2,1)S(1)}, bf16[32,2048]{1,0:T(8,128)(2,1)S(1)}, u32[]{:S(2)}, u32[]{:S(2)}) collective-permute-start(bf16[32,2048]{1,0:T(8,128)(2,1)S(1)} %shard_map.114.refs_1_), channel_id=1, source_target_pairs={{0,1},{1,0},{2,3},{3,2},{4,5},{5,4},{6,7},{7,6},{8,9},{9,8},{10,11... | collective-permute-start | bytes 393224 | tf_op jit(solution)/shard_map/ppermute | solution.py:329
  20.3 1.9 %collective-permute-start.12 = (bf16[32,2048]{1,0:T(8,128)(2,1)S(1)}, bf16[32,2048]{1,0:T(8,128)(2,1)S(1)}, u32[]{:S(2)}, u32[]{:S(2)}) collective-permute-start(bf16[32,2048]{1,0:T(8,128)(2,1)S(1)} %collective-permute-done.10.refs_1_.refs_5_), channel_id=1, source_target_pairs={{0,1},{1,0},{2,3},{3,2},{4,5},{5,4},{6,7},{7,6},{8,9},{9,8},{10,11... | collective-permute-start | bytes 393224 | tf_op jit(solution)/shard_map/ppermute | solution.py:329
  20.5 1.7 %collective-permute-start.11 = (bf16[32,2048]{1,0:T(8,128)(2,1)S(1)}, bf16[32,2048]{1,0:T(8,128)(2,1)S(1)}, u32[]{:S(2)}, u32[]{:S(2)}) collective-permute-start(bf16[32,2048]{1,0:T(8,128)(2,1)S(1)} %collective-permute-done.9.refs_0_.refs_4_), channel_id=1, source_target_pairs={{0,1},{1,0},{2,3},{3,2},{4,5},{5,4},{6,7},{7,6},{8,9},{9,8},{10,11... | collective-permute-start | bytes 393224 | tf_op jit(solution)/shard_map/ppermute | solution.py:329
  21.5 5.7 %collective-permute-start.6 = (bf16[64,768]{1,0:T(8,128)(2,1)S(1)}, bf16[64,768]{1,0:T(8,128)(2,1)S(1)}, u32[]{:S(2)}, u32[]{:S(2)}) collective-permute-start(bf16[64,768]{1,0:T(8,128)(2,1)S(1)} %get-tuple-element.63), channel_id=1, source_target_pairs={{0,16},{1,17},{2,18},{3,19},{4,20},{5,21},{6,22},{7,23},{8,24},{9,... | collective-permute-start | bytes 294920 | tf_op jit(solution)/shard_map/ppermute | solution.py:329
  22.9 5.7 %collective-permute-start.13 = (bf16[64,768]{1,0:T(8,128)(2,1)S(1)}, bf16[64,768]{1,0:T(8,128)(2,1)S(1)}, u32[]{:S(2)}, u32[]{:S(2)}) collective-permute-start(bf16[64,768]{1,0:T(8,128)(2,1)S(1)} %get-tuple-element.73), channel_id=1, source_target_pairs={{0,16},{1,17},{2,18},{3,19},{4,20},{5,21},{6,22},{7,23},{8,24},{9,... | collective-permute-start | bytes 294920 | tf_op jit(solution)/shard_map/ppermute | solution.py:329
  27.9 1.6 %collective-permute-start.7 = (bf16[64,2048]{1,0:T(8,128)(2,1)S(1)}, bf16[64,2048]{1,0:T(8,128)(2,1)S(1)}, u32[]{:S(2)}, u32[]{:S(2)}) collective-permute-start(bf16[64,2048]{1,0:T(8,128)(2,1)S(1)} %get-tuple-element.68), channel_id=1, source_target_pairs={{0,1},{1,0},{2,3},{3,2},{4,5},{5,4},{6,7},{7,6},{8,9},{9,8},{10,11... | collective-permute-start | bytes 786440 | tf_op jit(solution)/shard_map/ppermute | solution.py:329
  29.3 2.3 %collective-permute-start.14 = (bf16[64,2048]{1,0:T(8,128)(2,1)S(1)}, bf16[64,2048]{1,0:T(8,128)(2,1)S(1)}, u32[]{:S(2)}, u32[]{:S(2)}) collective-permute-start(bf16[64,2048]{1,0:T(8,128)(2,1)S(1)} %get-tuple-element.76), channel_id=1, source_target_pairs={{0,1},{1,0},{2,3},{3,2},{4,5},{5,4},{6,7},{7,6},{8,9},{9,8},{10,11... | collective-permute-start | bytes 786440 | tf_op jit(solution)/shard_map/ppermute | solution.py:329
  29.6 7.2 %collective-permute-start.8 = (bf16[32,2048]{1,0:T(8,128)(2,1)S(1)}, bf16[32,2048]{1,0:T(8,128)(2,1)S(1)}, u32[]{:S(2)}, u32[]{:S(2)}) collective-permute-start(bf16[32,2048]{1,0:T(8,128)(2,1)S(1)} %get-tuple-element.70), channel_id=1, source_target_pairs={{0,6},{1,7},{2,4},{3,5},{4,2},{5,3},{6,0},{7,1},{8,14},{9,15},{10,... | collective-permute-start | bytes 393224 | tf_op jit(solution)/shard_map/ppermute | solution.py:329
  31.7 7.4 %collective-permute-start.15 = (bf16[32,2048]{1,0:T(8,128)(2,1)S(1)}, bf16[32,2048]{1,0:T(8,128)(2,1)S(1)}, u32[]{:S(2)}, u32[]{:S(2)}) collective-permute-start(bf16[32,2048]{1,0:T(8,128)(2,1)S(1)} %get-tuple-element.77), channel_id=1, source_target_pairs={{0,2},{1,3},{2,0},{3,1},{4,6},{5,7},{6,4},{7,5},{8,10},{9,11},{10,... | collective-permute-start | bytes 393224 | tf_op jit(solution)/shard_map/ppermute | solution.py:329
  32.7 6.4 %collective-permute-start.16 = (bf16[32,2048]{1,0:T(8,128)(2,1)S(1)}, bf16[32,2048]{1,0:T(8,128)(2,1)S(1)}, u32[]{:S(2)}, u32[]{:S(2)}) collective-permute-start(bf16[32,2048]{1,0:T(8,128)(2,1)S(1)} %get-tuple-element.78), channel_id=1, source_target_pairs={{0,4},{1,5},{2,6},{3,7},{4,0},{5,1},{6,2},{7,3},{8,12},{9,13},{10,... | collective-permute-start | bytes 393224 | tf_op jit(solution)/shard_map/ppermute | solution.py:329
  39.3 6.1 %collective-permute-start.17 = (bf16[8,2048]{1,0:T(8,128)(2,1)S(1)}, bf16[8,2048]{1,0:T(8,128)(2,1)S(1)}, u32[]{:S(2)}, u32[]{:S(2)}) collective-permute-start(bf16[8,2048]{1,0:T(8,128)(2,1)S(1)} %get-tuple-element.86), channel_id=1, source_target_pairs={{0,24},{1,25},{2,26},{3,27},{4,28},{5,29},{6,30},{7,31},{8,16},{9,... | collective-permute-start | bytes 98312 | tf_op jit(solution)/shard_map/ppermute | solution.py:329
  41.4 5.1 %collective-permute-start.18 = (bf16[8,2048]{1,0:T(8,128)(2,1)S(1)}, bf16[8,2048]{1,0:T(8,128)(2,1)S(1)}, u32[]{:S(2)}, u32[]{:S(2)}) collective-permute-start(bf16[8,2048]{1,0:T(8,128)(2,1)S(1)} %get-tuple-element.87), channel_id=1, source_target_pairs={{0,8},{1,9},{2,10},{3,11},{4,12},{5,13},{6,14},{7,15},{8,0},{9,1},... | collective-permute-start | bytes 98312 | tf_op jit(solution)/shard_map/ppermute | solution.py:329
  42.3 4.2 %collective-permute-start.19 = (bf16[8,2048]{1,0:T(8,128)(2,1)S(1)}, bf16[8,2048]{1,0:T(8,128)(2,1)S(1)}, u32[]{:S(2)}, u32[]{:S(2)}) collective-permute-start(bf16[8,2048]{1,0:T(8,128)(2,1)S(1)} %get-tuple-element.88), channel_id=1, source_target_pairs={{0,16},{1,17},{2,18},{3,19},{4,20},{5,21},{6,22},{7,23},{8,24},{9,... | collective-permute-start | bytes 98312 | tf_op jit(solution)/shard_map/ppermute | solution.py:329

commit v7 on v6

--- a/solution.py
+++ b/solution.py
@@ -148,12 +148,12 @@
     out[...] = mm(pick, wide[...].astype(BF)).astype(BF)
 
 
-def load_body(experts, slots, src, routes_in, gates_in, dst, put_out, put_grad, scale, routes, gates, sems):
-    moves = ((src, dst), (routes_in, routes), (gates_in, gates))
+def prepare_body(experts, slots, routes_in, gates_in, put_out, put_grad, scale, routes, gates, sems):
+    moves = ((routes_in, routes), (gates_in, gates))
     copies = [pltpu.make_async_copy(*move, sems.at[i]) for i, move in enumerate(moves)]
     for copy in copies:
         copy.start()
-    for copy in copies[1:]:
+    for copy in copies:
         copy.wait()
     expert = own_expert(experts)
     each = 2 * slots
@@ -167,7 +167,6 @@
     hit = lax.broadcasted_iota(jnp.int32, (block, count), 0) == pos
     put_out[...] = jnp.where(hit & is_out_lane, 1.0, 0.0).astype(BF)
     put_grad[...] = jnp.where(hit & ~is_out_lane, 1.0, 0.0).astype(BF)
-    copies[0].wait()
 
 
 def forward_body(*refs):
@@ -186,15 +185,14 @@
     dst[...] = src[...]
 
 
-def flip_body(wg_in, wu_in, wd, wg, wu, wg_t, wu_t, wd_t, sems):
+def flip_body(*refs):
+    srcs, dsts, flipped, sems = refs[:3], refs[3:6], refs[6:9], refs[9]
     copies = [
-        pltpu.make_async_copy(src, dst, sems.at[i])
-        for i, (src, dst) in enumerate(((wg_in, wg), (wu_in, wu)))
+        pltpu.make_async_copy(src, dst, sems.at[i]) for i, (src, dst) in enumerate(zip(srcs, dsts))
     ]
     for copy in copies:
         copy.start()
-    wd_t[...] = wd[0].T
-    for copy, src, dst in zip(copies, (wg, wu), (wg_t, wu_t)):
+    for copy, src, dst in zip(copies, dsts, flipped):
         copy.wait()
         dst[...] = src[0].T
 
@@ -348,12 +346,12 @@
         got[kind] = send(got[kind], home_perm(*kind, 1))
     count = each * experts
     small = [pltpu.SMEM((experts, slots), jnp.int32), pltpu.SMEM((experts, slots), F32)]
-    down, put_out, put_grad, scale, mark = call(
-        functools.partial(load_body, experts, slots),
-        [sds(wd.shape, BF)] + [sds((block, count), BF)] * 2 + [sds((count, 1), F32)],
-        [in_hbm(x) for x in (wd, routes[0], gate_values[0])],
-        in_specs=[HBM] * 3,
-        scratch=[*small, pltpu.SemaphoreType.DMA((3,))],
+    put_out, put_grad, scale, mark = call(
+        functools.partial(prepare_body, experts, slots),
+        [sds((block, count), BF)] * 2 + [sds((count, 1), F32)],
+        [in_hbm(x) for x in (routes[0], gate_values[0])],
+        in_specs=[HBM] * 2,
+        scratch=[*small, pltpu.SemaphoreType.DMA((2,))],
         mark=True,
     )
     rows = each * n_msg
@@ -367,12 +365,12 @@
         after=[mark],
     )
     own_pieces = [piece] + [send(piece, part_perm(q)) for q in range(2, SPLIT, 2)]
-    gate, up, *flipped, last = call(
+    gate, up, down, *flipped, last = call(
         flip_body,
-        [sds(wg.shape, BF)] * 2 + [sds((hid, half), BF)] * 3,
-        (in_hbm(wg), in_hbm(wu), down),
-        in_specs=[HBM] * 2 + [VMEM],
-        scratch=[pltpu.SemaphoreType.DMA((2,))],
+        [sds(wg.shape, BF)] * 3 + [sds((hid, half), BF)] * 3,
+        [in_hbm(x) for x in (wg, wu, wd)],
+        in_specs=[HBM] * 3,
+        scratch=[pltpu.SemaphoreType.DMA((3,))],
         extra=8 * hid * half,
         mark=True,
     )

time: 48.3 us -> 48.3 us (level)
  no operation moved by 1% of the time
where the time goes in v7:
time: 48.3 us; the launch traced here: 48.1 us
  starting transfers between devices  20.5 us (42%)
  waiting for transfers between devices  14.8 us (31%)
  Pallas kernels  12.1 us (25%)
  between operations  0.77 us (2%)
    ppermute x20, starting transfers between devices, send(): return lax.ppermute(x, AXES, perm)  20.5 us
    ppermute x20, waiting for transfers between devices, send(): return lax.ppermute(x, AXES, perm)  14.8 us
    pallas_call x14, Pallas kernels, call(): pl.pallas_call(whole, out_shape=[*out_shape, *[jax.ShapeDtypeStruct((8, 1...  12.1 us
  transfers between devices with their start and end apart: 20, of which 12 were waited for; matrix products, arithmetic and copies ran while one was open for 0% of the time, Pallas kernels for 17%

profile of v7, /device:TPU:0, one launch (start us, length us, event | category | flops | bytes accessed | tf_op | source)
XLA Modules:
  0.0 48.1 jit_solution(7866003711592817676)
XLA Ops:
  0.6 1.8 %shard_map.111 = (bf16[8,2048]{1,0:T(8,128)(2,1)S(1)}, bf16[8,2048]{1,0:T(8,128)(2,1)S(1)}, bf16[8,2048]{1,0:T(8,128)(2,1)S(1)}, bf16[8,2048]{1,0:T(8,128)(2,1)S(1)}) custom-call(s32[2,4]{1,0:T(2,128)} %bitcast.2, f32[2,4]{1,0:T(2,128)} %bitcast.4, bf16[128,4096]{1,0:T(8,128)(2,1)} %refs_2_.2, bf16[128,4096]{1,0:T(8,128)(2,1)} %refs_3_.1), custom_call_target="tpu_custom_call" | custom-call | tf_op jit(solution)/shard_map/pallas_call | solution.py:60
  2.5 5.0 %collective-permute-start = (bf16[8,2048]{1,0:T(8,128)(2,1)S(1)}, bf16[8,2048]{1,0:T(8,128)(2,1)S(1)}, u32[]{:S(2)}, u32[]{:S(2)}) collective-permute-start(bf16[8,2048]{1,0:T(8,128)(2,1)S(1)} %get-tuple-element.53), channel_id=1, source_target_pairs={{0,24},{1,25},{2,26},{3,27},{4,28},{5,29},{6,30},{7,31},{8,16},{9,... | collective-permute-start | bytes 98312 | tf_op jit(solution)/shard_map/ppermute | solution.py:327
  7.5 0.3 collective-permute-start.1
  7.8 0.3 collective-permute-start.2
  8.2 0.8 %shard_map.110 = (bf16[128,16]{1,0:T(8,128)(2,1)S(1)}, bf16[128,16]{1,0:T(8,128)(2,1)S(1)}, f32[16,1]{1,0:T(8,128)S(1)}, f32[8,128]{1,0:T(8,128)S(1)}) custom-call(s32[2,4]{1,0:T(2,128)} %bitcast.3, f32[2,4]{1,0:T(2,128)} %bitcast.5), custom_call_target="tpu_custom_call" | custom-call | tf_op jit(solution)/shard_map/pallas_call | solution.py:60
  8.9 0.8 %collective-permute-done.refs_0_ = bf16[8,2048]{1,0:T(8,128)(2,1)S(1)} collective-permute-done((bf16[8,2048]{1,0:T(8,128)(2,1)S(1)}, bf16[8,2048]{1,0:T(8,128)(2,1)S(1)}, u32[]{:S(2)}, u32[]{:S(2)}) %collective-permute-start) | collective-permute-done | bytes 32800 | tf_op jit(solution)/shard_map/ppermute | solution.py:327
  9.8 2.6 %collective-permute-done.1.refs_1_ = bf16[8,2048]{1,0:T(8,128)(2,1)S(1)} collective-permute-done((bf16[8,2048]{1,0:T(8,128)(2,1)S(1)}, bf16[8,2048]{1,0:T(8,128)(2,1)S(1)}, u32[]{:S(2)}, u32[]{:S(2)}) %collective-permute-start.1) | collective-permute-done | bytes 32800 | tf_op jit(solution)/shard_map/ppermute | solution.py:327
  12.3 0.0 collective-permute-done.2.refs_2_
  12.3 0.2 shard_map.112.refs_0_
  12.5 2.6 %collective-permute-start.3 = (bf16[32,2048]{1,0:T(8,128)(2,1)S(1)}, bf16[32,2048]{1,0:T(8,128)(2,1)S(1)}, u32[]{:S(2)}, u32[]{:S(2)}) collective-permute-start(bf16[32,2048]{1,0:T(8,128)(2,1)S(1)} %shard_map.112.refs_0_), channel_id=1, source_target_pairs={{0,6},{1,7},{2,4},{3,5},{4,2},{5,3},{6,0},{7,1},{8,14},{9,15},{10,... | collective-permute-start | bytes 393224 | tf_op jit(solution)/shard_map/ppermute | solution.py:327
  15.1 0.4 collective-permute-start.10
  15.6 0.5 %collective-permute-start.9 = (bf16[32,2048]{1,0:T(8,128)(2,1)S(1)}, bf16[32,2048]{1,0:T(8,128)(2,1)S(1)}, u32[]{:S(2)}, u32[]{:S(2)}) collective-permute-start(bf16[32,2048]{1,0:T(8,128)(2,1)S(1)} %shard_map.112.refs_0_), channel_id=1, source_target_pairs={{0,2},{1,3},{2,0},{3,1},{4,6},{5,7},{6,4},{7,5},{8,10},{9,11},{10,... | collective-permute-start | bytes 393224 | tf_op jit(solution)/shard_map/ppermute | solution.py:327
  16.1 2.3 %shard_map.113 = (bf16[1,2048,256]{2,1,0:T(8,128)(2,1)S(1)}, bf16[1,2048,256]{2,1,0:T(8,128)(2,1)S(1)}, bf16[1,2048,256]{2,1,0:T(8,128)(2,1)S(1)}, bf16[256,2048...) custom-call(bf16[1,2048,256]{2,1,0:T(8,128)(2,1)} %refs_0_.1, ...), custom_call_target="tpu_custom_call" | custom-call | tf_op jit(solution)/shard_map/pallas_call | solution.py:60
  18.4 0.1 collective-permute-start.4
  18.4 0.5 %collective-permute-done.3.refs_0_ = bf16[32,2048]{1,0:T(8,128)(2,1)S(1)} collective-permute-done((bf16[32,2048]{1,0:T(8,128)(2,1)S(1)}, bf16[32,2048]{1,0:T(8,128)(2,1)S(1)}, u32[]{:S(2)}, u32[]{:S(2)}) %collective-permute-start.3) | collective-permute-done | bytes 131104 | tf_op jit(solution)/shard_map/ppermute | solution.py:327
  19.0 0.1 collective-permute-start.5
  19.1 1.3 %collective-permute-done.10.refs_1_.refs_5_ = bf16[32,2048]{1,0:T(8,128)(2,1)S(1)} collective-permute-done((bf16[32,2048]{1,0:T(8,128)(2,1)S(1)}, bf16[32,2048]{1,0:T(8,128)(2,1)S(1)}, u32[]{:S(2)}, u32[]{:S(2)}) %collective-permute-start.10) | collective-permute-done | bytes 131104 | tf_op jit(solution)/shard_map/ppermute | solution.py:327
  20.3 0.2 collective-permute-done.9.refs_0_.refs_4_
  20.5 0.3 collective-permute-start.11
  20.9 0.0 collective-permute-done.4.refs_2_
  20.9 0.0 collective-permute-done.5.refs_3_
  20.9 0.7 %shard_map.115 = (f32[64,768]{1,0:T(8,128)S(1)}, bf16[64,768]{1,0:T(8,128)(2,1)S(1)}, f32[8,128]{1,0:T(8,128)S(1)}) custom-call(bf16[32,2048]{1,0:T(8,128)(2,1)S(1)} %shard_map.112.refs_0_, bf16[32,2048]{1,0:T(8,128)(2,1)S(1)} %shard_map.114.refs_1_, bf16[32,2048]{1,0:T(8,128)(2,1)S(1)} %collective-permute-done.4.refs_2_, ...), custom_call_target="tpu_custom_call" | custom-call | tf_op jit(solution)/shard_map/pallas_call | solution.py:60
  21.5 0.7 %collective-permute-start.6 = (bf16[64,768]{1,0:T(8,128)(2,1)S(1)}, bf16[64,768]{1,0:T(8,128)(2,1)S(1)}, u32[]{:S(2)}, u32[]{:S(2)}) collective-permute-start(bf16[64,768]{1,0:T(8,128)(2,1)S(1)} %get-tuple-element.63), channel_id=1, source_target_pairs={{0,16},{1,17},{2,18},{3,19},{4,20},{5,21},{6,22},{7,23},{8,24},{9,... | collective-permute-start | bytes 294920 | tf_op jit(solution)/shard_map/ppermute | solution.py:327
  22.2 0.7 %shard_map.118 = (f32[64,768]{1,0:T(8,128)S(1)}, bf16[64,768]{1,0:T(8,128)(2,1)S(1)}) custom-call(bf16[32,2048]{1,0:T(8,128)(2,1)S(1)} %collective-permute-done.9.refs_0_.refs_4_, bf16[32,2048]{1,0:T(8,128)(2,1)S(1)} %collective-permute-done.10.refs_1_.refs_5_, bf16[32,2048]{1,0:T(8,128)(2,1)S(1)} %collective-permute-done.11.refs_2_.refs_6_, ...), custom_call_target="tpu_custom_call" | custom-call | tf_op jit(solution)/shard_map/pallas_call | solution.py:60
  22.9 1.5 %collective-permute-start.13 = (bf16[64,768]{1,0:T(8,128)(2,1)S(1)}, bf16[64,768]{1,0:T(8,128)(2,1)S(1)}, u32[]{:S(2)}, u32[]{:S(2)}) collective-permute-start(bf16[64,768]{1,0:T(8,128)(2,1)S(1)} %get-tuple-element.73), channel_id=1, source_target_pairs={{0,16},{1,17},{2,18},{3,19},{4,20},{5,21},{6,22},{7,23},{8,24},{9,... | collective-permute-start | bytes 294920 | tf_op jit(solution)/shard_map/ppermute | solution.py:327
  24.4 2.9 %collective-permute-done.6.refs_1_ = bf16[64,768]{1,0:T(8,128)(2,1)S(1)} collective-permute-done((bf16[64,768]{1,0:T(8,128)(2,1)S(1)}, bf16[64,768]{1,0:T(8,128)(2,1)S(1)}, u32[]{:S(2)}, u32[]{:S(2)}) %collective-permute-start.6) | collective-permute-done | bytes 98336 | tf_op jit(solution)/shard_map/ppermute | solution.py:327
  27.2 0.7 %shard_map.116 = (bf16[64,256]{1,0:T(8,128)(2,1)S(1)}, bf16[64,256]{1,0:T(8,128)(2,1)S(1)}, bf16[64,256]{1,0:T(8,128)(2,1)S(1)}, bf16[64,2048]{1,0:T(8,128)(2,1)...) custom-call(f32[64,768]{1,0:T(8,128)S(1)} %get-tuple-element.62.refs_0_, ...), custom_call_target="tpu_custom_call" | custom-call | tf_op jit(solution)/shard_map/pallas_call | solution.py:60
  27.9 0.1 collective-permute-start.7
  28.0 0.6 %collective-permute-done.13.refs_1_ = bf16[64,768]{1,0:T(8,128)(2,1)S(1)} collective-permute-done((bf16[64,768]{1,0:T(8,128)(2,1)S(1)}, bf16[64,768]{1,0:T(8,128)(2,1)S(1)}, u32[]{:S(2)}, u32[]{:S(2)}) %collective-permute-start.13) | collective-permute-done | bytes 98336 | tf_op jit(solution)/shard_map/ppermute | solution.py:327
  28.6 0.7 %shard_map.119 = (bf16[64,256]{1,0:T(8,128)(2,1)S(1)}, bf16[64,256]{1,0:T(8,128)(2,1)S(1)}, bf16[64,256]{1,0:T(8,128)(2,1)S(1)}, bf16[64,2048]{1,0:T(8,128)(2,1)S(1)}, bf16[64,2048]{1,0:T(8,128)(2,1)S(1)}) custom-call(f32[64,768]{1,0:T(8,128)S(1)} %get-tuple-element.72.refs_0_, bf16[64,768]{1,0:T(8,128)(2,1)S(1)} %collective-permute-done.13.refs_1_, ...), custom_call_target="tpu_custom_call" | custom-call | tf_op jit(solution)/shard_map/pallas_call | solution.py:60
  29.3 0.1 collective-permute-start.14
  29.3 0.2 collective-permute-done.7.refs_1_
  29.5 0.1 shard_map.117
  29.6 2.0 %collective-permute-start.8 = (bf16[32,2048]{1,0:T(8,128)(2,1)S(1)}, bf16[32,2048]{1,0:T(8,128)(2,1)S(1)}, u32[]{:S(2)}, u32[]{:S(2)}) collective-permute-start(bf16[32,2048]{1,0:T(8,128)(2,1)S(1)} %get-tuple-element.70), channel_id=1, source_target_pairs={{0,6},{1,7},{2,4},{3,5},{4,2},{5,3},{6,0},{7,1},{8,14},{9,15},{10,... | collective-permute-start | bytes 393224 | tf_op jit(solution)/shard_map/ppermute | solution.py:327
  31.6 0.0 collective-permute-done.14.refs_1_
  31.6 0.1 shard_map.120
  31.6 1.0 %collective-permute-start.15 = (bf16[32,2048]{1,0:T(8,128)(2,1)S(1)}, bf16[32,2048]{1,0:T(8,128)(2,1)S(1)}, u32[]{:S(2)}, u32[]{:S(2)}) collective-permute-start(bf16[32,2048]{1,0:T(8,128)(2,1)S(1)} %get-tuple-element.77), channel_id=1, source_target_pairs={{0,2},{1,3},{2,0},{3,1},{4,6},{5,7},{6,4},{7,5},{8,10},{9,11},{10,... | collective-permute-start | bytes 393224 | tf_op jit(solution)/shard_map/ppermute | solution.py:327
  32.7 1.0 %collective-permute-start.16 = (bf16[32,2048]{1,0:T(8,128)(2,1)S(1)}, bf16[32,2048]{1,0:T(8,128)(2,1)S(1)}, u32[]{:S(2)}, u32[]{:S(2)}) collective-permute-start(bf16[32,2048]{1,0:T(8,128)(2,1)S(1)} %get-tuple-element.78), channel_id=1, source_target_pairs={{0,4},{1,5},{2,6},{3,7},{4,0},{5,1},{6,2},{7,3},{8,12},{9,13},{10,... | collective-permute-start | bytes 393224 | tf_op jit(solution)/shard_map/ppermute | solution.py:327
  33.6 2.4 %shard_map.121 = (bf16[1,2048,256]{2,1,0:T(8,128)(2,1)}, bf16[1,2048,256]{2,1,0:T(8,128)(2,1)}, bf16[1,2048,256]{2,1,0:T(8,128)(2,1)}, f32[8,128]{1,0:T(8,128)S(1)}) custom-call(bf16[32,2048]{1,0:T(8,128)(2,1)S(1)} %shard_map.112.refs_0_, bf16[32,2048]{1,0:T(8,128)(2,1)S(1)} %shard_map.114.refs_1_, bf16[32,2048]{1,0:T(8,128)(2,1)S(1)} %collective-permute-done.4.refs_2_, ...), custom_call_target="tpu_custom_call" | custom-call | flops 402653184 | bytes 3145728 | tf_op jit(solution)/shard_map/pallas_call | solution.py:60
  36.0 0.8 %collective-permute-done.8.refs_1_ = bf16[32,2048]{1,0:T(8,128)(2,1)S(1)} collective-permute-done((bf16[32,2048]{1,0:T(8,128)(2,1)S(1)}, bf16[32,2048]{1,0:T(8,128)(2,1)S(1)}, u32[]{:S(2)}, u32[]{:S(2)}) %collective-permute-start.8) | collective-permute-done | bytes 131104 | tf_op jit(solution)/shard_map/ppermute | solution.py:327
  36.8 2.3 %collective-permute-done.15.refs_2_ = bf16[32,2048]{1,0:T(8,128)(2,1)S(1)} collective-permute-done((bf16[32,2048]{1,0:T(8,128)(2,1)S(1)}, bf16[32,2048]{1,0:T(8,128)(2,1)S(1)}, u32[]{:S(2)}, u32[]{:S(2)}) %collective-permute-start.15) | collective-permute-done | bytes 131104 | tf_op jit(solution)/shard_map/ppermute | solution.py:327
  39.1 0.2 shard_map.122
  39.3 2.1 %collective-permute-start.17 = (bf16[8,2048]{1,0:T(8,128)(2,1)S(1)}, bf16[8,2048]{1,0:T(8,128)(2,1)S(1)}, u32[]{:S(2)}, u32[]{:S(2)}) collective-permute-start(bf16[8,2048]{1,0:T(8,128)(2,1)S(1)} %get-tuple-element.86), channel_id=1, source_target_pairs={{0,24},{1,25},{2,26},{3,27},{4,28},{5,29},{6,30},{7,31},{8,16},{9,... | collective-permute-start | bytes 98312 | tf_op jit(solution)/shard_map/ppermute | solution.py:327
  41.4 0.9 %collective-permute-start.18 = (bf16[8,2048]{1,0:T(8,128)(2,1)S(1)}, bf16[8,2048]{1,0:T(8,128)(2,1)S(1)}, u32[]{:S(2)}, u32[]{:S(2)}) collective-permute-start(bf16[8,2048]{1,0:T(8,128)(2,1)S(1)} %get-tuple-element.87), channel_id=1, source_target_pairs={{0,8},{1,9},{2,10},{3,11},{4,12},{5,13},{6,14},{7,15},{8,0},{9,1},... | collective-permute-start | bytes 98312 | tf_op jit(solution)/shard_map/ppermute | solution.py:327
  42.2 1.5 %collective-permute-start.19 = (bf16[8,2048]{1,0:T(8,128)(2,1)S(1)}, bf16[8,2048]{1,0:T(8,128)(2,1)S(1)}, u32[]{:S(2)}, u32[]{:S(2)}) collective-permute-start(bf16[8,2048]{1,0:T(8,128)(2,1)S(1)} %get-tuple-element.88), channel_id=1, source_target_pairs={{0,16},{1,17},{2,18},{3,19},{4,20},{5,21},{6,22},{7,23},{8,24},{9,... | collective-permute-start | bytes 98312 | tf_op jit(solution)/shard_map/ppermute | solution.py:327
  43.7 1.7 %collective-permute-done.17.refs_3_ = bf16[8,2048]{1,0:T(8,128)(2,1)S(1)} collective-permute-done((bf16[8,2048]{1,0:T(8,128)(2,1)S(1)}, bf16[8,2048]{1,0:T(8,128)(2,1)S(1)}, u32[]{:S(2)}, u32[]{:S(2)}) %collective-permute-start.17) | collective-permute-done | bytes 32800 | tf_op jit(solution)/shard_map/ppermute | solution.py:327
  45.4 1.0 %collective-permute-done.18.refs_4_ = bf16[8,2048]{1,0:T(8,128)(2,1)S(1)} collective-permute-done((bf16[8,2048]{1,0:T(8,128)(2,1)S(1)}, bf16[8,2048]{1,0:T(8,128)(2,1)S(1)}, u32[]{:S(2)}, u32[]{:S(2)}) %collective-permute-start.18) | collective-permute-done | bytes 32800 | tf_op jit(solution)/shard_map/ppermute | solution.py:327
  46.4 1.7 %shard_map.123 = (bf16[128,4096]{1,0:T(8,128)(2,1)}, bf16[128,4096]{1,0:T(8,128)(2,1)}) custom-call(bf16[128,16]{1,0:T(8,128)(2,1)S(1)} %get-tuple-element.50.refs_0_, bf16[128,16]{1,0:T(8,128)(2,1)S(1)} %get-tuple-element.51.refs_1_, f32[16,1]{1,0:T(8,128)S(1)} %get-tuple-element.52.refs_2_, bf16[8,2048]{1,0:T(8,128)(2,1)S(1)} %collective-permute-done.17.refs_3_, ...), custom_call_target="tpu_custom_call" | custom-call | tf_op jit(solution)/shard_map/pallas_call | solution.py:60
  (6 shorter events, 0.0 us)
Async XLA Ops:
  2.5 7.3 %collective-permute-start = (bf16[8,2048]{1,0:T(8,128)(2,1)S(1)}, bf16[8,2048]{1,0:T(8,128)(2,1)S(1)}, u32[]{:S(2)}, u32[]{:S(2)}) collective-permute-start(bf16[8,2048]{1,0:T(8,128)(2,1)S(1)} %get-tuple-element.53), channel_id=1, source_target_pairs={{0,24},{1,25},{2,26},{3,27},{4,28},{5,29},{6,30},{7,31},{8,16},{9,... | collective-permute-start | bytes 98312 | tf_op jit(solution)/shard_map/ppermute | solution.py:327
  7.5 4.8 %collective-permute-start.1 = (bf16[8,2048]{1,0:T(8,128)(2,1)S(1)}, bf16[8,2048]{1,0:T(8,128)(2,1)S(1)}, u32[]{:S(2)}, u32[]{:S(2)}) collective-permute-start(bf16[8,2048]{1,0:T(8,128)(2,1)S(1)} %get-tuple-element.54), channel_id=1, source_target_pairs={{0,8},{1,9},{2,10},{3,11},{4,12},{5,13},{6,14},{7,15},{8,0},{9,1},... | collective-permute-start | bytes 98312 | tf_op jit(solution)/shard_map/ppermute | solution.py:327
  7.8 4.5 %collective-permute-start.2 = (bf16[8,2048]{1,0:T(8,128)(2,1)S(1)}, bf16[8,2048]{1,0:T(8,128)(2,1)S(1)}, u32[]{:S(2)}, u32[]{:S(2)}) collective-permute-start(bf16[8,2048]{1,0:T(8,128)(2,1)S(1)} %get-tuple-element.55), channel_id=1, source_target_pairs={{0,16},{1,17},{2,18},{3,19},{4,20},{5,21},{6,22},{7,23},{8,24},{9,... | collective-permute-start | bytes 98312 | tf_op jit(solution)/shard_map/ppermute | solution.py:327
  12.5 6.5 %collective-permute-start.3 = (bf16[32,2048]{1,0:T(8,128)(2,1)S(1)}, bf16[32,2048]{1,0:T(8,128)(2,1)S(1)}, u32[]{:S(2)}, u32[]{:S(2)}) collective-permute-start(bf16[32,2048]{1,0:T(8,128)(2,1)S(1)} %shard_map.112.refs_0_), channel_id=1, source_target_pairs={{0,6},{1,7},{2,4},{3,5},{4,2},{5,3},{6,0},{7,1},{8,14},{9,15},{10,... | collective-permute-start | bytes 393224 | tf_op jit(solution)/shard_map/ppermute | solution.py:327
  15.1 5.2 %collective-permute-start.10 = (bf16[32,2048]{1,0:T(8,128)(2,1)S(1)}, bf16[32,2048]{1,0:T(8,128)(2,1)S(1)}, u32[]{:S(2)}, u32[]{:S(2)}) collective-permute-start(bf16[32,2048]{1,0:T(8,128)(2,1)S(1)} %shard_map.112.refs_0_), channel_id=1, source_target_pairs={{0,4},{1,5},{2,6},{3,7},{4,0},{5,1},{6,2},{7,3},{8,12},{9,13},{10,... | collective-permute-start | bytes 393224 | tf_op jit(solution)/shard_map/ppermute | solution.py:327
  15.6 5.0 %collective-permute-start.9 = (bf16[32,2048]{1,0:T(8,128)(2,1)S(1)}, bf16[32,2048]{1,0:T(8,128)(2,1)S(1)}, u32[]{:S(2)}, u32[]{:S(2)}) collective-permute-start(bf16[32,2048]{1,0:T(8,128)(2,1)S(1)} %shard_map.112.refs_0_), channel_id=1, source_target_pairs={{0,2},{1,3},{2,0},{3,1},{4,6},{5,7},{6,4},{7,5},{8,10},{9,11},{10,... | collective-permute-start | bytes 393224 | tf_op jit(solution)/shard_map/ppermute | solution.py:327
  18.4 2.5 %collective-permute-start.4 = (bf16[32,2048]{1,0:T(8,128)(2,1)S(1)}, bf16[32,2048]{1,0:T(8,128)(2,1)S(1)}, u32[]{:S(2)}, u32[]{:S(2)}) collective-permute-start(bf16[32,2048]{1,0:T(8,128)(2,1)S(1)} %shard_map.112.refs_0_), channel_id=1, source_target_pairs={{0,1},{1,0},{2,3},{3,2},{4,5},{5,4},{6,7},{7,6},{8,9},{9,8},{10,11... | collective-permute-start | bytes 393224 | tf_op jit(solution)/shard_map/ppermute | solution.py:327
  19.0 1.9 %collective-permute-start.5 = (bf16[32,2048]{1,0:T(8,128)(2,1)S(1)}, bf16[32,2048]{1,0:T(8,128)(2,1)S(1)}, u32[]{:S(2)}, u32[]{:S(2)}) collective-permute-start(bf16[32,2048]{1,0:T(8,128)(2,1)S(1)} %shard_map.114.refs_1_), channel_id=1, source_target_pairs={{0,1},{1,0},{2,3},{3,2},{4,5},{5,4},{6,7},{7,6},{8,9},{9,8},{10,11... | collective-permute-start | bytes 393224 | tf_op jit(solution)/shard_map/ppermute | solution.py:327
  20.3 1.9 %collective-permute-start.12 = (bf16[32,2048]{1,0:T(8,128)(2,1)S(1)}, bf16[32,2048]{1,0:T(8,128)(2,1)S(1)}, u32[]{:S(2)}, u32[]{:S(2)}) collective-permute-start(bf16[32,2048]{1,0:T(8,128)(2,1)S(1)} %collective-permute-done.10.refs_1_.refs_5_), channel_id=1, source_target_pairs={{0,1},{1,0},{2,3},{3,2},{4,5},{5,4},{6,7},{7,6},{8,9},{9,8},{10,11... | collective-permute-start | bytes 393224 | tf_op jit(solution)/shard_map/ppermute | solution.py:327
  20.5 1.7 %collective-permute-start.11 = (bf16[32,2048]{1,0:T(8,128)(2,1)S(1)}, bf16[32,2048]{1,0:T(8,128)(2,1)S(1)}, u32[]{:S(2)}, u32[]{:S(2)}) collective-permute-start(bf16[32,2048]{1,0:T(8,128)(2,1)S(1)} %collective-permute-done.9.refs_0_.refs_4_), channel_id=1, source_target_pairs={{0,1},{1,0},{2,3},{3,2},{4,5},{5,4},{6,7},{7,6},{8,9},{9,8},{10,11... | collective-permute-start | bytes 393224 | tf_op jit(solution)/shard_map/ppermute | solution.py:327
  21.5 5.7 %collective-permute-start.6 = (bf16[64,768]{1,0:T(8,128)(2,1)S(1)}, bf16[64,768]{1,0:T(8,128)(2,1)S(1)}, u32[]{:S(2)}, u32[]{:S(2)}) collective-permute-start(bf16[64,768]{1,0:T(8,128)(2,1)S(1)} %get-tuple-element.63), channel_id=1, source_target_pairs={{0,16},{1,17},{2,18},{3,19},{4,20},{5,21},{6,22},{7,23},{8,24},{9,... | collective-permute-start | bytes 294920 | tf_op jit(solution)/shard_map/ppermute | solution.py:327
  22.9 5.7 %collective-permute-start.13 = (bf16[64,768]{1,0:T(8,128)(2,1)S(1)}, bf16[64,768]{1,0:T(8,128)(2,1)S(1)}, u32[]{:S(2)}, u32[]{:S(2)}) collective-permute-start(bf16[64,768]{1,0:T(8,128)(2,1)S(1)} %get-tuple-element.73), channel_id=1, source_target_pairs={{0,16},{1,17},{2,18},{3,19},{4,20},{5,21},{6,22},{7,23},{8,24},{9,... | collective-permute-start | bytes 294920 | tf_op jit(solution)/shard_map/ppermute | solution.py:327
  27.9 1.6 %collective-permute-start.7 = (bf16[64,2048]{1,0:T(8,128)(2,1)S(1)}, bf16[64,2048]{1,0:T(8,128)(2,1)S(1)}, u32[]{:S(2)}, u32[]{:S(2)}) collective-permute-start(bf16[64,2048]{1,0:T(8,128)(2,1)S(1)} %get-tuple-element.68), channel_id=1, source_target_pairs={{0,1},{1,0},{2,3},{3,2},{4,5},{5,4},{6,7},{7,6},{8,9},{9,8},{10,11... | collective-permute-start | bytes 786440 | tf_op jit(solution)/shard_map/ppermute | solution.py:327
  29.3 2.3 %collective-permute-start.14 = (bf16[64,2048]{1,0:T(8,128)(2,1)S(1)}, bf16[64,2048]{1,0:T(8,128)(2,1)S(1)}, u32[]{:S(2)}, u32[]{:S(2)}) collective-permute-start(bf16[64,2048]{1,0:T(8,128)(2,1)S(1)} %get-tuple-element.76), channel_id=1, source_target_pairs={{0,1},{1,0},{2,3},{3,2},{4,5},{5,4},{6,7},{7,6},{8,9},{9,8},{10,11... | collective-permute-start | bytes 786440 | tf_op jit(solution)/shard_map/ppermute | solution.py:327
  29.6 7.2 %collective-permute-start.8 = (bf16[32,2048]{1,0:T(8,128)(2,1)S(1)}, bf16[32,2048]{1,0:T(8,128)(2,1)S(1)}, u32[]{:S(2)}, u32[]{:S(2)}) collective-permute-start(bf16[32,2048]{1,0:T(8,128)(2,1)S(1)} %get-tuple-element.70), channel_id=1, source_target_pairs={{0,6},{1,7},{2,4},{3,5},{4,2},{5,3},{6,0},{7,1},{8,14},{9,15},{10,... | collective-permute-start | bytes 393224 | tf_op jit(solution)/shard_map/ppermute | solution.py:327
  31.6 7.4 %collective-permute-start.15 = (bf16[32,2048]{1,0:T(8,128)(2,1)S(1)}, bf16[32,2048]{1,0:T(8,128)(2,1)S(1)}, u32[]{:S(2)}, u32[]{:S(2)}) collective-permute-start(bf16[32,2048]{1,0:T(8,128)(2,1)S(1)} %get-tuple-element.77), channel_id=1, source_target_pairs={{0,2},{1,3},{2,0},{3,1},{4,6},{5,7},{6,4},{7,5},{8,10},{9,11},{10,... | collective-permute-start | bytes 393224 | tf_op jit(solution)/shard_map/ppermute | solution.py:327
  32.7 6.4 %collective-permute-start.16 = (bf16[32,2048]{1,0:T(8,128)(2,1)S(1)}, bf16[32,2048]{1,0:T(8,128)(2,1)S(1)}, u32[]{:S(2)}, u32[]{:S(2)}) collective-permute-start(bf16[32,2048]{1,0:T(8,128)(2,1)S(1)} %get-tuple-element.78), channel_id=1, source_target_pairs={{0,4},{1,5},{2,6},{3,7},{4,0},{5,1},{6,2},{7,3},{8,12},{9,13},{10,... | collective-permute-start | bytes 393224 | tf_op jit(solution)/shard_map/ppermute | solution.py:327
  39.3 6.1 %collective-permute-start.17 = (bf16[8,2048]{1,0:T(8,128)(2,1)S(1)}, bf16[8,2048]{1,0:T(8,128)(2,1)S(1)}, u32[]{:S(2)}, u32[]{:S(2)}) collective-permute-start(bf16[8,2048]{1,0:T(8,128)(2,1)S(1)} %get-tuple-element.86), channel_id=1, source_target_pairs={{0,24},{1,25},{2,26},{3,27},{4,28},{5,29},{6,30},{7,31},{8,16},{9,... | collective-permute-start | bytes 98312 | tf_op jit(solution)/shard_map/ppermute | solution.py:327
  41.4 5.1 %collective-permute-start.18 = (bf16[8,2048]{1,0:T(8,128)(2,1)S(1)}, bf16[8,2048]{1,0:T(8,128)(2,1)S(1)}, u32[]{:S(2)}, u32[]{:S(2)}) collective-permute-start(bf16[8,2048]{1,0:T(8,128)(2,1)S(1)} %get-tuple-element.87), channel_id=1, source_target_pairs={{0,8},{1,9},{2,10},{3,11},{4,12},{5,13},{6,14},{7,15},{8,0},{9,1},... | collective-permute-start | bytes 98312 | tf_op jit(solution)/shard_map/ppermute | solution.py:327
  42.2 4.2 %collective-permute-start.19 = (bf16[8,2048]{1,0:T(8,128)(2,1)S(1)}, bf16[8,2048]{1,0:T(8,128)(2,1)S(1)}, u32[]{:S(2)}, u32[]{:S(2)}) collective-permute-start(bf16[8,2048]{1,0:T(8,128)(2,1)S(1)} %get-tuple-element.88), channel_id=1, source_target_pairs={{0,16},{1,17},{2,18},{3,19},{4,20},{5,21},{6,22},{7,23},{8,24},{9,... | collective-permute-start | bytes 98312 | tf_op jit(solution)/shard_map/ppermute | solution.py:327

commit v8 on v7

--- a/solution.py
+++ b/solution.py
@@ -100,7 +100,7 @@
         for i, src in enumerate((tokens, cot)):
             moves.append((src.at[:, at], both.at[dx, pl.ds(i * block, block)]))
     copies = [pltpu.make_async_copy(*move, sems.at[i]) for i, move in enumerate(moves)]
-    for copy in copies:
+    for copy in copies[2:] + copies[:2]:
         copy.start()
     for copy in copies[:2]:
         copy.wait()
@@ -379,16 +379,14 @@
     chips = SPLIT // 2
     halves = [(0, chips - 1), tuple(range(1, chips - 1))]
     ordered = [[own_pieces[j] for j in js] + [sib_pieces[j] for j in js] for js in halves]
-    mark, parts, recv = (), [], []
-    for i, pieces in enumerate(ordered):
+    parts, recv = [], []
+    for pieces in ordered:
         n = len(pieces) * rows // 2
-        part, part_sent, *mark = call(
+        part, part_sent = call(
             forward_body,
             [sds((n, 3 * hid), F32), sds((n, 3 * hid), BF)],
             (*pieces, gate, up, down),
             extra=2 * n * half * 2 + n * hid * 4,
-            after=mark,
-            mark=i == 0,
         )
         parts.append(part)
         recv.append([send(part_sent, batch_perm(dx)) for dx in range(1, n_dp)])

time: 48.3 us -> 48.2 us (level)
  no operation moved by 1% of the time
where the time goes in v8:
time: 48.2 us; the launch traced here: 48.1 us
  starting transfers between devices  20.5 us (43%)
  waiting for transfers between devices  14.8 us (31%)
  Pallas kernels  12 us (25%)
  between operations  0.77 us (2%)
    ppermute x20, starting transfers between devices, send(): return lax.ppermute(x, AXES, perm)  20.5 us
    ppermute x20, waiting for transfers between devices, send(): return lax.ppermute(x, AXES, perm)  14.8 us
    pallas_call x14, Pallas kernels, call(): pl.pallas_call(whole, out_shape=[*out_shape, *[jax.ShapeDtypeStruct((8, 1...  12 us
  transfers between devices with their start and end apart: 20, of which 12 were waited for; matrix products, arithmetic and copies ran while one was open for 0% of the time, Pallas kernels for 17%

profile of v8, /device:TPU:0, one launch (start us, length us, event | category | flops | bytes accessed | tf_op | source)
XLA Modules:
  0.0 48.1 jit_solution(6670275372779659891)
XLA Ops:
  0.6 1.8 %shard_map.111 = (bf16[8,2048]{1,0:T(8,128)(2,1)S(1)}, bf16[8,2048]{1,0:T(8,128)(2,1)S(1)}, bf16[8,2048]{1,0:T(8,128)(2,1)S(1)}, bf16[8,2048]{1,0:T(8,128)(2,1)S(1)}) custom-call(s32[2,4]{1,0:T(2,128)} %bitcast.2, f32[2,4]{1,0:T(2,128)} %bitcast.4, bf16[128,4096]{1,0:T(8,128)(2,1)} %refs_2_.2, bf16[128,4096]{1,0:T(8,128)(2,1)} %refs_3_.1), custom_call_target="tpu_custom_call" | custom-call | tf_op jit(solution)/shard_map/pallas_call | solution.py:60
  2.5 5.0 %collective-permute-start = (bf16[8,2048]{1,0:T(8,128)(2,1)S(1)}, bf16[8,2048]{1,0:T(8,128)(2,1)S(1)}, u32[]{:S(2)}, u32[]{:S(2)}) collective-permute-start(bf16[8,2048]{1,0:T(8,128)(2,1)S(1)} %get-tuple-element.52), channel_id=1, source_target_pairs={{0,24},{1,25},{2,26},{3,27},{4,28},{5,29},{6,30},{7,31},{8,16},{9,... | collective-permute-start | bytes 98312 | tf_op jit(solution)/shard_map/ppermute | solution.py:327
  7.5 0.3 collective-permute-start.1
  7.8 0.3 collective-permute-start.2
  8.1 0.8 %shard_map.110 = (bf16[128,16]{1,0:T(8,128)(2,1)S(1)}, bf16[128,16]{1,0:T(8,128)(2,1)S(1)}, f32[16,1]{1,0:T(8,128)S(1)}, f32[8,128]{1,0:T(8,128)S(1)}) custom-call(s32[2,4]{1,0:T(2,128)} %bitcast.3, f32[2,4]{1,0:T(2,128)} %bitcast.5), custom_call_target="tpu_custom_call" | custom-call | tf_op jit(solution)/shard_map/pallas_call | solution.py:60
  8.9 0.8 %collective-permute-done.refs_0_ = bf16[8,2048]{1,0:T(8,128)(2,1)S(1)} collective-permute-done((bf16[8,2048]{1,0:T(8,128)(2,1)S(1)}, bf16[8,2048]{1,0:T(8,128)(2,1)S(1)}, u32[]{:S(2)}, u32[]{:S(2)}) %collective-permute-start) | collective-permute-done | bytes 32800 | tf_op jit(solution)/shard_map/ppermute | solution.py:327
  9.8 2.6 %collective-permute-done.1.refs_1_ = bf16[8,2048]{1,0:T(8,128)(2,1)S(1)} collective-permute-done((bf16[8,2048]{1,0:T(8,128)(2,1)S(1)}, bf16[8,2048]{1,0:T(8,128)(2,1)S(1)}, u32[]{:S(2)}, u32[]{:S(2)}) %collective-permute-start.1) | collective-permute-done | bytes 32800 | tf_op jit(solution)/shard_map/ppermute | solution.py:327
  12.3 0.0 collective-permute-done.2.refs_2_
  12.3 0.2 shard_map.112.refs_0_
  12.5 2.6 %collective-permute-start.3 = (bf16[32,2048]{1,0:T(8,128)(2,1)S(1)}, bf16[32,2048]{1,0:T(8,128)(2,1)S(1)}, u32[]{:S(2)}, u32[]{:S(2)}) collective-permute-start(bf16[32,2048]{1,0:T(8,128)(2,1)S(1)} %shard_map.112.refs_0_), channel_id=1, source_target_pairs={{0,6},{1,7},{2,4},{3,5},{4,2},{5,3},{6,0},{7,1},{8,14},{9,15},{10,... | collective-permute-start | bytes 393224 | tf_op jit(solution)/shard_map/ppermute | solution.py:327
  15.1 0.4 collective-permute-start.10
  15.6 0.5 %collective-permute-start.9 = (bf16[32,2048]{1,0:T(8,128)(2,1)S(1)}, bf16[32,2048]{1,0:T(8,128)(2,1)S(1)}, u32[]{:S(2)}, u32[]{:S(2)}) collective-permute-start(bf16[32,2048]{1,0:T(8,128)(2,1)S(1)} %shard_map.112.refs_0_), channel_id=1, source_target_pairs={{0,2},{1,3},{2,0},{3,1},{4,6},{5,7},{6,4},{7,5},{8,10},{9,11},{10,... | collective-permute-start | bytes 393224 | tf_op jit(solution)/shard_map/ppermute | solution.py:327
  16.1 2.3 %shard_map.113 = (bf16[1,2048,256]{2,1,0:T(8,128)(2,1)S(1)}, bf16[1,2048,256]{2,1,0:T(8,128)(2,1)S(1)}, bf16[1,2048,256]{2,1,0:T(8,128)(2,1)S(1)}, bf16[256,2048...) custom-call(bf16[1,2048,256]{2,1,0:T(8,128)(2,1)} %refs_0_.1, ...), custom_call_target="tpu_custom_call" | custom-call | tf_op jit(solution)/shard_map/pallas_call | solution.py:60
  18.4 0.1 collective-permute-start.4
  18.4 0.5 %collective-permute-done.3.refs_0_ = bf16[32,2048]{1,0:T(8,128)(2,1)S(1)} collective-permute-done((bf16[32,2048]{1,0:T(8,128)(2,1)S(1)}, bf16[32,2048]{1,0:T(8,128)(2,1)S(1)}, u32[]{:S(2)}, u32[]{:S(2)}) %collective-permute-start.3) | collective-permute-done | bytes 131104 | tf_op jit(solution)/shard_map/ppermute | solution.py:327
  19.0 0.1 collective-permute-start.5
  19.1 1.3 %collective-permute-done.10.refs_1_.refs_5_ = bf16[32,2048]{1,0:T(8,128)(2,1)S(1)} collective-permute-done((bf16[32,2048]{1,0:T(8,128)(2,1)S(1)}, bf16[32,2048]{1,0:T(8,128)(2,1)S(1)}, u32[]{:S(2)}, u32[]{:S(2)}) %collective-permute-start.10) | collective-permute-done | bytes 131104 | tf_op jit(solution)/shard_map/ppermute | solution.py:327
  20.3 0.0 collective-permute-start.12
  20.3 0.2 collective-permute-done.9.refs_0_.refs_4_
  20.5 0.3 collective-permute-start.11
  20.8 0.0 collective-permute-done.4.refs_2_
  20.9 0.0 collective-permute-done.5.refs_3_
  20.9 0.7 %shard_map.115 = (f32[64,768]{1,0:T(8,128)S(1)}, bf16[64,768]{1,0:T(8,128)(2,1)S(1)}) custom-call(bf16[32,2048]{1,0:T(8,128)(2,1)S(1)} %shard_map.112.refs_0_, bf16[32,2048]{1,0:T(8,128)(2,1)S(1)} %shard_map.114.refs_1_, bf16[32,2048]{1,0:T(8,128)(2,1)S(1)} %collective-permute-done.4.refs_2_, bf16[32,2048]{1,0:T(8,128)(2,1)S(1)} %collective-permute-done.5.refs_3_, ...), custom_call_target="tpu_custom_call" | custom-call | tf_op jit(solution)/shard_map/pallas_call | solution.py:60
  21.5 0.7 %collective-permute-start.6 = (bf16[64,768]{1,0:T(8,128)(2,1)S(1)}, bf16[64,768]{1,0:T(8,128)(2,1)S(1)}, u32[]{:S(2)}, u32[]{:S(2)}) collective-permute-start(bf16[64,768]{1,0:T(8,128)(2,1)S(1)} %get-tuple-element.62), channel_id=1, source_target_pairs={{0,16},{1,17},{2,18},{3,19},{4,20},{5,21},{6,22},{7,23},{8,24},{9,... | collective-permute-start | bytes 294920 | tf_op jit(solution)/shard_map/ppermute | solution.py:327
  22.2 0.7 %shard_map.118 = (f32[64,768]{1,0:T(8,128)S(1)}, bf16[64,768]{1,0:T(8,128)(2,1)S(1)}) custom-call(bf16[32,2048]{1,0:T(8,128)(2,1)S(1)} %collective-permute-done.9.refs_0_.refs_4_, bf16[32,2048]{1,0:T(8,128)(2,1)S(1)} %collective-permute-done.10.refs_1_.refs_5_, bf16[32,2048]{1,0:T(8,128)(2,1)S(1)} %collective-permute-done.11.refs_2_.refs_6_, ...), custom_call_target="tpu_custom_call" | custom-call | tf_op jit(solution)/shard_map/pallas_call | solution.py:60
  22.9 1.5 %collective-permute-start.13 = (bf16[64,768]{1,0:T(8,128)(2,1)S(1)}, bf16[64,768]{1,0:T(8,128)(2,1)S(1)}, u32[]{:S(2)}, u32[]{:S(2)}) collective-permute-start(bf16[64,768]{1,0:T(8,128)(2,1)S(1)} %get-tuple-element.71), channel_id=1, source_target_pairs={{0,16},{1,17},{2,18},{3,19},{4,20},{5,21},{6,22},{7,23},{8,24},{9,... | collective-permute-start | bytes 294920 | tf_op jit(solution)/shard_map/ppermute | solution.py:327
  24.4 2.9 %collective-permute-done.6.refs_1_ = bf16[64,768]{1,0:T(8,128)(2,1)S(1)} collective-permute-done((bf16[64,768]{1,0:T(8,128)(2,1)S(1)}, bf16[64,768]{1,0:T(8,128)(2,1)S(1)}, u32[]{:S(2)}, u32[]{:S(2)}) %collective-permute-start.6) | collective-permute-done | bytes 98336 | tf_op jit(solution)/shard_map/ppermute | solution.py:327
  27.2 0.7 %shard_map.116 = (bf16[64,256]{1,0:T(8,128)(2,1)S(1)}, bf16[64,256]{1,0:T(8,128)(2,1)S(1)}, bf16[64,256]{1,0:T(8,128)(2,1)S(1)}, bf16[64,2048]{1,0:T(8,128)(2,1)...) custom-call(f32[64,768]{1,0:T(8,128)S(1)} %get-tuple-element.61.refs_0_, ...), custom_call_target="tpu_custom_call" | custom-call | tf_op jit(solution)/shard_map/pallas_call | solution.py:60
  27.9 0.1 collective-permute-start.7
  28.0 0.6 %collective-permute-done.13.refs_1_ = bf16[64,768]{1,0:T(8,128)(2,1)S(1)} collective-permute-done((bf16[64,768]{1,0:T(8,128)(2,1)S(1)}, bf16[64,768]{1,0:T(8,128)(2,1)S(1)}, u32[]{:S(2)}, u32[]{:S(2)}) %collective-permute-start.13) | collective-permute-done | bytes 98336 | tf_op jit(solution)/shard_map/ppermute | solution.py:327
  28.6 0.7 %shard_map.119 = (bf16[64,256]{1,0:T(8,128)(2,1)S(1)}, bf16[64,256]{1,0:T(8,128)(2,1)S(1)}, bf16[64,256]{1,0:T(8,128)(2,1)S(1)}, bf16[64,2048]{1,0:T(8,128)(2,1)S(1)}, bf16[64,2048]{1,0:T(8,128)(2,1)S(1)}) custom-call(f32[64,768]{1,0:T(8,128)S(1)} %get-tuple-element.70.refs_0_, bf16[64,768]{1,0:T(8,128)(2,1)S(1)} %collective-permute-done.13.refs_1_, ...), custom_call_target="tpu_custom_call" | custom-call | tf_op jit(solution)/shard_map/pallas_call | solution.py:60
  29.2 0.1 collective-permute-start.14
  29.3 0.2 collective-permute-done.7.refs_1_
  29.5 0.1 shard_map.117
  29.6 2.0 %collective-permute-start.8 = (bf16[32,2048]{1,0:T(8,128)(2,1)S(1)}, bf16[32,2048]{1,0:T(8,128)(2,1)S(1)}, u32[]{:S(2)}, u32[]{:S(2)}) collective-permute-start(bf16[32,2048]{1,0:T(8,128)(2,1)S(1)} %get-tuple-element.69), channel_id=1, source_target_pairs={{0,6},{1,7},{2,4},{3,5},{4,2},{5,3},{6,0},{7,1},{8,14},{9,15},{10,... | collective-permute-start | bytes 393224 | tf_op jit(solution)/shard_map/ppermute | solution.py:327
  31.6 0.1 shard_map.120
  31.6 1.0 %collective-permute-start.15 = (bf16[32,2048]{1,0:T(8,128)(2,1)S(1)}, bf16[32,2048]{1,0:T(8,128)(2,1)S(1)}, u32[]{:S(2)}, u32[]{:S(2)}) collective-permute-start(bf16[32,2048]{1,0:T(8,128)(2,1)S(1)} %get-tuple-element.75), channel_id=1, source_target_pairs={{0,2},{1,3},{2,0},{3,1},{4,6},{5,7},{6,4},{7,5},{8,10},{9,11},{10,... | collective-permute-start | bytes 393224 | tf_op jit(solution)/shard_map/ppermute | solution.py:327
  32.6 1.0 %collective-permute-start.16 = (bf16[32,2048]{1,0:T(8,128)(2,1)S(1)}, bf16[32,2048]{1,0:T(8,128)(2,1)S(1)}, u32[]{:S(2)}, u32[]{:S(2)}) collective-permute-start(bf16[32,2048]{1,0:T(8,128)(2,1)S(1)} %get-tuple-element.76), channel_id=1, source_target_pairs={{0,4},{1,5},{2,6},{3,7},{4,0},{5,1},{6,2},{7,3},{8,12},{9,13},{10,... | collective-permute-start | bytes 393224 | tf_op jit(solution)/shard_map/ppermute | solution.py:327
  33.6 2.4 %shard_map.121 = (bf16[1,2048,256]{2,1,0:T(8,128)(2,1)}, bf16[1,2048,256]{2,1,0:T(8,128)(2,1)}, bf16[1,2048,256]{2,1,0:T(8,128)(2,1)}, f32[8,128]{1,0:T(8,128)S(1)}) custom-call(bf16[32,2048]{1,0:T(8,128)(2,1)S(1)} %shard_map.112.refs_0_, bf16[32,2048]{1,0:T(8,128)(2,1)S(1)} %shard_map.114.refs_1_, bf16[32,2048]{1,0:T(8,128)(2,1)S(1)} %collective-permute-done.4.refs_2_, ...), custom_call_target="tpu_custom_call" | custom-call | flops 402653184 | bytes 3145728 | tf_op jit(solution)/shard_map/pallas_call | solution.py:60
  36.0 0.8 %collective-permute-done.8.refs_1_ = bf16[32,2048]{1,0:T(8,128)(2,1)S(1)} collective-permute-done((bf16[32,2048]{1,0:T(8,128)(2,1)S(1)}, bf16[32,2048]{1,0:T(8,128)(2,1)S(1)}, u32[]{:S(2)}, u32[]{:S(2)}) %collective-permute-start.8) | collective-permute-done | bytes 131104 | tf_op jit(solution)/shard_map/ppermute | solution.py:327
  36.8 2.3 %collective-permute-done.15.refs_2_ = bf16[32,2048]{1,0:T(8,128)(2,1)S(1)} collective-permute-done((bf16[32,2048]{1,0:T(8,128)(2,1)S(1)}, bf16[32,2048]{1,0:T(8,128)(2,1)S(1)}, u32[]{:S(2)}, u32[]{:S(2)}) %collective-permute-start.15) | collective-permute-done | bytes 131104 | tf_op jit(solution)/shard_map/ppermute | solution.py:327
  39.1 0.2 shard_map.122
  39.3 2.1 %collective-permute-start.17 = (bf16[8,2048]{1,0:T(8,128)(2,1)S(1)}, bf16[8,2048]{1,0:T(8,128)(2,1)S(1)}, u32[]{:S(2)}, u32[]{:S(2)}) collective-permute-start(bf16[8,2048]{1,0:T(8,128)(2,1)S(1)} %get-tuple-element.84), channel_id=1, source_target_pairs={{0,24},{1,25},{2,26},{3,27},{4,28},{5,29},{6,30},{7,31},{8,16},{9,... | collective-permute-start | bytes 98312 | tf_op jit(solution)/shard_map/ppermute | solution.py:327
  41.3 0.9 %collective-permute-start.18 = (bf16[8,2048]{1,0:T(8,128)(2,1)S(1)}, bf16[8,2048]{1,0:T(8,128)(2,1)S(1)}, u32[]{:S(2)}, u32[]{:S(2)}) collective-permute-start(bf16[8,2048]{1,0:T(8,128)(2,1)S(1)} %get-tuple-element.85), channel_id=1, source_target_pairs={{0,8},{1,9},{2,10},{3,11},{4,12},{5,13},{6,14},{7,15},{8,0},{9,1},... | collective-permute-start | bytes 98312 | tf_op jit(solution)/shard_map/ppermute | solution.py:327
  42.2 1.5 %collective-permute-start.19 = (bf16[8,2048]{1,0:T(8,128)(2,1)S(1)}, bf16[8,2048]{1,0:T(8,128)(2,1)S(1)}, u32[]{:S(2)}, u32[]{:S(2)}) collective-permute-start(bf16[8,2048]{1,0:T(8,128)(2,1)S(1)} %get-tuple-element.86), channel_id=1, source_target_pairs={{0,16},{1,17},{2,18},{3,19},{4,20},{5,21},{6,22},{7,23},{8,24},{9,... | collective-permute-start | bytes 98312 | tf_op jit(solution)/shard_map/ppermute | solution.py:327
  43.7 1.7 %collective-permute-done.17.refs_3_ = bf16[8,2048]{1,0:T(8,128)(2,1)S(1)} collective-permute-done((bf16[8,2048]{1,0:T(8,128)(2,1)S(1)}, bf16[8,2048]{1,0:T(8,128)(2,1)S(1)}, u32[]{:S(2)}, u32[]{:S(2)}) %collective-permute-start.17) | collective-permute-done | bytes 32800 | tf_op jit(solution)/shard_map/ppermute | solution.py:327
  45.4 1.0 %collective-permute-done.18.refs_4_ = bf16[8,2048]{1,0:T(8,128)(2,1)S(1)} collective-permute-done((bf16[8,2048]{1,0:T(8,128)(2,1)S(1)}, bf16[8,2048]{1,0:T(8,128)(2,1)S(1)}, u32[]{:S(2)}, u32[]{:S(2)}) %collective-permute-start.18) | collective-permute-done | bytes 32800 | tf_op jit(solution)/shard_map/ppermute | solution.py:327
  46.4 1.7 %shard_map.123 = (bf16[128,4096]{1,0:T(8,128)(2,1)}, bf16[128,4096]{1,0:T(8,128)(2,1)}) custom-call(bf16[128,16]{1,0:T(8,128)(2,1)S(1)} %get-tuple-element.49.refs_0_, bf16[128,16]{1,0:T(8,128)(2,1)S(1)} %get-tuple-element.50.refs_1_, f32[16,1]{1,0:T(8,128)S(1)} %get-tuple-element.51.refs_2_, bf16[8,2048]{1,0:T(8,128)(2,1)S(1)} %collective-permute-done.17.refs_3_, ...), custom_call_target="tpu_custom_call" | custom-call | tf_op jit(solution)/shard_map/pallas_call | solution.py:60
  (6 shorter events, 0.0 us)
Async XLA Ops:
  2.5 7.3 %collective-permute-start = (bf16[8,2048]{1,0:T(8,128)(2,1)S(1)}, bf16[8,2048]{1,0:T(8,128)(2,1)S(1)}, u32[]{:S(2)}, u32[]{:S(2)}) collective-permute-start(bf16[8,2048]{1,0:T(8,128)(2,1)S(1)} %get-tuple-element.52), channel_id=1, source_target_pairs={{0,24},{1,25},{2,26},{3,27},{4,28},{5,29},{6,30},{7,31},{8,16},{9,... | collective-permute-start | bytes 98312 | tf_op jit(solution)/shard_map/ppermute | solution.py:327
  7.5 4.8 %collective-permute-start.1 = (bf16[8,2048]{1,0:T(8,128)(2,1)S(1)}, bf16[8,2048]{1,0:T(8,128)(2,1)S(1)}, u32[]{:S(2)}, u32[]{:S(2)}) collective-permute-start(bf16[8,2048]{1,0:T(8,128)(2,1)S(1)} %get-tuple-element.53), channel_id=1, source_target_pairs={{0,8},{1,9},{2,10},{3,11},{4,12},{5,13},{6,14},{7,15},{8,0},{9,1},... | collective-permute-start | bytes 98312 | tf_op jit(solution)/shard_map/ppermute | solution.py:327
  7.8 4.5 %collective-permute-start.2 = (bf16[8,2048]{1,0:T(8,128)(2,1)S(1)}, bf16[8,2048]{1,0:T(8,128)(2,1)S(1)}, u32[]{:S(2)}, u32[]{:S(2)}) collective-permute-start(bf16[8,2048]{1,0:T(8,128)(2,1)S(1)} %get-tuple-element.54), channel_id=1, source_target_pairs={{0,16},{1,17},{2,18},{3,19},{4,20},{5,21},{6,22},{7,23},{8,24},{9,... | collective-permute-start | bytes 98312 | tf_op jit(solution)/shard_map/ppermute | solution.py:327
  12.5 6.5 %collective-permute-start.3 = (bf16[32,2048]{1,0:T(8,128)(2,1)S(1)}, bf16[32,2048]{1,0:T(8,128)(2,1)S(1)}, u32[]{:S(2)}, u32[]{:S(2)}) collective-permute-start(bf16[32,2048]{1,0:T(8,128)(2,1)S(1)} %shard_map.112.refs_0_), channel_id=1, source_target_pairs={{0,6},{1,7},{2,4},{3,5},{4,2},{5,3},{6,0},{7,1},{8,14},{9,15},{10,... | collective-permute-start | bytes 393224 | tf_op jit(solution)/shard_map/ppermute | solution.py:327
  15.1 5.2 %collective-permute-start.10 = (bf16[32,2048]{1,0:T(8,128)(2,1)S(1)}, bf16[32,2048]{1,0:T(8,128)(2,1)S(1)}, u32[]{:S(2)}, u32[]{:S(2)}) collective-permute-start(bf16[32,2048]{1,0:T(8,128)(2,1)S(1)} %shard_map.112.refs_0_), channel_id=1, source_target_pairs={{0,4},{1,5},{2,6},{3,7},{4,0},{5,1},{6,2},{7,3},{8,12},{9,13},{10,... | collective-permute-start | bytes 393224 | tf_op jit(solution)/shard_map/ppermute | solution.py:327
  15.6 5.0 %collective-permute-start.9 = (bf16[32,2048]{1,0:T(8,128)(2,1)S(1)}, bf16[32,2048]{1,0:T(8,128)(2,1)S(1)}, u32[]{:S(2)}, u32[]{:S(2)}) collective-permute-start(bf16[32,2048]{1,0:T(8,128)(2,1)S(1)} %shard_map.112.refs_0_), channel_id=1, source_target_pairs={{0,2},{1,3},{2,0},{3,1},{4,6},{5,7},{6,4},{7,5},{8,10},{9,11},{10,... | collective-permute-start | bytes 393224 | tf_op jit(solution)/shard_map/ppermute | solution.py:327
  18.4 2.5 %collective-permute-start.4 = (bf16[32,2048]{1,0:T(8,128)(2,1)S(1)}, bf16[32,2048]{1,0:T(8,128)(2,1)S(1)}, u32[]{:S(2)}, u32[]{:S(2)}) collective-permute-start(bf16[32,2048]{1,0:T(8,128)(2,1)S(1)} %shard_map.112.refs_0_), channel_id=1, source_target_pairs={{0,1},{1,0},{2,3},{3,2},{4,5},{5,4},{6,7},{7,6},{8,9},{9,8},{10,11... | collective-permute-start | bytes 393224 | tf_op jit(solution)/shard_map/ppermute | solution.py:327
  19.0 1.9 %collective-permute-start.5 = (bf16[32,2048]{1,0:T(8,128)(2,1)S(1)}, bf16[32,2048]{1,0:T(8,128)(2,1)S(1)}, u32[]{:S(2)}, u32[]{:S(2)}) collective-permute-start(bf16[32,2048]{1,0:T(8,128)(2,1)S(1)} %shard_map.114.refs_1_), channel_id=1, source_target_pairs={{0,1},{1,0},{2,3},{3,2},{4,5},{5,4},{6,7},{7,6},{8,9},{9,8},{10,11... | collective-permute-start | bytes 393224 | tf_op jit(solution)/shard_map/ppermute | solution.py:327
  20.3 1.9 %collective-permute-start.12 = (bf16[32,2048]{1,0:T(8,128)(2,1)S(1)}, bf16[32,2048]{1,0:T(8,128)(2,1)S(1)}, u32[]{:S(2)}, u32[]{:S(2)}) collective-permute-start(bf16[32,2048]{1,0:T(8,128)(2,1)S(1)} %collective-permute-done.10.refs_1_.refs_5_), channel_id=1, source_target_pairs={{0,1},{1,0},{2,3},{3,2},{4,5},{5,4},{6,7},{7,6},{8,9},{9,8},{10,11... | collective-permute-start | bytes 393224 | tf_op jit(solution)/shard_map/ppermute | solution.py:327
  20.5 1.7 %collective-permute-start.11 = (bf16[32,2048]{1,0:T(8,128)(2,1)S(1)}, bf16[32,2048]{1,0:T(8,128)(2,1)S(1)}, u32[]{:S(2)}, u32[]{:S(2)}) collective-permute-start(bf16[32,2048]{1,0:T(8,128)(2,1)S(1)} %collective-permute-done.9.refs_0_.refs_4_), channel_id=1, source_target_pairs={{0,1},{1,0},{2,3},{3,2},{4,5},{5,4},{6,7},{7,6},{8,9},{9,8},{10,11... | collective-permute-start | bytes 393224 | tf_op jit(solution)/shard_map/ppermute | solution.py:327
  21.5 5.7 %collective-permute-start.6 = (bf16[64,768]{1,0:T(8,128)(2,1)S(1)}, bf16[64,768]{1,0:T(8,128)(2,1)S(1)}, u32[]{:S(2)}, u32[]{:S(2)}) collective-permute-start(bf16[64,768]{1,0:T(8,128)(2,1)S(1)} %get-tuple-element.62), channel_id=1, source_target_pairs={{0,16},{1,17},{2,18},{3,19},{4,20},{5,21},{6,22},{7,23},{8,24},{9,... | collective-permute-start | bytes 294920 | tf_op jit(solution)/shard_map/ppermute | solution.py:327
  22.9 5.7 %collective-permute-start.13 = (bf16[64,768]{1,0:T(8,128)(2,1)S(1)}, bf16[64,768]{1,0:T(8,128)(2,1)S(1)}, u32[]{:S(2)}, u32[]{:S(2)}) collective-permute-start(bf16[64,768]{1,0:T(8,128)(2,1)S(1)} %get-tuple-element.71), channel_id=1, source_target_pairs={{0,16},{1,17},{2,18},{3,19},{4,20},{5,21},{6,22},{7,23},{8,24},{9,... | collective-permute-start | bytes 294920 | tf_op jit(solution)/shard_map/ppermute | solution.py:327
  27.9 1.6 %collective-permute-start.7 = (bf16[64,2048]{1,0:T(8,128)(2,1)S(1)}, bf16[64,2048]{1,0:T(8,128)(2,1)S(1)}, u32[]{:S(2)}, u32[]{:S(2)}) collective-permute-start(bf16[64,2048]{1,0:T(8,128)(2,1)S(1)} %get-tuple-element.67), channel_id=1, source_target_pairs={{0,1},{1,0},{2,3},{3,2},{4,5},{5,4},{6,7},{7,6},{8,9},{9,8},{10,11... | collective-permute-start | bytes 786440 | tf_op jit(solution)/shard_map/ppermute | solution.py:327
  29.2 2.3 %collective-permute-start.14 = (bf16[64,2048]{1,0:T(8,128)(2,1)S(1)}, bf16[64,2048]{1,0:T(8,128)(2,1)S(1)}, u32[]{:S(2)}, u32[]{:S(2)}) collective-permute-start(bf16[64,2048]{1,0:T(8,128)(2,1)S(1)} %get-tuple-element.74), channel_id=1, source_target_pairs={{0,1},{1,0},{2,3},{3,2},{4,5},{5,4},{6,7},{7,6},{8,9},{9,8},{10,11... | collective-permute-start | bytes 786440 | tf_op jit(solution)/shard_map/ppermute | solution.py:327
  29.6 7.2 %collective-permute-start.8 = (bf16[32,2048]{1,0:T(8,128)(2,1)S(1)}, bf16[32,2048]{1,0:T(8,128)(2,1)S(1)}, u32[]{:S(2)}, u32[]{:S(2)}) collective-permute-start(bf16[32,2048]{1,0:T(8,128)(2,1)S(1)} %get-tuple-element.69), channel_id=1, source_target_pairs={{0,6},{1,7},{2,4},{3,5},{4,2},{5,3},{6,0},{7,1},{8,14},{9,15},{10,... | collective-permute-start | bytes 393224 | tf_op jit(solution)/shard_map/ppermute | solution.py:327
  31.6 7.4 %collective-permute-start.15 = (bf16[32,2048]{1,0:T(8,128)(2,1)S(1)}, bf16[32,2048]{1,0:T(8,128)(2,1)S(1)}, u32[]{:S(2)}, u32[]{:S(2)}) collective-permute-start(bf16[32,2048]{1,0:T(8,128)(2,1)S(1)} %get-tuple-element.75), channel_id=1, source_target_pairs={{0,2},{1,3},{2,0},{3,1},{4,6},{5,7},{6,4},{7,5},{8,10},{9,11},{10,... | collective-permute-start | bytes 393224 | tf_op jit(solution)/shard_map/ppermute | solution.py:327
  32.6 6.4 %collective-permute-start.16 = (bf16[32,2048]{1,0:T(8,128)(2,1)S(1)}, bf16[32,2048]{1,0:T(8,128)(2,1)S(1)}, u32[]{:S(2)}, u32[]{:S(2)}) collective-permute-start(bf16[32,2048]{1,0:T(8,128)(2,1)S(1)} %get-tuple-element.76), channel_id=1, source_target_pairs={{0,4},{1,5},{2,6},{3,7},{4,0},{5,1},{6,2},{7,3},{8,12},{9,13},{10,... | collective-permute-start | bytes 393224 | tf_op jit(solution)/shard_map/ppermute | solution.py:327
  39.3 6.1 %collective-permute-start.17 = (bf16[8,2048]{1,0:T(8,128)(2,1)S(1)}, bf16[8,2048]{1,0:T(8,128)(2,1)S(1)}, u32[]{:S(2)}, u32[]{:S(2)}) collective-permute-start(bf16[8,2048]{1,0:T(8,128)(2,1)S(1)} %get-tuple-element.84), channel_id=1, source_target_pairs={{0,24},{1,25},{2,26},{3,27},{4,28},{5,29},{6,30},{7,31},{8,16},{9,... | collective-permute-start | bytes 98312 | tf_op jit(solution)/shard_map/ppermute | solution.py:327
  41.3 5.1 %collective-permute-start.18 = (bf16[8,2048]{1,0:T(8,128)(2,1)S(1)}, bf16[8,2048]{1,0:T(8,128)(2,1)S(1)}, u32[]{:S(2)}, u32[]{:S(2)}) collective-permute-start(bf16[8,2048]{1,0:T(8,128)(2,1)S(1)} %get-tuple-element.85), channel_id=1, source_target_pairs={{0,8},{1,9},{2,10},{3,11},{4,12},{5,13},{6,14},{7,15},{8,0},{9,1},... | collective-permute-start | bytes 98312 | tf_op jit(solution)/shard_map/ppermute | solution.py:327
  42.2 4.2 %collective-permute-start.19 = (bf16[8,2048]{1,0:T(8,128)(2,1)S(1)}, bf16[8,2048]{1,0:T(8,128)(2,1)S(1)}, u32[]{:S(2)}, u32[]{:S(2)}) collective-permute-start(bf16[8,2048]{1,0:T(8,128)(2,1)S(1)} %get-tuple-element.86), channel_id=1, source_target_pairs={{0,16},{1,17},{2,18},{3,19},{4,20},{5,21},{6,22},{7,23},{8,24},{9,... | collective-permute-start | bytes 98312 | tf_op jit(solution)/shard_map/ppermute | solution.py:327
